TPU v7x, 32 devices: a whole 2x2x4 slice. The times are simulated.
32 devices in a mesh: beam: 4 (over y, core), strip: 8 (over z, x).
Axes of the slice: x: 2, y: 2, z: 4, core: 2. Of those that a mesh axis runs over, the one named last changes fastest.
Arguments:
- atoms: int32 [2, 1536, 4096], P(None, 'strip'), may hold values from 0 to 3
- phases: float32 [2, 4], replicated, may hold values from 0.2 to 3
- aperture: float32 [8], P('beam'), may hold values from 0.3 to 3
- tilts: int32 [8, 2], P('beam'), may hold values from -16 to 16
- positions: int32 [256, 2], P('strip'), may hold values from 0 to 4095, as said below
Outputs:
- intensity: float32 [256, 16384], P('strip')
Inputs may be any that keep to these rules, and one draw needn't show every extreme that they name: `positions`: probes 32 * s to 32 * s + 31 have their row in rows 192 * s to 192 * s + 191; columns lie in 0 to 4095. Probe 0 lies at row 0, column 0, and the last probe at row 1535, column 4095.
All inputs are finite; a program needn't handle non-finite values.
Results may differ from a plain program's by a relative error of at most 0.02.
Values may be sent and summed in bfloat16 or wider, within the bound.
No kernel may reach another device: no remote copies, remote signals or barrier semaphores. Data moves between devices by JAX's collectives and lax.ppermute only.
A program may use at most 192 MiB of HBM per device.

v0:
```python
import math

import jax
import jax.numpy as jnp
from jax import lax
from jax.sharding import PartitionSpec as P

XBLK = 128
HALFW = 32
TYPES = 4
WIN = 128


def padded_2(cells, sides, width):
    for axis, dim in sides:
        count = lax.axis_size(axis)
        head = lax.slice_in_dim(cells, 0, width, axis=dim)
        tail = lax.slice_in_dim(cells, cells.shape[dim] - width, cells.shape[dim], axis=dim)
        cells = jnp.concatenate(
            [
                lax.ppermute(tail, axis, [(i, (i + 1) % count) for i in range(count)]),
                cells,
                lax.ppermute(head, axis, [((i + 1) % count, i) for i in range(count)]),
            ],
            axis=dim,
        )
    return cells


def band_taps(offset):
    steps_all = jnp.arange(-HALFW, HALFW + 1).astype(jnp.float32)
    weights_all = 1.0 - 0.5 * (steps_all / (HALFW + 1.0)) ** 2
    norm_scale = jnp.sqrt(jnp.sum(weights_all * weights_all))
    weight = (1.0 - 0.5 * (offset / (HALFW + 1.0)) ** 2) / norm_scale
    chirp_phase = math.pi * offset * offset / (2.0 * HALFW + 1.0)
    inside = jnp.abs(offset) <= HALFW
    real_part = jnp.where(inside, jnp.cos(chirp_phase) * weight, 0.0)
    imag_part = jnp.where(inside, jnp.sin(chirp_phase) * weight, 0.0)
    return (real_part.astype(jnp.bfloat16), imag_part.astype(jnp.bfloat16))


def cross_kernel(block_len):
    source = jnp.arange(3 * block_len)[:, None]
    target = jnp.arange(block_len)[None, :]
    real_part, imag_part = band_taps((target + block_len - source).astype(jnp.float32))
    from_real = jnp.stack([real_part, imag_part], axis=1)
    from_imag = jnp.stack([-imag_part, real_part], axis=1)
    return jnp.stack([from_real, from_imag], axis=0)


def along_x(wave_now, kernel):
    beams_here, pairs, rows_here, width_x = wave_now.shape
    blocks = wave_now.reshape(beams_here, pairs, rows_here, width_x // XBLK, XBLK)
    from_left = jnp.einsum(
        "bcrnq,cqeo->berno", blocks, kernel[:, :XBLK], preferred_element_type=jnp.float32
    )
    from_self = jnp.einsum(
        "bcrnq,cqeo->berno", blocks, kernel[:, XBLK : 2 * XBLK], preferred_element_type=jnp.float32
    )
    from_right = jnp.einsum(
        "bcrnq,cqeo->berno", blocks, kernel[:, 2 * XBLK :], preferred_element_type=jnp.float32
    )
    result = jnp.roll(from_left, 1, axis=3) + from_self + jnp.roll(from_right, -1, axis=3)
    return result.reshape(beams_here, pairs, rows_here, width_x).astype(jnp.bfloat16)


def down_kernel(rows_out, rows_in, depth_out, depth_in):
    target = jnp.arange(rows_out)[:, None]
    source = jnp.arange(rows_in)[None, :]
    real_part, imag_part = band_taps((target - depth_out - source + depth_in).astype(jnp.float32))
    upper = jnp.concatenate([real_part, -imag_part], axis=1)
    lower = jnp.concatenate([imag_part, real_part], axis=1)
    return jnp.concatenate([upper, lower], axis=0)


def along_y(padded, rows_here, depth_out, depth_in):
    beams_here, pairs, rows_in, width_x = padded.shape
    rows_out = rows_here + 2 * depth_out
    matrix = down_kernel(rows_out, rows_in, depth_out, depth_in)
    flat_rows = padded.reshape(beams_here, 2 * rows_in, width_x)
    result = jnp.einsum("ij,bjx->bix", matrix, flat_rows, preferred_element_type=jnp.float32)
    return result.reshape(beams_here, 2, rows_out, width_x)


def transmit(atom_map, phase_row):
    angles = jnp.zeros(atom_map.shape, jnp.float32)
    for atom_type in range(TYPES):
        angles = angles + jnp.where(atom_map == atom_type, phase_row[atom_type], 0.0)
    return (jnp.cos(angles), jnp.sin(angles))


def complex_times(values_in, cos_part, sin_part):
    real_in = values_in[:, 0]
    imag_in = values_in[:, 1]
    return jnp.stack(
        [real_in * cos_part - imag_in * sin_part, real_in * sin_part + imag_in * cos_part], axis=1
    )


def local(atoms, phases, aperture, tilts, positions):
    rows_here = atoms.shape[1]
    width_x = atoms.shape[2]
    beams_here = tilts.shape[0]
    strip_index = lax.axis_index("strip")
    strip_count = lax.axis_size("strip")
    rows_total = rows_here * strip_count
    beams_total = beams_here * lax.axis_size("beam")
    row_ids = strip_index * rows_here + jnp.arange(rows_here, dtype=jnp.int32)
    col_ids = jnp.arange(width_x, dtype=jnp.int32)
    tilt_x = tilts[:, 0][:, None, None]
    tilt_y = tilts[:, 1][:, None, None]
    phase_x = (tilt_x * col_ids[None, None, :] % width_x).astype(jnp.float32) / width_x
    phase_y = (tilt_y * row_ids[None, :, None] % rows_total).astype(jnp.float32) / rows_total
    plane_angle = 2.0 * math.pi * (phase_y + phase_x)
    plane_wave = jnp.stack([jnp.cos(plane_angle), jnp.sin(plane_angle)], axis=1)
    cos_part, sin_part = transmit(atoms[0], phases[0])
    wave_now = complex_times(plane_wave, cos_part, sin_part).astype(jnp.bfloat16)
    kernel = cross_kernel(XBLK)
    half_win = WIN // 2
    crossed = along_x(wave_now, kernel)
    padded = padded_2(crossed, (("strip", 2),), HALFW)
    down_field = along_y(padded, rows_here, 0, HALFW)
    cos_part, sin_part = transmit(atoms[1], phases[1])
    wave_now = complex_times(down_field, cos_part, sin_part).astype(jnp.bfloat16)
    crossed = along_x(wave_now, kernel)
    padded = padded_2(crossed, (("strip", 2),), HALFW)
    exit_core = along_y(padded, rows_here, 0, HALFW).astype(jnp.bfloat16)
    exit_wave = padded_2(exit_core, (("strip", 2),), half_win)
    widened = jnp.concatenate(
        [exit_wave[..., width_x - half_win :], exit_wave, exit_wave[..., :half_win]], axis=-1
    )
    local_rows = positions[:, 0] - strip_index * rows_here
    probe_cols = positions[:, 1]

    def crop_window(row_start, col_start):
        return lax.dynamic_slice(widened, (0, 0, row_start, col_start), (beams_here, 2, WIN, WIN))

    windows = jax.vmap(crop_window)(local_rows, probe_cols).astype(jnp.float32)
    probe_x = (tilts[:, 0][None, :] * probe_cols[:, None] % width_x).astype(jnp.float32) / width_x
    probe_y = (tilts[:, 1][None, :] * positions[:, 0][:, None] % rows_total).astype(
        jnp.float32
    ) / rows_total
    probe_angle = -2.0 * math.pi * (probe_y + probe_x)
    coef_re = (aperture[None, :] * jnp.cos(probe_angle))[:, :, None, None]
    coef_im = (aperture[None, :] * jnp.sin(probe_angle))[:, :, None, None]
    psi_re = jnp.sum(coef_re * windows[:, :, 0] - coef_im * windows[:, :, 1], axis=1)
    psi_im = jnp.sum(coef_re * windows[:, :, 1] + coef_im * windows[:, :, 0], axis=1)
    probe_count = positions.shape[0]
    partial_value = jnp.stack([psi_re, psi_im], axis=1).reshape(probe_count, 2, WIN * WIN)
    summed = lax.psum(partial_value.astype(jnp.bfloat16), "beam").astype(jnp.float32)
    return (summed[:, 0] * summed[:, 0] + summed[:, 1] * summed[:, 1]) / beams_total


def solution(mesh):
    in_specs = (P(None, "strip", None), P(), P("beam"), P("beam", None), P("strip", None))
    out_specs = P("strip", None)
    return jax.shard_map(local, mesh=mesh, in_specs=in_specs, out_specs=out_specs, check_vma=False)
```

profile of v0, /device:TPU:0, one launch (start us, length us, event | category | flops | bytes accessed | tf_op | source)
XLA Modules:
  0.0 649.1 jit_solution(11250583084471188242)
XLA Ops:
  11.1 31.3 %cosine_bitcast_fusion = (f32[192,4096]{1,0:T(8,128)}, f32[24,8,32,128]{3,1,2,0:T(8,128)S(1)}, f32[24,8,32,128]{3,1,2,0:T(8,128)S(1)}, f32[192,4096]{1,0:T(8,128)}) fusion(f32[]{:T(128)} %bitcast.35, f32[]{:T(128)} %bitcast.34, f32[]{:T(128)} %bitcast.33, f32[]{:T(128)} %bitcast.32, s32[2,192,4096]{2,1,0:T(8,128)} %param.5, f32[]{:T(128)} %bitcast.11, ...), kind=kLoop, calls=%fused_computation.32 | loop fusion | flops 17301504 | bytes 18874400 | tf_op jit(solution)/shard_map/mul | solution.py:96
  50.9 25.6 %subtract_convert_fusion.1 = (bf16[2,1,192,32,128]{4,2,1,3,0:T(8,128)(2,1)S(1)}, bf16[2,1,192,32,128]{4,2,1,3,0:T(8,128)(2,1)S(1)}) fusion(f32[192,32,128]{2,0,1:T(8,128)} %copy.15, f32[192,32,128]{2,0,1:T(8,128)} %copy.14, f32[2,32,128]{2,1,0:T(8,128)S(1)} %fusion.19, f32[2,192]{1,0:T(2,128)S(1)} %fusion.27), kind=kLoop, calls=%fused_computation.19 | loop fusion | flops 15728640 | bytes 12617216 | tf_op jit(solution)/shard_map/convert.8
  76.5 5.6 convolution_bitcast_fusion.2
  82.0 10.5 %slice.219 = f32[2,2,192,31,128]{4,2,3,0,1:T(8,128)} slice(f32[2,2,192,32,128]{4,2,3,0,1:T(8,128)} %convolution_bitcast_fusion.2), slice={[0:2], [0:2], [0:192], [1:32], [0:128]} | slice | bytes 24379392 | tf_op jit(solution)/shard_map/jit(_roll_static)/slice | solution.py:63
  92.5 5.6 convolution_bitcast_fusion.3
  98.1 10.5 %slice.216 = f32[2,2,192,31,128]{4,2,3,0,1:T(8,128)} slice(f32[2,2,192,32,128]{4,2,3,0,1:T(8,128)} %convolution_bitcast_fusion.3), slice={[0:2], [0:2], [0:192], [0:31], [0:128]} | slice | bytes 24379392 | tf_op jit(solution)/shard_map/jit(_roll_static)/slice | solution.py:63
  108.6 13.9 %fusion.1 = bf16[2,2,192,32,128]{4,2,3,0,1:T(8,128)(2,1)} fusion(f32[2,2,192,31,128]{4,2,3,0,1:T(8,128)} %slice.216, f32[2,2,192,1,128]{4,2,3,0,1:T(8,128)S(1)} %slice-done.1, f32[2,2,192,1,128]{4,2,3,0,1:T(8,128)S(1)} %slice-done, f32[2,2,192,31,128]{4,2,3,0,1:T(8,128)} %slice.219, bf16[2,1,192,32,128]{4,2,1,3,0:T(8,128)(2,1)} %copy-done.1, ...), kind=kOutput, calls=%fused_computation.4 | convolution fusion | flops 1639186432 | bytes 38141952 | tf_op jit(solution)/shard_map/bcrnq,cqeo->berno/dot_general | solution.py:57
  122.5 9.4 %copy.16 = bf16[2,2,192,32,128]{4,3,2,1,0:T(8,128)(2,1)} copy(bf16[2,2,192,32,128]{4,2,3,0,1:T(8,128)(2,1)} %fusion.1) | data formatting | bytes 12582912 | tf_op jit(solution)/shard_map/convert_element_type | solution.py:64
  132.0 10.3 %convert_element_type.153 = bf16[2,2,192,4096]{3,2,1,0:T(8,128)(2,1)} reshape(bf16[2,2,192,32,128]{4,3,2,1,0:T(8,128)(2,1)} %copy.16) | data formatting | bytes 12582912 | tf_op jit(solution)/shard_map/convert_element_type | solution.py:64
  151.7 40.2 %collective-permute-done = bf16[2,2,32,4096]{3,2,1,0:T(8,128)(2,1)S(1)} collective-permute-done((bf16[2,2,32,4096]{3,2,1,0:T(8,128)(2,1)S(1)}, bf16[2,2,32,4096]{3,2,1,0:T(8,128)(2,1)S(1)}, u32[]{:S(2)}, u32[]{:S(2)}) %collective-permute-start) | collective-permute-done | bytes 1048608 | tf_op jit(solution)/shard_map/ppermute | solution.py:21
  194.0 4.3 pad_maximum_fusion.1
  201.8 3.7 subtract_convert_fusion
  209.7 5.6 convolution_bitcast_fusion
  215.2 10.5 %slice.227 = f32[2,2,192,31,128]{4,2,3,0,1:T(8,128)} slice(f32[2,2,192,32,128]{4,2,3,0,1:T(8,128)} %convolution_bitcast_fusion), slice={[0:2], [0:2], [0:192], [1:32], [0:128]} | slice | bytes 24379392 | tf_op jit(solution)/shard_map/jit(_roll_static)/slice | solution.py:63
  225.7 5.6 convolution_bitcast_fusion.1
  231.3 10.5 %slice.226 = f32[2,2,192,31,128]{4,2,3,0,1:T(8,128)} slice(f32[2,2,192,32,128]{4,2,3,0,1:T(8,128)} %convolution_bitcast_fusion.1), slice={[0:2], [0:2], [0:192], [0:31], [0:128]} | slice | bytes 24379392 | tf_op jit(solution)/shard_map/jit(_roll_static)/slice | solution.py:63
  241.8 13.9 %fusion.3 = bf16[2,2,192,32,128]{4,2,3,0,1:T(8,128)(2,1)} fusion(f32[2,2,192,31,128]{4,2,3,0,1:T(8,128)} %slice.226, f32[2,2,192,1,128]{4,2,3,0,1:T(8,128)S(1)} %slice-done.3, f32[2,2,192,1,128]{4,2,3,0,1:T(8,128)S(1)} %slice-done.2, f32[2,2,192,31,128]{4,2,3,0,1:T(8,128)} %slice.227, bf16[2,1,192,32,128]{4,2,1,3,0:T(8,128)(2,1)} %copy-done, ...), kind=kOutput, calls=%fused_computation.7 | convolution fusion | flops 1639186432 | bytes 38141952 | tf_op jit(solution)/shard_map/bcrnq,cqeo->berno/dot_general | solution.py:57
  255.6 9.4 %copy.21 = bf16[2,2,192,32,128]{4,3,2,1,0:T(8,128)(2,1)} copy(bf16[2,2,192,32,128]{4,2,3,0,1:T(8,128)(2,1)} %fusion.3) | data formatting | bytes 12582912 | tf_op jit(solution)/shard_map/convert_element_type | solution.py:64
  265.1 10.3 %convert_element_type.158 = bf16[2,2,192,4096]{3,2,1,0:T(8,128)(2,1)} reshape(bf16[2,2,192,32,128]{4,3,2,1,0:T(8,128)(2,1)} %copy.21) | data formatting | bytes 12582912 | tf_op jit(solution)/shard_map/convert_element_type | solution.py:64
  277.4 4.4 collective-permute-start.3
  281.8 39.6 %collective-permute-done.2 = bf16[2,2,32,4096]{3,2,1,0:T(8,128)(2,1)S(1)} collective-permute-done((bf16[2,2,32,4096]{3,2,1,0:T(8,128)(2,1)S(1)}, bf16[2,2,32,4096]{3,2,1,0:T(8,128)(2,1)S(1)}, u32[]{:S(2)}, u32[]{:S(2)}) %collective-permute-start.2) | collective-permute-done | bytes 1048608 | tf_op jit(solution)/shard_map/ppermute | solution.py:21
  321.4 4.0 collective-permute-done.3
  325.4 3.9 pad_maximum_fusion.2
  329.2 3.7 convolution_convert_fusion
  337.9 4.7 collective-permute-start.5
  343.0 84.9 %collective-permute-done.4 = bf16[2,2,64,4096]{3,2,1,0:T(8,128)(2,1)S(1)} collective-permute-done((bf16[2,2,64,4096]{3,2,1,0:T(8,128)(2,1)}, bf16[2,2,64,4096]{3,2,1,0:T(8,128)(2,1)S(1)}, u32[]{:S(2)}, u32[]{:S(2)}) %collective-permute-start.4) | collective-permute-done | bytes 2097184 | tf_op jit(solution)/shard_map/ppermute | solution.py:21
  427.9 3.7 collective-permute-done.5
  431.7 7.5 %pad_maximum_fusion = bf16[2,2,320,4096]{3,2,1,0:T(8,128)(2,1)S(1)} fusion(bf16[2,2,64,4096]{3,2,1,0:T(8,128)(2,1)} %collective-permute-done.5, bf16[2,2,192,4096]{3,2,1,0:T(8,128)(2,1)} %bitcast.161, bf16[2,2,64,4096]{3,2,1,0:T(8,128)(2,1)S(1)} %collective-permute-done.4), kind=kLoop, calls=%fused_computation.8 | loop fusion | flops 31457280 | bytes 20971520 | tf_op jit(solution)/shard_map/concatenate | solution.py:19
  439.2 3.8 copy-done.2
  443.2 20.4 %concatenate.58 = bf16[2,2,320,4224]{3,2,1,0:T(8,128)(2,1)} concatenate(bf16[2,2,320,64]{3,2,1,0:T(8,128)(2,1)S(1)} %get-tuple-element.30, bf16[2,2,320,4096]{3,2,1,0:T(8,128)(2,1)} %copy-done.2, bf16[2,2,320,64]{3,2,1,0:T(8,128)(2,1)S(1)} %get-tuple-element.29), dimensions={3} | concatenate | bytes 21626880 | tf_op jit(solution)/shard_map/concatenate | solution.py:129
  463.7 116.7 %while.1 = (s32[]{:T(128)}, bf16[2,2,320,4224]{3,2,1,0:T(8,128)(2,1)}, s32[32,4]{0,1:T(4,128)S(1)}, bf16[32,2,2,128,128]{4,3,2,1,0:T(8,128)(2,1)}, s32[]{:T(128)}) while((s32[]{:T(128)}, bf16[2,2,320,4224]{3,2,1,0:T(8,128)(2,1)}, s32[32,4]{0,1:T(4,128)S(1)}, bf16[32,2,2,128,128]{4,3,2,1,0:T(8,128)(2,1)}, s32[]{:T(128)}) %tuple.44), condition=%wide.while_cond, body=%wide.while_body.sunk | while | flops 2 | bytes 263793 | solution.py:136
  588.6 50.0 %all-reduce.2.cloned.1.call-done = bf16[32,2,16384]{2,0,1:T(8,128)(2,1)} async-done(((bf16[32,2,16384]{2,0,1:T(8,128)(2,1)}), bf16[32,2,16384]{2,0,1:T(8,128)(2,1)}) %all-reduce.2.cloned.1.call-update) | async-done | bytes 2097168 | tf_op jit(solution)/shard_map/psum | solution.py:150
  (166 shorter events, 167.3 us)
Async XLA Ops:
  6.5 632.0 %all-reduce.2.cloned.1.call-start = ((), (), s32[]{:S(2)}) async-start(), calls=%async_computation | async-start | bytes 4194304 | tf_op jit(solution)/shard_map/psum | solution.py:150
  46.5 4.0 copy-start.5
  76.5 16.1 %copy-start.1 = (bf16[2,1,192,32,128]{4,2,1,3,0:T(8,128)(2,1)}, bf16[2,1,192,32,128]{4,2,1,3,0:T(8,128)(2,1)S(1)}, u32[]{:S(2)}) copy-start(bf16[2,1,192,32,128]{4,2,1,3,0:T(8,128)(2,1)S(1)} %get-tuple-element.32) | copy-start | bytes 9437188
  98.1 10.5 %slice-start = ((f32[2,2,192,32,128]{4,2,3,0,1:T(8,128)}), f32[2,2,192,1,128]{4,2,3,0,1:T(8,128)S(1)}, s32[]{:S(2)}) async-start(f32[2,2,192,32,128]{4,2,3,0,1:T(8,128)} %convolution_bitcast_fusion.2), calls=%async_computation.1 | async-start | bytes 786432 | tf_op jit(solution)/shard_map/jit(_roll_static)/slice | solution.py:63
  98.1 10.5 %slice-start.1 = ((f32[2,2,192,32,128]{4,2,3,0,1:T(8,128)}), f32[2,2,192,1,128]{4,2,3,0,1:T(8,128)S(1)}, s32[]{:S(2)}) async-start(f32[2,2,192,32,128]{4,2,3,0,1:T(8,128)} %convolution_bitcast_fusion.3), calls=%async_computation.2 | async-start | bytes 786432 | tf_op jit(solution)/shard_map/jit(_roll_static)/slice | solution.py:63
  143.9 47.9 %collective-permute-start = (bf16[2,2,32,4096]{3,2,1,0:T(8,128)(2,1)S(1)}, bf16[2,2,32,4096]{3,2,1,0:T(8,128)(2,1)S(1)}, u32[]{:S(2)}, u32[]{:S(2)}) collective-permute-start(bf16[2,2,32,4096]{3,2,1,0:T(8,128)(2,1)S(1)} %get-tuple-element.41), channel_id=1, source_target_pairs={{0,1},{1,2},{2,3},{3,4},{4,5},{5,6},{6,7},{7,0},{8,9},{9,10},{10,1... | collective-permute-start | bytes 3145736 | tf_op jit(solution)/shard_map/ppermute | solution.py:21
  146.9 47.1 %collective-permute-start.1 = (bf16[2,2,32,4096]{3,2,1,0:T(8,128)(2,1)S(1)}, bf16[2,2,32,4096]{3,2,1,0:T(8,128)(2,1)S(1)}, u32[]{:S(2)}, u32[]{:S(2)}) collective-permute-start(bf16[2,2,32,4096]{3,2,1,0:T(8,128)(2,1)S(1)} %get-tuple-element.42), channel_id=1, source_target_pairs={{1,0},{2,1},{3,2},{4,3},{5,4},{6,5},{7,6},{0,7},{9,8},{10,9},{11,1... | collective-permute-start | bytes 3145736 | tf_op jit(solution)/shard_map/ppermute | solution.py:23
  198.3 3.5 copy-start.4
  209.7 16.1 %copy-start = (bf16[2,1,192,32,128]{4,2,1,3,0:T(8,128)(2,1)}, bf16[2,1,192,32,128]{4,2,1,3,0:T(8,128)(2,1)S(1)}, u32[]{:S(2)}) copy-start(bf16[2,1,192,32,128]{4,2,1,3,0:T(8,128)(2,1)S(1)} %copy.20) | copy-start | bytes 9437188
  231.3 10.5 %slice-start.2 = ((f32[2,2,192,32,128]{4,2,3,0,1:T(8,128)}), f32[2,2,192,1,128]{4,2,3,0,1:T(8,128)S(1)}, s32[]{:S(2)}) async-start(f32[2,2,192,32,128]{4,2,3,0,1:T(8,128)} %convolution_bitcast_fusion), calls=%async_computation.3 | async-start | bytes 786432 | tf_op jit(solution)/shard_map/jit(_roll_static)/slice | solution.py:63
  231.3 10.5 %slice-start.3 = ((f32[2,2,192,32,128]{4,2,3,0,1:T(8,128)}), f32[2,2,192,1,128]{4,2,3,0,1:T(8,128)S(1)}, s32[]{:S(2)}) async-start(f32[2,2,192,32,128]{4,2,3,0,1:T(8,128)} %convolution_bitcast_fusion.1), calls=%async_computation.4 | async-start | bytes 786432 | tf_op jit(solution)/shard_map/jit(_roll_static)/slice | solution.py:63
  277.1 44.4 %collective-permute-start.2 = (bf16[2,2,32,4096]{3,2,1,0:T(8,128)(2,1)S(1)}, bf16[2,2,32,4096]{3,2,1,0:T(8,128)(2,1)S(1)}, u32[]{:S(2)}, u32[]{:S(2)}) collective-permute-start(bf16[2,2,32,4096]{3,2,1,0:T(8,128)(2,1)S(1)} %get-tuple-element.35), channel_id=1, source_target_pairs={{0,1},{1,2},{2,3},{3,4},{4,5},{5,6},{6,7},{7,0},{8,9},{9,10},{10,1... | collective-permute-start | bytes 3145736 | tf_op jit(solution)/shard_map/ppermute | solution.py:21
  277.4 48.0 %collective-permute-start.3 = (bf16[2,2,32,4096]{3,2,1,0:T(8,128)(2,1)S(1)}, bf16[2,2,32,4096]{3,2,1,0:T(8,128)(2,1)S(1)}, u32[]{:S(2)}, u32[]{:S(2)}) collective-permute-start(bf16[2,2,32,4096]{3,2,1,0:T(8,128)(2,1)S(1)} %get-tuple-element.36), channel_id=1, source_target_pairs={{1,0},{2,1},{3,2},{4,3},{5,4},{6,5},{7,6},{0,7},{9,8},{10,9},{11,1... | collective-permute-start | bytes 3145736 | tf_op jit(solution)/shard_map/ppermute | solution.py:23
  332.9 2.7 copy-start.3
  332.9 9.7 %copy-start.6 = (s32[32,2]{0,1:T(2,128)S(1)}, s32[32,2]{0,1:T(2,128)}, u32[]{:S(2)}) copy-start(s32[32,2]{0,1:T(2,128)} %param.9) | copy-start | bytes 772
  332.9 9.7 %copy-start.7 = (f32[2]{0:T(128)S(1)}, f32[2]{0:T(128)}, u32[]{:S(2)}) copy-start(f32[2]{0:T(128)} %param.7) | copy-start | bytes 28
  337.9 90.0 %collective-permute-start.4 = (bf16[2,2,64,4096]{3,2,1,0:T(8,128)(2,1)}, bf16[2,2,64,4096]{3,2,1,0:T(8,128)(2,1)S(1)}, u32[]{:S(2)}, u32[]{:S(2)}) collective-permute-start(bf16[2,2,64,4096]{3,2,1,0:T(8,128)(2,1)} %get-tuple-element.33), channel_id=1, source_target_pairs={{0,1},{1,2},{2,3},{3,4},{4,5},{5,6},{6,7},{7,0},{8,9},{9,10},{10,1... | collective-permute-start | bytes 6291464 | tf_op jit(solution)/shard_map/ppermute | solution.py:21
  337.9 93.7 %collective-permute-start.5 = (bf16[2,2,64,4096]{3,2,1,0:T(8,128)(2,1)}, bf16[2,2,64,4096]{3,2,1,0:T(8,128)(2,1)}, u32[]{:S(2)}, u32[]{:S(2)}) collective-permute-start(bf16[2,2,64,4096]{3,2,1,0:T(8,128)(2,1)} %get-tuple-element.34), channel_id=1, source_target_pairs={{1,0},{2,1},{3,2},{4,3},{5,4},{6,5},{7,6},{0,7},{9,8},{10,9},{11,1... | collective-permute-start | bytes 6291464 | tf_op jit(solution)/shard_map/ppermute | solution.py:23
  439.2 3.9 copy-start.2
Sparse Core Ops, SparseCore 0:
  588.7 49.8 all-reduce.1
where the time goes:
time: 659 us; the launch traced here: 649 us
  local copies, waits for them, and re-layouts  246 us (37%)
  waiting for transfers between devices  225 us (34%)
  other arithmetic  91.1 us (14%)
  matrix products  57.2 us (9%)
  starting transfers between devices  15.6 us (2%)
  between operations  14.6 us (2%)
    ppermute x3, waiting for transfers between devices, padded_2(): lax.ppermute(tail, axis, [(i, (i + 1) % count) for i in range(count)])  165 us
    gather x96, local copies, waits for them, and re-layouts  117 us
    psum x1, waiting for transfers between devices, local(): lax.psum(partial_value.astype(jnp.bfloat16), 'beam').astype(jnp.float32)  50 us
    convert_element_type x4, local copies, waits for them, and re-layouts, along_x(): result.reshape(beams_here, pairs, rows_here, width_x).astype(jnp.bfloat16)  39.5 us
    mul x1, other arithmetic, complex_times(): real_in * cos_part - imag_in * sin_part  31.3 us
    another operation x2, other arithmetic  29.3 us
    dot_general x2, matrix products, along_x(): jnp.einsum('bcrnq,cqeo->berno', blocks, kernel[:, XBLK:2 * XBLK], preferr...  27.8 us
    slice x6, local copies, waits for them, and re-layouts, along_x(): jnp.roll(from_right, -1, axis=3)  21 us
  transfers between devices with their start and end apart: 7, of which 7 were waited for; matrix products, arithmetic and copies ran while one was open for 0% of the time, Pallas kernels for 0%

commit v1 on v0

v1 whole, which is shorter than its diff:
```python
import math

import jax
import jax.numpy as jnp
import ml_dtypes
import numpy as np
from jax import lax
from jax.experimental import pallas as pl
from jax.experimental.pallas import tpu as pltpu
from jax.sharding import PartitionSpec as P

HALFW = 32
TYPES = 4
WIN = 128
LANES = 128
GROUP = 64
HALO0 = 64
HALO1 = 32
TABLE = 384
MIB = 1024 * 1024


def taps(offset):
    steps = np.arange(-HALFW, HALFW + 1, dtype=np.float32)
    weights = 1.0 - 0.5 * (steps / (HALFW + 1.0)) ** 2
    scale = np.sqrt(np.sum(weights * weights))
    offset = offset.astype(np.float32)
    weight = (1.0 - 0.5 * (offset / (HALFW + 1.0)) ** 2) / scale
    chirp = np.float32(math.pi) * offset * offset / np.float32(2.0 * HALFW + 1.0)
    inside = np.abs(offset) <= HALFW
    real = np.where(inside, np.cos(chirp) * weight, 0.0)
    imag = np.where(inside, np.sin(chirp) * weight, 0.0)
    return real.astype(np.float32), imag.astype(np.float32)


def x_matrix(sources, targets):
    rows = []
    for start in range(0, len(sources), LANES):
        src = sources[start : start + LANES]
        real, imag = taps(targets[None, :] - src[:, None] + HALFW)
        rows.append(np.concatenate([real, imag], axis=1))
        rows.append(np.concatenate([-imag, real], axis=1))
    return np.concatenate(rows, axis=0).astype(ml_dtypes.bfloat16)


def y_matrix():
    out = np.arange(GROUP)[:, None]
    src = np.arange(2 * GROUP)[None, :]
    real, imag = taps(out - src + HALFW)
    upper = np.concatenate([real, -imag], axis=1)
    lower = np.concatenate([imag, real], axis=1)
    return np.concatenate([upper, lower], axis=0).astype(ml_dtypes.bfloat16)


def matrices():
    first = x_matrix(np.arange(2 * LANES), np.arange(LANES))
    second = x_matrix(np.arange(LANES, 2 * LANES), np.arange(LANES, 2 * LANES))
    second = second.reshape(2 * LANES, 2, LANES)
    second[:, :, LANES // 2 :] = 0
    return first, second.reshape(2 * LANES, 2 * LANES), y_matrix()


def pack_kernel(place_ref, pos_ref, first_ref, second_ref, out_ref):
    lane = lax.broadcasted_iota(jnp.int32, (16, LANES), 1)
    out_ref[0:HALO0, :] = first_ref[0].astype(jnp.int16)
    out_ref[HALO0 : HALO0 + HALO1, :] = second_ref[0].astype(jnp.int16)
    tail = jnp.zeros((16, LANES), jnp.int32)
    count = pos_ref.shape[0]
    for probe in range(count):
        tail = jnp.where(lane == probe, pos_ref[probe, 0], tail)
        tail = jnp.where(lane == count + probe, pos_ref[probe, 1], tail)
    tail = tail.astype(jnp.int16)
    for start in range(0, out_ref.shape[1], LANES):
        out_ref[HALO0 + HALO1 :, start : start + LANES] = tail


def pack_rows(place, positions, atoms):
    rows, width = atoms.shape[1], atoms.shape[2]
    half = width // 2
    step = 512
    steps = half // step
    last0, last1 = rows // HALO0 - 1, rows // HALO1 - 1
    return pl.pallas_call(
        pack_kernel,
        out_shape=jax.ShapeDtypeStruct((HALO0 + HALO1 + 16, half), jnp.int16),
        grid_spec=pltpu.PrefetchScalarGridSpec(
            num_scalar_prefetch=1,
            grid=(steps,),
            in_specs=[
                pl.BlockSpec(memory_space=pltpu.SMEM),
                pl.BlockSpec((1, HALO0, step), lambda i, at: (0, (1 - at[0]) * last0, at[1] * steps + i)),
                pl.BlockSpec((1, HALO1, step), lambda i, at: (1, (1 - at[0]) * last1, at[1] * steps + i)),
            ],
            out_specs=pl.BlockSpec((HALO0 + HALO1 + 16, step), lambda i, at: (0, i)),
        ),
    )(place, positions, atoms, atoms)


def words_kernel(place_ref, atoms_ref, out_ref):
    upper = place_ref[0] == 1
    for tile in range(out_ref.shape[0]):
        at = slice(tile * LANES, (tile + 1) * LANES)
        codes = [
            atoms_ref[0, g * GROUP : (g + 1) * GROUP, at]
            + TYPES * atoms_ref[1, g * GROUP : (g + 1) * GROUP, at]
            for g in range(3)
        ]
        own = codes[0] | (codes[1] << 8) | (codes[2] << 16)
        low = (codes[0] << 8) | (codes[1] << 16)
        high = codes[1] | (codes[2] << 8)
        out_ref[tile, 0:GROUP, :] = jnp.where(upper, own, low)
        out_ref[tile, GROUP:, :] = jnp.where(upper, high, own)


def own_words(place, atoms):
    rows, width = atoms.shape[1], atoms.shape[2]
    tiles = 4
    return pl.pallas_call(
        words_kernel,
        out_shape=jax.ShapeDtypeStruct((width // LANES, 2 * GROUP, LANES), jnp.int32),
        grid_spec=pltpu.PrefetchScalarGridSpec(
            num_scalar_prefetch=1,
            grid=(width // (tiles * LANES),),
            in_specs=[pl.BlockSpec((2, rows, tiles * LANES), lambda i, at: (0, 0, i))],
            out_specs=pl.BlockSpec((tiles, 2 * GROUP, LANES), lambda i, at: (i, 0, 0)),
        ),
    )(place, atoms)


def probe_kernel(rows_total, width, beam_ref, out_ref):
    beams = beam_ref.shape[0]
    precise = lax.Precision.HIGHEST

    def cos_turns(turns):
        return jnp.cos((2.0 * math.pi) * (turns - jnp.round(turns)))

    lane = lax.broadcasted_iota(jnp.int32, (1, LANES), 1)
    tilt_y = jnp.zeros((1, LANES), jnp.float32)
    for beam in range(beams):
        tilt_y = jnp.where(lane % beams == beam, beam_ref[beam, 1], tilt_y)
    quarter = jnp.where(lane < beams, 0.0, 0.25)
    row = lax.broadcasted_iota(jnp.int32, (TABLE, LANES), 0) - TABLE // 2
    along_y = cos_turns(row.astype(jnp.float32) * tilt_y / rows_total - quarter)
    along_y = jnp.where(lane < 2 * beams, along_y, 0.0)

    sub = lax.broadcasted_iota(jnp.int32, (LANES, 1), 0)
    tilt_x = jnp.zeros((LANES, 1), jnp.float32)
    weight = jnp.zeros((LANES, 1), jnp.float32)
    for beam in range(beams):
        mine = (sub % beams == beam) & (sub < 2 * beams)
        tilt_x = jnp.where(mine, beam_ref[beam, 0], tilt_x)
        weight = jnp.where(mine, beam_ref[beam, 2], weight)
    col = lax.broadcasted_iota(jnp.int32, (LANES, 2 * LANES), 1) - LANES
    turns = col.astype(jnp.float32) * tilt_x / width
    shift = jnp.where(sub < beams, 0.0, 0.25)
    right_re = weight * cos_turns(turns + shift)
    right_im = weight * cos_turns(turns + shift - 0.25)
    for part, right in ((0, right_re), (1, right_im)):
        table = jnp.dot(along_y, right, precision=precise, preferred_element_type=jnp.float32)
        for tile in range(2):
            out_ref[part, tile] = table[:, tile * LANES : (tile + 1) * LANES]


def probe_table(beam_rows, rows_total, width):
    def kernel(beam_ref, out_ref):
        probe_kernel(rows_total, width, beam_ref, out_ref)

    return pl.pallas_call(
        kernel,
        out_shape=jax.ShapeDtypeStruct((2, 2, TABLE, LANES), jnp.float32),
        in_specs=[pl.BlockSpec(memory_space=pltpu.SMEM)],
        out_specs=pl.BlockSpec(memory_space=pltpu.VMEM),
    )(beam_rows)


def main_kernel(
    beams,
    place_ref,
    pos_ref,
    near_ref,
    phase_ref,
    words_in,
    mine_ref,
    other_ref,
    table_ref,
    first_ref,
    second_ref,
    ymat_ref,
    own_ref,
    ext_ref,
    words,
    list_ref,
):
    side, core, row_base, near_base = place_ref[0], place_ref[1], place_ref[2], place_ref[3]
    tiles = words.shape[0]
    half_tiles = tiles // 2
    f32, bf16 = jnp.float32, jnp.bfloat16

    def merge(upper):
        base = GROUP if upper else 0
        sft = 16 if upper else 0
        lo = 0 if upper else GROUP - HALO1
        for source, at in ((mine_ref, core), (other_ref, 1 - core)):
            for tile in range(half_tiles):
                cols = slice(tile * LANES, (tile + 1) * LANES)
                zero = source[0:HALO0, cols].astype(jnp.int32)
                one = source[HALO0 : HALO0 + HALO1, cols].astype(jnp.int32) * TYPES
                pieces = []
                if lo:
                    pieces.append(zero[0:lo])
                pieces.append(zero[lo : lo + HALO1] + one)
                if lo + HALO1 < GROUP:
                    pieces.append(zero[lo + HALO1 :])
                code = jnp.concatenate(pieces, axis=0) << sft
                index = at * half_tiles + tile
                words[index, base : base + GROUP, :] = words_in[index, base : base + GROUP, :] | code
                rest = GROUP - base
                words[index, rest : rest + GROUP, :] = words_in[index, rest : rest + GROUP, :]

    @pl.when(side == 0)
    def _():
        merge(False)

    @pl.when(side == 1)
    def _():
        merge(True)

    def values(layer):
        angle = [jnp.full((8, LANES), phase_ref[layer, t], f32) for t in range(TYPES)]
        return [jnp.cos(a)[0:1] for a in angle], [jnp.sin(a)[0:1] for a in angle]

    cos0, sin0 = values(0)
    cos1, sin1 = values(1)
    lane = lax.broadcasted_iota(jnp.int32, (1, LANES), 1)
    rows64 = (GROUP, LANES)

    def transmission(word, bit, cos_v, sin_v):
        b0 = (word & (1 << bit)) != 0
        b1 = (word & (2 << bit)) != 0
        out = []
        for v in (cos_v, sin_v):
            low = jnp.where(b0, jnp.broadcast_to(v[1], rows64), jnp.broadcast_to(v[0], rows64))
            high = jnp.where(b0, jnp.broadcast_to(v[3], rows64), jnp.broadcast_to(v[2], rows64))
            out.append(jnp.where(b1, high, low))
        return out

    def task(row, col):
        start = jnp.clip(row - GROUP, 0, GROUP)
        delta = start - GROUP * (1 - side) - row + TABLE // 2
        tile0 = col // LANES + tiles - 1
        shift = lax.rem(col, LANES)
        back = lax.rem(LANES - shift, LANES)
        rolled = []
        for j in range(3):
            word = words[lax.rem(tile0 + j, tiles), pl.ds(start, GROUP), :]
            rolled.append(pltpu.roll(word, back, 1))
        keep = lane < LANES - shift
        window = [jnp.where(keep, rolled[j], rolled[j + 1]) for j in range(2)]

        blocks = []
        for g in range(3):
            parts = []
            for j in range(2):
                t_re, t_im = transmission(window[j], 8 * g, cos0, sin0)
                p_re = table_ref[0, j, pl.ds(delta + g * GROUP, GROUP), :]
                p_im = table_ref[1, j, pl.ds(delta + g * GROUP, GROUP), :]
                parts.append((p_re * t_re - p_im * t_im).astype(bf16))
                parts.append((p_re * t_im + p_im * t_re).astype(bf16))
            blocks.append(jnp.concatenate(parts, axis=1))
        wave = jnp.concatenate(blocks, axis=0)
        one = jnp.dot(wave, first_ref[...], preferred_element_type=f32).astype(bf16)
        two = jnp.dot(wave[:, 2 * LANES :], second_ref[...], preferred_element_type=f32).astype(bf16)
        real = jnp.concatenate([one[:, :LANES], two[:, :LANES]], axis=1)
        imag = jnp.concatenate([one[:, LANES:], two[:, LANES:]], axis=1)

        turned = [pltpu.roll(w, LANES - HALFW, 1) for w in window]
        mid = [jnp.where(lane < LANES - HALFW, turned[0], turned[1]), turned[1]]
        blocks = []
        for b in range(2):
            rows = slice(b * GROUP, b * GROUP + 2 * GROUP)
            stacked = jnp.concatenate([real[rows], imag[rows]], axis=0)
            down = jnp.dot(ymat_ref[...], stacked, preferred_element_type=f32)
            parts = []
            for j in range(2):
                cols = slice(j * LANES, (j + 1) * LANES)
                d_re, d_im = down[:GROUP, cols], down[GROUP:, cols]
                word = jnp.concatenate(
                    [mid[j][HALO1:] >> (8 * b), mid[j][:HALO1] >> (8 * b + 8)], axis=0
                )
                t_re, t_im = transmission(word, 2, cos1, sin1)
                parts.append((d_re * t_re - d_im * t_im).astype(bf16))
                parts.append((d_re * t_im + d_im * t_re).astype(bf16))
            blocks.append(jnp.concatenate(parts, axis=1))
        wave = jnp.concatenate(blocks, axis=0)
        one = jnp.dot(wave, first_ref[...], preferred_element_type=f32).astype(bf16)
        stacked = jnp.concatenate([one[:, :LANES], one[:, LANES:]], axis=0)
        exit_wave = jnp.dot(ymat_ref[...], stacked, preferred_element_type=f32)
        exit_wave = exit_wave.astype(bf16).astype(f32)
        re, im = exit_wave[:GROUP], exit_wave[GROUP:]
        return ((re * re + im * im) * (1.0 / beams)).astype(bf16)

    count = own_ref.shape[0]

    def own_step(i, carry):
        for k in (2 * i, 2 * i + 1):
            probe = 2 * k + core
            own_ref[k] = task(pos_ref[probe, 0] - row_base, pos_ref[probe, 1])
        return carry

    lax.fori_loop(0, count // 2, own_step, 0)

    def find(k, found):
        row = near_ref[2 * k + core] - near_base
        reaches = jnp.where(side == 0, row > -GROUP, row < 4 * GROUP)
        list_ref[found] = k
        return found + reaches.astype(jnp.int32)

    found = lax.fori_loop(0, count, find, 0)

    def ext_step(i, carry):
        for k in (2 * i, jnp.minimum(2 * i + 1, found - 1)):
            slot = list_ref[k]
            probe = 2 * slot + core
            ext_ref[slot] = task(near_ref[probe] - near_base, near_ref[2 * count + probe])
        return carry

    lax.fori_loop(0, (found + 1) // 2, ext_step, 0)


def propagate(beams, place, positions, near, phases, words, mine, other, table):
    count = positions.shape[0] // 2
    first, second, ymat = matrices()
    smem = pl.BlockSpec(memory_space=pltpu.SMEM)
    vmem = pl.BlockSpec(memory_space=pltpu.VMEM)

    def kernel(*refs):
        main_kernel(beams, *refs)

    shape = jax.ShapeDtypeStruct((count, GROUP, WIN), jnp.bfloat16)
    return pl.pallas_call(
        kernel,
        out_shape=[shape, shape],
        in_specs=[smem] * 4 + [vmem] * 7,
        out_specs=[vmem, vmem],
        scratch_shapes=[pltpu.VMEM(words.shape, jnp.int32), pltpu.SMEM((count + 1,), jnp.int32)],
        compiler_params=pltpu.CompilerParams(vmem_limit_bytes=40 * MIB),
    )(place, positions, near, phases, words, mine, other, table, first, second, ymat)


def gather_kernel(place_ref, pos_ref, *refs):
    out_ref, column, window = refs[8], refs[9], refs[10]
    side, core, row_base = place_ref[0], place_ref[1], place_ref[2]
    group = pl.program_id(0)
    f32 = jnp.float32
    for par in range(2):
        parity = core if par == 0 else 1 - core
        own, across, below_or_above, far = refs[4 * par : 4 * par + 4]
        for i in range(4):
            at = 8 * group + 2 * i + parity
            row = pos_ref[at, 0] - row_base
            start = jnp.where(row < GROUP, row, jnp.where(row > 2 * GROUP, row - GROUP, GROUP))
            column[pl.ds(pl.multiple_of(GROUP + GROUP * side, GROUP), GROUP), :] = own[i].astype(f32)
            column[pl.ds(pl.multiple_of(2 * GROUP - GROUP * side, GROUP), GROUP), :] = across[i].astype(f32)
            column[pl.ds(pl.multiple_of(3 * GROUP * (1 - side), GROUP), GROUP), :] = below_or_above[i].astype(f32)
            column[pl.ds(pl.multiple_of(3 * GROUP * side, GROUP), GROUP), :] = far[i].astype(f32)
            slot = pl.multiple_of((2 * i + parity) * WIN, WIN)
            window[pl.ds(slot, WIN), :] = column[pl.ds(start, WIN), :]
    for u in range(WIN):
        out_ref[:, u * WIN : (u + 1) * WIN] = window[pl.ds(u, 8, stride=WIN), :]


def put_together(place, positions, pieces):
    probes = positions.shape[0]
    piece = pl.BlockSpec((4, GROUP, WIN), lambda i, *_: (i, 0, 0))
    return pl.pallas_call(
        gather_kernel,
        out_shape=jax.ShapeDtypeStruct((probes, WIN * WIN), jnp.float32),
        grid_spec=pltpu.PrefetchScalarGridSpec(
            num_scalar_prefetch=2,
            grid=(probes // 8,),
            in_specs=[piece] * 8,
            out_specs=pl.BlockSpec((8, WIN * WIN), lambda i, *_: (i, 0)),
            scratch_shapes=[
                pltpu.VMEM((4 * GROUP, LANES), jnp.float32),
                pltpu.VMEM((8 * WIN, LANES), jnp.float32),
            ],
        ),
    )(place, positions, *pieces)


def local(atoms, phases, aperture, tilts, positions):
    rows_here, width = atoms.shape[1], atoms.shape[2]
    probes = positions.shape[0]
    strip, beam = lax.axis_index("strip"), lax.axis_index("beam")
    strips, ways = lax.axis_size("strip"), lax.axis_size("beam")
    rows_total = rows_here * strips
    beams = tilts.shape[0] * ways
    cores = 2
    side, core = beam // cores, beam % cores
    near_strip = jnp.where(side == 0, strip - 1 + strips, strip + 1) % strips
    near_base = near_strip * rows_here + jnp.where(side == 0, rows_here, -rows_here)
    place = jnp.stack([side, core, strip * rows_here, near_base]).astype(jnp.int32)

    def across(array, dest):
        pairs = []
        for s in range(strips):
            for b in range(ways):
                to_s, to_b = dest(s, b // cores, b % cores)
                pairs.append((b * strips + s, (to_b[0] * cores + to_b[1]) * strips + to_s % strips))
        return lax.ppermute(array, ("beam", "strip"), pairs)

    def swap_cores(array):
        return across(array, lambda s, y, c: (s, (y, 1 - c)))

    payload = pack_rows(place, positions, atoms)
    mine = across(payload, lambda s, y, c: (s + 1 - 2 * y, (y, c)))
    beam_rows = jnp.concatenate([tilts.astype(jnp.float32), aperture[:, None]], axis=1)
    beam_rows = lax.all_gather(beam_rows, "beam", axis=0, tiled=True)
    words = own_words(place, atoms)
    table = probe_table(beam_rows, rows_total, width)
    other = swap_cores(mine)
    near = mine[HALO0 + HALO1, : 2 * probes].astype(jnp.int32)
    own, ext = propagate(beams, place, positions, near, phases, words, mine, other, table)
    far = across(ext, lambda s, y, c: (s - 1 + 2 * y, (1 - y, c)))
    same = across(ext, lambda s, y, c: (s - 1 + 2 * y, (y, c)))
    facing = across(own, lambda s, y, c: (s, (1 - y, c)))
    pieces = [own, facing, same, far]
    return put_together(place, positions, pieces + [swap_cores(piece) for piece in pieces])


def solution(mesh):
    in_specs = (P(None, "strip", None), P(), P("beam"), P("beam", None), P("strip", None))
    out_specs = P("strip", None)
    return jax.shard_map(local, mesh=mesh, in_specs=in_specs, out_specs=out_specs, check_vma=False)
```

time: 659 us -> 86.5 us (0.13); the launches traced: 649 us -> 85.7 us
  local copies, waits for them, and re-layouts: 246 us -> 4.92 us
  waiting for transfers between devices: 225 us -> 22.6 us
  other arithmetic: 91.1 us -> 0.68 us
  matrix products: 57.2 us -> 0 us
  Pallas kernels: 0 us -> 37.9 us
  between operations: 14.6 us -> 0.18 us
    ppermute x6 -> x9, waiting for transfers between devices: 175 us -> 22.6 us  [across(): return lax.ppermute(array, ('beam', 'strip'), pairs)]
    gather x96 -> x0, local copies, waits for them, and re-layouts: 117 us -> none
    dot_general x8 -> x0, matrix products: 57.2 us -> none  [the longest x2 27.8 us: along_x(): jnp.einsum('bcrnq,cqeo->berno', blocks, kernel[:, XBLK:2 * XBLK], preferr...]
    psum x1 -> x0, waiting for transfers between devices: 50 us -> none  [local(): lax.psum(partial_value.astype(jnp.bfloat16), 'beam').astype(jnp.float32)]
    slice x18 -> x0, local copies, waits for them, and re-layouts: 49.7 us -> none  [the longest x6 21 us: along_x(): jnp.roll(from_right, -1, axis=3)]
    convert_element_type x4 -> x0, local copies, waits for them, and re-layouts: 39.5 us -> none  [along_x(): result.reshape(beams_here, pairs, rows_here, width_x).astype(jnp.bfloat16)]
    pallas_call x0 -> x5, Pallas kernels: none -> 37.9 us  [the longest x1 17.4 us: propagate(): pl.pallas_call(kernel, out_shape=[shape, shape], in_specs=[smem] * 4 + [v...]
    mul x3 -> x0, other arithmetic: 31.5 us -> none  [the longest x1 31.3 us: complex_times(): real_in * cos_part - imag_in * sin_part]
  transfers between devices with their start and end apart: 7 -> 9, of which waited for: 7 -> 5; matrix products, arithmetic and copies ran while one was open for 0% -> 0% of each run, Pallas kernels for 0% -> 13%
where the time goes in v1:
time: 86.5 us; the launch traced here: 85.7 us
  Pallas kernels  37.9 us (44%)
  waiting for transfers between devices  22.6 us (26%)
  starting transfers between devices  14 us (16%)
  blocking collectives  5.51 us (6%)
  local copies, waits for them, and re-layouts  4.92 us (6%)
    ppermute x9, waiting for transfers between devices, across(): return lax.ppermute(array, ('beam', 'strip'), pairs)  22.6 us
    pallas_call x1, Pallas kernels, propagate(): pl.pallas_call(kernel, out_shape=[shape, shape], in_specs=[smem] * 4 + [v...  17.4 us
    ppermute x9, starting transfers between devices, across(): return lax.ppermute(array, ('beam', 'strip'), pairs)  14 us
    pallas_call x1, Pallas kernels, own_words(): pl.pallas_call(words_kernel, out_shape=jax.ShapeDtypeStruct((width // LAN...  7.56 us
    all_gather x1, blocking collectives, local(): beam_rows = lax.all_gather(beam_rows, 'beam', axis=0, tiled=True)  5.51 us
    pallas_call x1, Pallas kernels, put_together(): pl.pallas_call(gather_kernel, out_shape=jax.ShapeDtypeStruct((probes, WIN...  5.49 us
    unnamed x37, local copies, waits for them, and re-layouts  4.83 us
    pallas_call x1, Pallas kernels, pack_rows(): pl.pallas_call(pack_kernel, out_shape=jax.ShapeDtypeStruct((HALO0 + HALO1...  4.22 us
  transfers between devices with their start and end apart: 9, of which 5 were waited for; matrix products, arithmetic and copies ran while one was open for 0% of the time, Pallas kernels for 13%

profile of v1, /device:TPU:0, one launch (start us, length us, event | category | flops | bytes accessed | tf_op | source)
XLA Modules:
  0.0 85.7 jit_solution(774366085063788857)
XLA Ops:
  0.0 1.4 %copy.16.pos_ref.refs_1_ = s32[32,2]{1,0:T(8,128)} copy(s32[32,2]{0,1:T(2,128)} %param.12) | data formatting | bytes 512 | tf_op args[4]
  1.4 0.6 pad_add_fusion.place_ref.refs_0_
  2.0 4.2 %shard_map.82 = s16[112,2048]{1,0:T(8,128)(2,1)} custom-call(s32[4]{0:T(128)} %pad_add_fusion.place_ref.refs_0_, s32[32,2]{1,0:T(8,128)} %copy.16.pos_ref.refs_1_, s32[2,192,4096]{2,1,0:T(8,128)} %atoms_ref.1, s32[2,192,4096]{2,1,0:T(8,128)} %atoms_ref.1), custom_call_target="tpu_custom_call" | custom-call | tf_op jit(solution)/shard_map/pallas_call | solution.py:83
  6.2 2.9 %collective-permute-start = (s16[112,2048]{1,0:T(8,128)(2,1)}, s16[112,2048]{1,0:T(8,128)(2,1)S(1)}, u32[]{:S(2)}, u32[]{:S(2)}) collective-permute-start(s16[112,2048]{1,0:T(8,128)(2,1)} %shard_map.82), channel_id=1, source_target_pairs={{0,1},{8,9},{16,23},{24,31},{1,2},{9,10},{17,16},{25,24},{2,3},{10... | collective-permute-start | bytes 1376264 | tf_op jit(solution)/shard_map/ppermute | solution.py:410
  9.1 13.8 %collective-permute-done.refs_5_ = s16[112,2048]{1,0:T(8,128)(2,1)S(1)} collective-permute-done((s16[112,2048]{1,0:T(8,128)(2,1)}, s16[112,2048]{1,0:T(8,128)(2,1)S(1)}, u32[]{:S(2)}, u32[]{:S(2)}) %collective-permute-start) | collective-permute-done | bytes 458784 | tf_op jit(solution)/shard_map/ppermute | solution.py:410
  22.9 0.0 collective-permute-start.1
  22.9 0.1 copy.14
  23.0 0.1 maximum_bitcast_fusion
  23.1 5.5 %all-gather = f32[4,2,3]{2,1,0:T(2,128)} all-gather(f32[1,2,3]{2,1,0:T(2,128)S(1)} %maximum_bitcast_fusion), channel_id=1, replica_groups=mesh['beam'=4,'strip'=8] {'beam'}, dimensions={0}, use_global_device_ids=true | all-gather | bytes 120 | tf_op jit(solution)/shard_map/all_gather | solution.py:418
  28.6 0.0 copy-start.8
  28.6 7.6 %shard_map.83.refs_4_ = s32[32,128,128]{2,1,0:T(8,128)} custom-call(s32[4]{0:T(128)} %pad_add_fusion.place_ref.refs_0_, s32[2,192,4096]{2,1,0:T(8,128)} %atoms_ref.1), custom_call_target="tpu_custom_call" | custom-call | tf_op jit(solution)/shard_map/pallas_call | solution.py:118
  36.2 3.2 %shard_map.84.refs_7_ = f32[2,2,384,128]{3,2,1,0:T(8,128)} custom-call(f32[8,3]{1,0:T(8,128)} %bitcast.13), custom_call_target="tpu_custom_call" | custom-call | tf_op jit(solution)/shard_map/pallas_call | solution.py:168
  39.4 0.0 collective-permute-done.1.refs_6_
  39.4 0.0 copy-start
  39.4 1.6 %copy-done = s32[32,128,128]{2,1,0:T(8,128)S(1)} copy-done((s32[32,128,128]{2,1,0:T(8,128)S(1)}, s32[32,128,128]{2,1,0:T(8,128)}, u32[]{:S(2)}) %copy-start) | copy-done | bytes 2097176
  41.0 1.1 %copy-done.1 = f32[2,2,384,128]{3,2,1,0:T(8,128)S(1)} copy-done((f32[2,2,384,128]{3,2,1,0:T(8,128)S(1)}, f32[2,2,384,128]{3,2,1,0:T(8,128)}, u32[]{:S(2)}) %copy-start.1) | copy-done | bytes 786456
  42.1 17.4 %shard_map.85 = (bf16[16,64,128]{2,1,0:T(8,128)(2,1)S(1)}, bf16[16,64,128]{2,1,0:T(8,128)(2,1)S(1)}) custom-call(s32[4]{0:T(128)S(1)} %copy-done.7, s32[32,2]{1,0:T(8,128)S(1)} %copy-done.2, s32[64]{0:T(128)S(1)} %fusion.refs_2_, f32[2,4]{1,0:T(2,128)S(1)} %copy-done.8, s32[32,128,128]{2,1,0:T(8,128)S(1)} %copy-done, ...), custom_call_target="tpu_custom_call" | custom-call | tf_op jit(solution)/shard_map/pallas_call | solution.py:340
  59.6 4.0 %collective-permute-start.4 = (bf16[16,64,128]{2,1,0:T(8,128)(2,1)S(1)}, bf16[16,64,128]{2,1,0:T(8,128)(2,1)S(1)}, u32[]{:S(2)}, u32[]{:S(2)}) collective-permute-start(bf16[16,64,128]{2,1,0:T(8,128)(2,1)S(1)} %get-tuple-element.8), channel_id=1, source_target_pairs={{0,23},{8,31},{16,1},{24,9},{1,16},{9,24},{17,2},{25,10},{2,17},{1... | collective-permute-start | bytes 786440 | tf_op jit(solution)/shard_map/ppermute | solution.py:410
  63.6 0.0 collective-permute-start.3
  63.6 2.9 %collective-permute-start.5 = (bf16[16,64,128]{2,1,0:T(8,128)(2,1)S(1)}, bf16[16,64,128]{2,1,0:T(8,128)(2,1)S(1)}, u32[]{:S(2)}, u32[]{:S(2)}) collective-permute-start(bf16[16,64,128]{2,1,0:T(8,128)(2,1)S(1)} %get-tuple-element.7.refs_0_), channel_id=1, source_target_pairs={{0,8},{8,0},{16,24},{24,16},{1,9},{9,1},{17,25},{25,17},{2,10},{10... | collective-permute-start | bytes 786440 | tf_op jit(solution)/shard_map/ppermute | solution.py:410
  66.6 5.1 %collective-permute-done.4.refs_3_ = bf16[16,64,128]{2,1,0:T(8,128)(2,1)S(1)} collective-permute-done((bf16[16,64,128]{2,1,0:T(8,128)(2,1)S(1)}, bf16[16,64,128]{2,1,0:T(8,128)(2,1)S(1)}, u32[]{:S(2)}, u32[]{:S(2)}) %collective-permute-start.4) | collective-permute-done | bytes 262176 | tf_op jit(solution)/shard_map/ppermute | solution.py:410
  71.7 1.5 %collective-permute-start.8 = (bf16[16,64,128]{2,1,0:T(8,128)(2,1)S(1)}, bf16[16,64,128]{2,1,0:T(8,128)(2,1)S(1)}, u32[]{:S(2)}, u32[]{:S(2)}) collective-permute-start(bf16[16,64,128]{2,1,0:T(8,128)(2,1)S(1)} %collective-permute-done.4.refs_3_), channel_id=1, source_target_pairs={{0,8},{8,0},{16,24},{24,16},{1,9},{9,1},{17,25},{25,17},{2,10},{10... | collective-permute-start | bytes 786440 | tf_op jit(solution)/shard_map/ppermute | solution.py:410
  73.2 0.5 collective-permute-done.3.refs_2_
  73.6 2.4 %collective-permute-start.7 = (bf16[16,64,128]{2,1,0:T(8,128)(2,1)S(1)}, bf16[16,64,128]{2,1,0:T(8,128)(2,1)S(1)}, u32[]{:S(2)}, u32[]{:S(2)}) collective-permute-start(bf16[16,64,128]{2,1,0:T(8,128)(2,1)S(1)} %collective-permute-done.3.refs_2_), channel_id=1, source_target_pairs={{0,8},{8,0},{16,24},{24,16},{1,9},{9,1},{17,25},{25,17},{2,10},{10... | collective-permute-start | bytes 786440 | tf_op jit(solution)/shard_map/ppermute | solution.py:410
  76.1 1.9 %collective-permute-done.2.refs_1_ = bf16[16,64,128]{2,1,0:T(8,128)(2,1)S(1)} collective-permute-done((bf16[16,64,128]{2,1,0:T(8,128)(2,1)S(1)}, bf16[16,64,128]{2,1,0:T(8,128)(2,1)S(1)}, u32[]{:S(2)}, u32[]{:S(2)}) %collective-permute-start.2) | collective-permute-done | bytes 262176 | tf_op jit(solution)/shard_map/ppermute | solution.py:410
  78.0 0.1 collective-permute-start.6
  78.1 0.0 collective-permute-done.5.refs_4_
  78.1 0.0 collective-permute-done.8.refs_7_
  78.1 0.0 collective-permute-done.7.refs_6_
  78.1 1.4 %collective-permute-done.6.refs_5_ = bf16[16,64,128]{2,1,0:T(8,128)(2,1)S(1)} collective-permute-done((bf16[16,64,128]{2,1,0:T(8,128)(2,1)S(1)}, bf16[16,64,128]{2,1,0:T(8,128)(2,1)S(1)}, u32[]{:S(2)}, u32[]{:S(2)}) %collective-permute-start.6) | collective-permute-done | bytes 262176 | tf_op jit(solution)/shard_map/ppermute | solution.py:410
  79.6 0.7 copy-done.15
  80.2 5.5 %shard_map.86 = f32[32,16384]{1,0:T(8,128)} custom-call(s32[4]{0:T(128)} %pad_add_fusion.place_ref.refs_0_, s32[32,2]{1,0:T(8,128)} %copy.16.pos_ref.refs_1_, bf16[16,64,128]{2,1,0:T(8,128)(2,1)} %copy-done.3, bf16[16,64,128]{2,1,0:T(8,128)(2,1)} %copy-done.11, bf16[16,64,128]{2,1,0:T(8,128)(2,1)} %copy-done.10, bf16[16,64,128]{2,1,0:T(8,128)(2,1)} %copy-done.9, ...), custom_call_target="tpu_custom_call" | custom-call | tf_op jit(solution)/shard_map/pallas_call | solution.py:375
  (34 shorter events, 0.1 us)
Async XLA Ops:
  2.0 20.9 %copy-start.17 = (f32[2]{0:T(128)S(1)}, f32[2]{0:T(128)}, u32[]{:S(2)}) copy-start(f32[2]{0:T(128)} %param.10) | copy-start | bytes 28
  2.0 21.0 %copy-start.16 = (s32[2,2]{1,0:T(2,128)S(1)}, s32[2,2]{1,0:T(2,128)}, u32[]{:S(2)}) copy-start(s32[2,2]{1,0:T(2,128)} %param.11) | copy-start | bytes 52
  6.2 16.7 %collective-permute-start = (s16[112,2048]{1,0:T(8,128)(2,1)}, s16[112,2048]{1,0:T(8,128)(2,1)S(1)}, u32[]{:S(2)}, u32[]{:S(2)}) collective-permute-start(s16[112,2048]{1,0:T(8,128)(2,1)} %shard_map.82), channel_id=1, source_target_pairs={{0,1},{8,9},{16,23},{24,31},{1,2},{9,10},{17,16},{25,24},{2,3},{10... | collective-permute-start | bytes 1376264 | tf_op jit(solution)/shard_map/ppermute | solution.py:410
  22.9 16.5 %collective-permute-start.1 = (s16[112,2048]{1,0:T(8,128)(2,1)S(1)}, s16[112,2048]{1,0:T(8,128)(2,1)S(1)}, u32[]{:S(2)}, u32[]{:S(2)}) collective-permute-start(s16[112,2048]{1,0:T(8,128)(2,1)S(1)} %collective-permute-done.refs_5_), channel_id=1, source_target_pairs={{0,8},{8,0},{16,24},{24,16},{1,9},{9,1},{17,25},{25,17},{2,10},{10... | collective-permute-start | bytes 1376264 | tf_op jit(solution)/shard_map/ppermute | solution.py:410
  28.6 10.8 %copy-start.2 = (s32[32,2]{1,0:T(8,128)S(1)}, s32[32,2]{1,0:T(8,128)}, u32[]{:S(2)}) copy-start(s32[32,2]{1,0:T(8,128)} %copy.16.pos_ref.refs_1_) | copy-start | bytes 772
  28.6 10.8 %copy-start.4 = (bf16[512,256]{1,0:T(8,128)(2,1)S(1)}, bf16[512,256]{1,0:T(8,128)(2,1)}, u32[]{:S(2)}) copy-start(bf16[512,256]{1,0:T(8,128)(2,1)} %constant.56.clone.refs_8_) | copy-start | bytes 786436
  28.6 10.8 %copy-start.5 = (bf16[256,256]{1,0:T(8,128)(2,1)S(1)}, bf16[256,256]{1,0:T(8,128)(2,1)}, u32[]{:S(2)}) copy-start(bf16[256,256]{1,0:T(8,128)(2,1)} %constant.57.clone.refs_9_) | copy-start | bytes 393220
  28.6 10.8 %copy-start.6 = (bf16[128,256]{1,0:T(8,128)(2,1)S(1)}, bf16[128,256]{1,0:T(8,128)(2,1)}, u32[]{:S(2)}) copy-start(bf16[128,256]{1,0:T(8,128)(2,1)} %constant.58.clone.refs_10_) | copy-start | bytes 196612
  28.6 10.8 %copy-start.7 = (s32[4]{0:T(128)S(1)}, s32[4]{0:T(128)}, u32[]{:S(2)}) copy-start(s32[4]{0:T(128)} %pad_add_fusion.place_ref.refs_0_) | copy-start | bytes 52
  28.6 10.8 %copy-start.8 = (f32[2,4]{1,0:T(2,128)S(1)}, f32[2,4]{1,0:T(2,128)}, u32[]{:S(2)}) copy-start(f32[2,4]{1,0:T(2,128)} %refs_3_.1) | copy-start | bytes 100
  39.4 1.6 %copy-start = (s32[32,128,128]{2,1,0:T(8,128)S(1)}, s32[32,128,128]{2,1,0:T(8,128)}, u32[]{:S(2)}) copy-start(s32[32,128,128]{2,1,0:T(8,128)} %shard_map.83.refs_4_) | copy-start | bytes 6291460
  41.0 1.1 %copy-start.1 = (f32[2,2,384,128]{3,2,1,0:T(8,128)S(1)}, f32[2,2,384,128]{3,2,1,0:T(8,128)}, u32[]{:S(2)}) copy-start(f32[2,2,384,128]{3,2,1,0:T(8,128)} %shard_map.84.refs_7_) | copy-start | bytes 2359300
  59.6 19.9 %copy-start.3 = (bf16[16,64,128]{2,1,0:T(8,128)(2,1)}, bf16[16,64,128]{2,1,0:T(8,128)(2,1)S(1)}, u32[]{:S(2)}) copy-start(bf16[16,64,128]{2,1,0:T(8,128)(2,1)S(1)} %get-tuple-element.7.refs_0_) | copy-start | bytes 786436
  59.6 12.1 %collective-permute-start.4 = (bf16[16,64,128]{2,1,0:T(8,128)(2,1)S(1)}, bf16[16,64,128]{2,1,0:T(8,128)(2,1)S(1)}, u32[]{:S(2)}, u32[]{:S(2)}) collective-permute-start(bf16[16,64,128]{2,1,0:T(8,128)(2,1)S(1)} %get-tuple-element.8), channel_id=1, source_target_pairs={{0,23},{8,31},{16,1},{24,9},{1,16},{9,24},{17,2},{25,10},{2,17},{1... | collective-permute-start | bytes 786440 | tf_op jit(solution)/shard_map/ppermute | solution.py:410
  63.6 10.0 %collective-permute-start.3 = (bf16[16,64,128]{2,1,0:T(8,128)(2,1)S(1)}, bf16[16,64,128]{2,1,0:T(8,128)(2,1)S(1)}, u32[]{:S(2)}, u32[]{:S(2)}) collective-permute-start(bf16[16,64,128]{2,1,0:T(8,128)(2,1)S(1)} %get-tuple-element.8), channel_id=1, source_target_pairs={{0,7},{8,15},{16,17},{24,25},{1,0},{9,8},{17,18},{25,26},{2,1},{10... | collective-permute-start | bytes 786440 | tf_op jit(solution)/shard_map/ppermute | solution.py:410
  63.6 14.3 %collective-permute-start.2 = (bf16[16,64,128]{2,1,0:T(8,128)(2,1)S(1)}, bf16[16,64,128]{2,1,0:T(8,128)(2,1)S(1)}, u32[]{:S(2)}, u32[]{:S(2)}) collective-permute-start(bf16[16,64,128]{2,1,0:T(8,128)(2,1)S(1)} %get-tuple-element.7.refs_0_), channel_id=1, source_target_pairs={{0,16},{8,24},{16,0},{24,8},{1,17},{9,25},{17,1},{25,9},{2,18},{10... | collective-permute-start | bytes 786440 | tf_op jit(solution)/shard_map/ppermute | solution.py:410
  63.6 14.4 %collective-permute-start.5 = (bf16[16,64,128]{2,1,0:T(8,128)(2,1)S(1)}, bf16[16,64,128]{2,1,0:T(8,128)(2,1)S(1)}, u32[]{:S(2)}, u32[]{:S(2)}) collective-permute-start(bf16[16,64,128]{2,1,0:T(8,128)(2,1)S(1)} %get-tuple-element.7.refs_0_), channel_id=1, source_target_pairs={{0,8},{8,0},{16,24},{24,16},{1,9},{9,1},{17,25},{25,17},{2,10},{10... | collective-permute-start | bytes 786440 | tf_op jit(solution)/shard_map/ppermute | solution.py:410
  71.7 7.8 %copy-start.9 = (bf16[16,64,128]{2,1,0:T(8,128)(2,1)}, bf16[16,64,128]{2,1,0:T(8,128)(2,1)S(1)}, u32[]{:S(2)}) copy-start(bf16[16,64,128]{2,1,0:T(8,128)(2,1)S(1)} %collective-permute-done.4.refs_3_) | copy-start | bytes 786436
  71.7 6.4 %collective-permute-start.8 = (bf16[16,64,128]{2,1,0:T(8,128)(2,1)S(1)}, bf16[16,64,128]{2,1,0:T(8,128)(2,1)S(1)}, u32[]{:S(2)}, u32[]{:S(2)}) collective-permute-start(bf16[16,64,128]{2,1,0:T(8,128)(2,1)S(1)} %collective-permute-done.4.refs_3_), channel_id=1, source_target_pairs={{0,8},{8,0},{16,24},{24,16},{1,9},{9,1},{17,25},{25,17},{2,10},{10... | collective-permute-start | bytes 786440 | tf_op jit(solution)/shard_map/ppermute | solution.py:410
  73.6 5.9 %copy-start.10 = (bf16[16,64,128]{2,1,0:T(8,128)(2,1)}, bf16[16,64,128]{2,1,0:T(8,128)(2,1)S(1)}, u32[]{:S(2)}) copy-start(bf16[16,64,128]{2,1,0:T(8,128)(2,1)S(1)} %collective-permute-done.3.refs_2_) | copy-start | bytes 786436
  73.6 4.5 %collective-permute-start.7 = (bf16[16,64,128]{2,1,0:T(8,128)(2,1)S(1)}, bf16[16,64,128]{2,1,0:T(8,128)(2,1)S(1)}, u32[]{:S(2)}, u32[]{:S(2)}) collective-permute-start(bf16[16,64,128]{2,1,0:T(8,128)(2,1)S(1)} %collective-permute-done.3.refs_2_), channel_id=1, source_target_pairs={{0,8},{8,0},{16,24},{24,16},{1,9},{9,1},{17,25},{25,17},{2,10},{10... | collective-permute-start | bytes 786440 | tf_op jit(solution)/shard_map/ppermute | solution.py:410
  78.0 1.6 %copy-start.11 = (bf16[16,64,128]{2,1,0:T(8,128)(2,1)}, bf16[16,64,128]{2,1,0:T(8,128)(2,1)S(1)}, u32[]{:S(2)}) copy-start(bf16[16,64,128]{2,1,0:T(8,128)(2,1)S(1)} %collective-permute-done.2.refs_1_) | copy-start | bytes 786436
  78.0 1.5 %collective-permute-start.6 = (bf16[16,64,128]{2,1,0:T(8,128)(2,1)S(1)}, bf16[16,64,128]{2,1,0:T(8,128)(2,1)S(1)}, u32[]{:S(2)}, u32[]{:S(2)}) collective-permute-start(bf16[16,64,128]{2,1,0:T(8,128)(2,1)S(1)} %collective-permute-done.2.refs_1_), channel_id=1, source_target_pairs={{0,8},{8,0},{16,24},{24,16},{1,9},{9,1},{17,25},{25,17},{2,10},{10... | collective-permute-start | bytes 786440 | tf_op jit(solution)/shard_map/ppermute | solution.py:410
  78.1 1.4 %copy-start.12 = (bf16[16,64,128]{2,1,0:T(8,128)(2,1)}, bf16[16,64,128]{2,1,0:T(8,128)(2,1)S(1)}, u32[]{:S(2)}) copy-start(bf16[16,64,128]{2,1,0:T(8,128)(2,1)S(1)} %collective-permute-done.5.refs_4_) | copy-start | bytes 786436
  78.1 1.4 %copy-start.13 = (bf16[16,64,128]{2,1,0:T(8,128)(2,1)}, bf16[16,64,128]{2,1,0:T(8,128)(2,1)S(1)}, u32[]{:S(2)}) copy-start(bf16[16,64,128]{2,1,0:T(8,128)(2,1)S(1)} %collective-permute-done.8.refs_7_) | copy-start | bytes 786436
  78.1 1.4 %copy-start.14 = (bf16[16,64,128]{2,1,0:T(8,128)(2,1)}, bf16[16,64,128]{2,1,0:T(8,128)(2,1)S(1)}, u32[]{:S(2)}) copy-start(bf16[16,64,128]{2,1,0:T(8,128)(2,1)S(1)} %collective-permute-done.7.refs_6_) | copy-start | bytes 786436
  79.5 0.7 copy-start.15

commit v2 on v1

v2 whole, which is shorter than its diff:
```python
import math

import jax
import jax.numpy as jnp
import ml_dtypes
import numpy as np
from jax import lax
from jax.experimental import pallas as pl
from jax.experimental.pallas import tpu as pltpu
from jax.sharding import PartitionSpec as P

HALFW = 32
TYPES = 4
WIN = 128
LANES = 128
GROUP = 64
HALO0 = 64
HALO1 = 32
TABLE = 384
MIB = 1024 * 1024


def taps(offset):
    steps = np.arange(-HALFW, HALFW + 1, dtype=np.float32)
    weights = 1.0 - 0.5 * (steps / (HALFW + 1.0)) ** 2
    scale = np.sqrt(np.sum(weights * weights))
    offset = offset.astype(np.float32)
    weight = (1.0 - 0.5 * (offset / (HALFW + 1.0)) ** 2) / scale
    chirp = np.float32(math.pi) * offset * offset / np.float32(2.0 * HALFW + 1.0)
    inside = np.abs(offset) <= HALFW
    real = np.where(inside, np.cos(chirp) * weight, 0.0)
    imag = np.where(inside, np.sin(chirp) * weight, 0.0)
    return real.astype(np.float32), imag.astype(np.float32)


def x_matrix(sources, targets):
    rows = []
    for start in range(0, len(sources), LANES):
        src = sources[start : start + LANES]
        real, imag = taps(targets[None, :] - src[:, None] + HALFW)
        rows.append(np.concatenate([real, imag], axis=1))
        rows.append(np.concatenate([-imag, real], axis=1))
    return np.concatenate(rows, axis=0).astype(ml_dtypes.bfloat16)


def y_matrix():
    out = np.arange(GROUP)[:, None]
    src = np.arange(2 * GROUP)[None, :]
    real, imag = taps(out - src + HALFW)
    upper = np.concatenate([real, -imag], axis=1)
    lower = np.concatenate([imag, real], axis=1)
    return np.concatenate([upper, lower], axis=0).astype(ml_dtypes.bfloat16)


def matrices():
    first = x_matrix(np.arange(2 * LANES), np.arange(LANES))
    second = x_matrix(np.arange(LANES, 2 * LANES), np.arange(LANES, 2 * LANES))
    second = second.reshape(2 * LANES, 2, LANES)
    second[:, :, LANES // 2 :] = 0
    return first, second.reshape(2 * LANES, 2 * LANES), y_matrix()


def pack_kernel(place_ref, atoms_hbm, zero_ref, one_ref, zero_buf, one_buf, sems):
    half = zero_ref.shape[1]
    rows = atoms_hbm.shape[1]
    side, core = place_ref[0], place_ref[1]
    step = half // 2
    copies = []
    for layer, buf in ((0, zero_buf), (1, one_buf)):
        depth = buf.shape[0]
        top = pl.multiple_of((1 - side) * (rows - depth), depth)
        for part in range(2):
            left = pl.multiple_of(core * half + part * step, LANES)
            copies.append(
                pltpu.make_async_copy(
                    atoms_hbm.at[layer, pl.ds(top, depth), pl.ds(left, step)],
                    buf.at[:, pl.ds(part * step, step)],
                    sems.at[2 * layer + part],
                )
            )
    for copy in copies:
        copy.start()
    for layer, (buf, out_ref) in enumerate(((zero_buf, zero_ref), (one_buf, one_ref))):
        for part in range(2):
            copies[2 * layer + part].wait()
            cols = slice(part * step, (part + 1) * step)
            out_ref[:, cols] = buf[:, cols].astype(jnp.int16)


def pack_rows(place, atoms):
    half = atoms.shape[2] // 2
    vmem = pl.BlockSpec(memory_space=pltpu.VMEM)
    return pl.pallas_call(
        pack_kernel,
        out_shape=[jax.ShapeDtypeStruct((depth, half), jnp.int16) for depth in (HALO0, HALO1)],
        in_specs=[pl.BlockSpec(memory_space=pltpu.SMEM), pl.BlockSpec(memory_space=pltpu.HBM)],
        out_specs=[vmem, vmem],
        scratch_shapes=[
            pltpu.VMEM((HALO0, half), jnp.int32),
            pltpu.VMEM((HALO1, half), jnp.int32),
            pltpu.SemaphoreType.DMA((4,)),
        ],
        compiler_params=pltpu.CompilerParams(vmem_limit_bytes=60 * MIB),
    )(place, atoms)


def words_kernel(place_ref, atoms_hbm, out_ref, buf, sems):
    upper = place_ref[0] == 1
    parts = sems.shape[0]
    step = buf.shape[2] // parts
    copies = [
        pltpu.make_async_copy(
            atoms_hbm.at[:, :, pl.ds(k * step, step)], buf.at[:, :, pl.ds(k * step, step)], sems.at[k]
        )
        for k in range(parts)
    ]
    for copy in copies:
        copy.start()
    for k in range(parts):
        copies[k].wait()
        for tile in range(k * step // LANES, (k + 1) * step // LANES):
            at = slice(tile * LANES, (tile + 1) * LANES)
            codes = []
            for g in range(3):
                rows = slice(g * GROUP, (g + 1) * GROUP)
                codes.append(buf[0, rows, at] + TYPES * buf[1, rows, at])
            own = codes[0] | (codes[1] << 8) | (codes[2] << 16)
            low = (codes[0] << 8) | (codes[1] << 16)
            high = codes[1] | (codes[2] << 8)
            out_ref[tile, 0:GROUP, :] = jnp.where(upper, own, low)
            out_ref[tile, GROUP:, :] = jnp.where(upper, high, own)


def own_words(place, atoms):
    width = atoms.shape[2]
    return pl.pallas_call(
        words_kernel,
        out_shape=pltpu.VMEM((width // LANES, 2 * GROUP, LANES), jnp.int32),
        in_specs=[pl.BlockSpec(memory_space=pltpu.SMEM), pl.BlockSpec(memory_space=pltpu.HBM)],
        out_specs=pl.BlockSpec(memory_space=pltpu.VMEM),
        scratch_shapes=[pltpu.VMEM(atoms.shape, jnp.int32), pltpu.SemaphoreType.DMA((8,))],
        compiler_params=pltpu.CompilerParams(vmem_limit_bytes=60 * MIB),
        cost_estimate=pl.CostEstimate(flops=20 * atoms.size, bytes_accessed=6 * atoms.size, transcendentals=0),
    )(place, atoms)


def cos_turns(turns):
    angle = (2.0 * math.pi) * (0.25 - jnp.abs(turns - jnp.round(turns)))
    square = angle * angle
    total = jnp.full_like(square, 1.0)
    for k in (12, 10, 8, 6, 4, 2):
        total = 1.0 - square * total * (1.0 / (k * (k + 1)))
    return angle * total


def probe_kernel(rows_total, width, beam_ref, phase_ref, out_ref, values_ref):
    beams = beam_ref.shape[0]
    precise = lax.Precision.HIGHEST
    lane = lax.broadcasted_iota(jnp.int32, (1, LANES), 1)
    tilt_y = jnp.zeros((1, LANES), jnp.float32)
    for beam in range(beams):
        tilt_y = jnp.where(lane % beams == beam, beam_ref[beam, 1], tilt_y)
    quarter = jnp.where(lane < beams, 0.0, 0.25)
    row = lax.broadcasted_iota(jnp.int32, (TABLE, LANES), 0) - TABLE // 2
    along_y = cos_turns(row.astype(jnp.float32) * tilt_y / rows_total - quarter)
    along_y = jnp.where(lane < 2 * beams, along_y, 0.0)

    sub = lax.broadcasted_iota(jnp.int32, (2 * beams, 1), 0)
    tilt_x = jnp.zeros((2 * beams, 1), jnp.float32)
    weight = jnp.zeros((2 * beams, 1), jnp.float32)
    for beam in range(beams):
        tilt_x = jnp.where(sub % beams == beam, beam_ref[beam, 0], tilt_x)
        weight = jnp.where(sub % beams == beam, beam_ref[beam, 2], weight)
    col = lax.broadcasted_iota(jnp.int32, (2 * beams, 2 * LANES), 1) - LANES
    turns = col.astype(jnp.float32) * tilt_x / width
    shift = jnp.where(sub < beams, 0.0, 0.25)
    right_re = weight * cos_turns(turns + shift)
    right_im = weight * cos_turns(turns + shift - 0.25)
    right = jnp.concatenate([right_re, right_im], axis=1)
    right = jnp.concatenate([right, jnp.zeros((LANES - 2 * beams, 4 * LANES), jnp.float32)], axis=0)
    table = jnp.dot(along_y, right, precision=precise, preferred_element_type=jnp.float32)
    for part in range(2):
        for tile in range(2):
            lo = (2 * part + tile) * LANES
            out_ref[part, tile] = table[:, lo : lo + LANES]

    sub = lax.broadcasted_iota(jnp.int32, (4 * TYPES, LANES), 0)
    angle = jnp.zeros((4 * TYPES, LANES), jnp.float32)
    for layer in range(2):
        for kind in range(TYPES):
            mine = (sub // (2 * TYPES) == layer) & (sub % TYPES == kind)
            angle = jnp.where(mine, phase_ref[layer, kind], angle)
    quarter = jnp.where((sub // TYPES) % 2 == 0, 0.0, 0.25)
    values_ref[...] = cos_turns(angle * (0.5 / math.pi) - quarter)


def probe_table(beam_rows, phases, rows_total, width):
    def kernel(*refs):
        probe_kernel(rows_total, width, *refs)

    smem = pl.BlockSpec(memory_space=pltpu.SMEM)
    vmem = pl.BlockSpec(memory_space=pltpu.VMEM)
    return pl.pallas_call(
        kernel,
        out_shape=[pltpu.VMEM((2, 2, TABLE, LANES), jnp.float32), pltpu.VMEM((4 * TYPES, LANES), jnp.float32)],
        in_specs=[smem, smem],
        out_specs=[vmem, vmem],
        cost_estimate=pl.CostEstimate(flops=10**8, bytes_accessed=10**6, transcendentals=10**5),
    )(beam_rows, phases)


def main_kernel(
    beams,
    place_ref,
    pos_ref,
    near_ref,
    words_in,
    mine0_ref,
    mine1_ref,
    other0_ref,
    other1_ref,
    table_ref,
    values_ref,
    first_ref,
    second_ref,
    ymat_ref,
    own_hbm,
    ext_hbm,
    words,
    left,
    right,
    middle,
    result,
    row_list,
    col_list,
    slot_list,
    sems,
):
    side, core, row_base, near_base = place_ref[0], place_ref[1], place_ref[2], place_ref[3]
    tiles = words.shape[0]
    half_tiles = tiles // 2
    f32, bf16 = jnp.float32, jnp.bfloat16

    def merge(upper):
        base = GROUP if upper else 0
        sft = 16 if upper else 0
        lo = 0 if upper else GROUP - HALO1
        for zeros, ones, at in ((mine0_ref, mine1_ref, core), (other0_ref, other1_ref, 1 - core)):
            for tile in range(half_tiles):
                cols = slice(tile * LANES, (tile + 1) * LANES)
                zero = zeros[:, cols].astype(jnp.int32)
                one = ones[:, cols].astype(jnp.int32) * TYPES
                pieces = []
                if lo:
                    pieces.append(zero[0:lo])
                pieces.append(zero[lo : lo + HALO1] + one)
                if lo + HALO1 < GROUP:
                    pieces.append(zero[lo + HALO1 :])
                code = jnp.concatenate(pieces, axis=0) << sft
                index = at * half_tiles + tile
                words[index, base : base + GROUP, :] = words_in[index, base : base + GROUP, :] | code

    @pl.when(side == 0)
    def _():
        merge(False)

    @pl.when(side == 1)
    def _():
        merge(True)

    def values(layer):
        rows = [values_ref[2 * TYPES * layer + k : 2 * TYPES * layer + k + 1, :].astype(bf16) for k in range(2 * TYPES)]
        return rows[:TYPES], rows[TYPES:]

    cos0, sin0 = values(0)
    cos1, sin1 = values(1)
    lane = lax.broadcasted_iota(jnp.int32, (1, LANES), 1)

    def transmission(code, bit, cos_v, sin_v):
        b0 = (code & jnp.int16(1 << bit)) != 0
        b1 = (code & jnp.int16(2 << bit)) != 0
        out = []
        for v in (cos_v, sin_v):
            spread = [jnp.broadcast_to(value, code.shape) for value in v]
            out.append(jnp.where(b1, jnp.where(b0, spread[3], spread[2]), jnp.where(b0, spread[1], spread[0])))
        return out

    def probe_window(t, buf, mid_buf):
        row, col = row_list[t], col_list[t]
        start = jnp.clip(row - GROUP, 0, GROUP)
        delta = start - GROUP * (1 - side) - row + TABLE // 2
        tile0 = col // LANES + tiles - 1
        shift = lax.rem(col, LANES)
        back = lax.rem(LANES - shift, LANES)
        rolled = []
        for j in range(3):
            word = words[lax.rem(tile0 + j, tiles), pl.ds(start, GROUP), :]
            rolled.append(pltpu.roll(word, back, 1))
        keep = lane < LANES - shift
        window = [jnp.where(keep, rolled[j], rolled[j + 1]) for j in range(2)]
        turned = [pltpu.roll(w, LANES - HALFW, 1) for w in window]
        inner = [jnp.where(lane < LANES - HALFW, turned[0], turned[1]), turned[1]]
        for j in range(2):
            mid_buf[j, 0] = inner[j].astype(jnp.int16)
            mid_buf[j, 1] = (inner[j] >> 16).astype(jnp.int16)
            codes = (window[j].astype(jnp.int16), (window[j] >> 16).astype(jnp.int16))
            for g in range(3):
                t_re, t_im = transmission(codes[g // 2], 8 * (g % 2), cos0, sin0)
                p_re = table_ref[0, j, pl.ds(delta + g * GROUP, GROUP), :].astype(bf16)
                p_im = table_ref[1, j, pl.ds(delta + g * GROUP, GROUP), :].astype(bf16)
                at = slice(g * GROUP, (g + 1) * GROUP)
                lo = 2 * j * LANES
                buf[at, lo : lo + LANES] = p_re * t_re - p_im * t_im
                buf[at, lo + LANES : lo + 2 * LANES] = p_re * t_im + p_im * t_re

    count = own_hbm.shape[0]

    def own_task(k, carry):
        probe = 2 * k + core
        row_list[k] = pos_ref[probe, 0] - row_base
        col_list[k] = pos_ref[probe, 1]
        slot_list[k] = k
        return carry

    def ext_task(k, found):
        probe = 2 * k + core
        row = near_ref[probe, 0] - near_base
        reaches = jnp.where(side == 0, row > -GROUP, row < 4 * GROUP)
        row_list[found] = row
        col_list[found] = near_ref[probe, 1]
        slot_list[found] = count + k
        return found + reaches.astype(jnp.int32)

    lax.fori_loop(0, count, own_task, 0)
    total = lax.fori_loop(0, count, ext_task, count)

    def step(t, p):
        q = 1 - p
        one = jnp.dot(left[q], first_ref[...], preferred_element_type=f32).astype(bf16)
        two = jnp.dot(left[q, : 3 * GROUP, 2 * LANES :], second_ref[...], preferred_element_type=f32)
        two = two.astype(bf16)
        down = jnp.dot(ymat_ref[...], right[p], preferred_element_type=f32)
        for part in range(2):
            to = slice(2 * GROUP * part, 2 * GROUP * (part + 1))
            cols = slice(part * LANES, (part + 1) * LANES)
            for b in range(2):
                rows = slice(b * GROUP, b * GROUP + 2 * GROUP)
                right[q, to, 2 * b * LANES : (2 * b + 1) * LANES] = one[rows, cols]
                right[q, to, (2 * b + 1) * LANES : (2 * b + 2) * LANES] = two[rows, cols]
            right[q, to, 4 * LANES :] = one[3 * GROUP :, cols]
        for b in range(2):
            for j in range(2):
                lo = (2 * b + j) * LANES
                cols = slice(2 * j * LANES, (2 * j + 1) * LANES)
                imag_cols = slice((2 * j + 1) * LANES, (2 * j + 2) * LANES)
                for part in range(2):
                    group = b + part
                    code = middle[p, j, group // 2, (1 - part) * HALO1 : (2 - part) * HALO1]
                    t_re, t_im = transmission(code, 8 * (group % 2) + 2, cos1, sin1)
                    d_re = down[part * HALO1 : (part + 1) * HALO1, lo : lo + LANES].astype(bf16)
                    d_im = down[GROUP + part * HALO1 : GROUP + (part + 1) * HALO1, lo : lo + LANES].astype(bf16)
                    first_row = (3 + b) * GROUP + part * HALO1
                    rows = slice(first_row, first_row + HALO1)
                    left[p, rows, cols] = d_re * t_re - d_im * t_im
                    left[p, rows, imag_cols] = d_re * t_im + d_im * t_re
        exit_wave = down[:, 4 * LANES :].astype(bf16).astype(f32)
        re, im = exit_wave[:GROUP], exit_wave[GROUP:]
        slot = slot_list[jnp.clip(t - 4, 0, total - 1)]
        result[slot] = ((re * re + im * im) * (1.0 / beams)).astype(bf16)
        probe_window(jnp.minimum(t, total - 1), left.at[p], middle.at[p])

    def steps(i, carry):
        step(2 * i, 0)
        step(2 * i + 1, 1)
        return carry

    lax.fori_loop(0, (total + 5) // 2, steps, 0)
    copies = [
        pltpu.make_async_copy(result.at[pl.ds(0, count)], own_hbm, sems.at[0]),
        pltpu.make_async_copy(result.at[pl.ds(count, count)], ext_hbm, sems.at[1]),
    ]
    for copy in copies:
        copy.start()
    for copy in copies:
        copy.wait()


def propagate(beams, place, positions, near, words, halo, table):
    count = positions.shape[0] // 2
    first, second, ymat = matrices()
    smem = pl.BlockSpec(memory_space=pltpu.SMEM)
    vmem = pl.BlockSpec(memory_space=pltpu.VMEM)
    hbm = pl.BlockSpec(memory_space=pltpu.HBM)

    def kernel(*refs):
        main_kernel(beams, *refs)

    shape = jax.ShapeDtypeStruct((count, GROUP, WIN), jnp.bfloat16)
    own, ext, _ = pl.pallas_call(
        kernel,
        out_shape=[shape, shape, pltpu.VMEM(words.shape, jnp.int32)],
        in_specs=[smem] * 3 + [vmem] * 10,
        out_specs=[hbm, hbm, vmem],
        input_output_aliases={3: 2},
        scratch_shapes=[
            pltpu.VMEM((2, 5 * GROUP, 4 * LANES), jnp.bfloat16),
            pltpu.VMEM((2, 4 * GROUP, 5 * LANES), jnp.bfloat16),
            pltpu.VMEM((2, 2, 2, GROUP, LANES), jnp.int16),
            pltpu.VMEM((2 * count, GROUP, WIN), jnp.bfloat16),
            pltpu.SMEM((2 * count + 1,), jnp.int32),
            pltpu.SMEM((2 * count + 1,), jnp.int32),
            pltpu.SMEM((2 * count + 1,), jnp.int32),
            pltpu.SemaphoreType.DMA((2,)),
        ],
        compiler_params=pltpu.CompilerParams(vmem_limit_bytes=40 * MIB),
    )(place, positions, near, words, *halo, *table, first, second, ymat)
    return own, ext


PAD = 3 * WIN


def gather_kernel(place_ref, pos_ref, *refs):
    out_hbm, window, out_buf, sems = refs[8:]
    side, core, row_base = place_ref[0], place_ref[1], place_ref[2]

    def copy(group):
        rows = pl.ds(pl.multiple_of(8 * group, 8), 8)
        return pltpu.make_async_copy(out_buf.at[rows], out_hbm.at[rows], sems.at[group])

    def step(group, carry):
        for par in range(2):
            parity = core if par == 0 else 1 - core
            for i in range(4):
                k = 4 * group + i
                row = pos_ref[2 * k + parity, 0] - row_base
                start = jnp.where(row < GROUP, row, jnp.where(row > 2 * GROUP, row - GROUP, GROUP))
                base = (2 * i + parity) * PAD + WIN - start
                places = (GROUP + GROUP * side, 2 * GROUP - GROUP * side, 3 * GROUP * (1 - side), 3 * GROUP * side)
                for piece, at in zip(refs[4 * par : 4 * par + 4], places):
                    window[pl.ds(base + at, GROUP), :] = piece[k].astype(jnp.float32)
        rows = pl.ds(pl.multiple_of(8 * group, 8), 8)
        for u in range(WIN):
            out_buf[rows, u * WIN : (u + 1) * WIN] = window[pl.ds(WIN + u, 8, stride=PAD), :]
        copy(group).start()
        return carry

    groups = out_buf.shape[0] // 8
    lax.fori_loop(0, groups, step, 0)
    for group in range(groups):
        copy(group).wait()


def put_together(place, positions, pieces):
    probes = positions.shape[0]
    smem = pl.BlockSpec(memory_space=pltpu.SMEM)
    vmem = pl.BlockSpec(memory_space=pltpu.VMEM)
    return pl.pallas_call(
        gather_kernel,
        out_shape=jax.ShapeDtypeStruct((probes, WIN * WIN), jnp.float32),
        in_specs=[smem, smem] + [vmem] * 8,
        out_specs=pl.BlockSpec(memory_space=pltpu.HBM),
        scratch_shapes=[
            pltpu.VMEM((8 * PAD, LANES), jnp.float32),
            pltpu.VMEM((probes, WIN * WIN), jnp.float32),
            pltpu.SemaphoreType.DMA((probes // 8,)),
        ],
        compiler_params=pltpu.CompilerParams(vmem_limit_bytes=16 * MIB),
    )(place, positions, *pieces)


def local(atoms, phases, aperture, tilts, positions):
    rows_here, width = atoms.shape[1], atoms.shape[2]
    probes = positions.shape[0]
    strip, beam = lax.axis_index("strip"), lax.axis_index("beam")
    strips, ways = lax.axis_size("strip"), lax.axis_size("beam")
    rows_total = rows_here * strips
    beams = tilts.shape[0] * ways
    cores = 2
    side, core = beam // cores, beam % cores
    near_strip = jnp.where(side == 0, strip - 1 + strips, strip + 1) % strips
    near_base = near_strip * rows_here + jnp.where(side == 0, rows_here, -rows_here)
    place = jnp.stack([side, core, strip * rows_here, near_base]).astype(jnp.int32)

    def across(array, dest):
        pairs = []
        for s in range(strips):
            for b in range(ways):
                to_s, to_b = dest(s, b // cores, b % cores)
                pairs.append((b * strips + s, (to_b[0] * cores + to_b[1]) * strips + to_s % strips))
        return lax.ppermute(array, ("beam", "strip"), pairs)

    def swap_cores(array):
        return across(array, lambda s, y, c: (s, (y, 1 - c)))

    packed = pack_rows(place, atoms)
    mine = [across(rows, lambda s, y, c: (s + 1 - 2 * y, (y, c))) for rows in packed]
    packed, positions, tilts, aperture = lax.optimization_barrier((packed, positions, tilts, aperture))
    near = across(positions, lambda s, y, c: (s + 1 - 2 * y, (y, c)))
    beam_rows = jnp.concatenate([tilts.astype(jnp.float32), aperture[:, None]], axis=1)
    beam_rows = [
        beam_rows,
        swap_cores(beam_rows),
        across(beam_rows, lambda s, y, c: (s, (1 - y, c))),
        across(beam_rows, lambda s, y, c: (s, (1 - y, 1 - c))),
    ]
    beam_rows = jnp.concatenate(beam_rows, axis=0)
    words = own_words(place, atoms)
    table = probe_table(beam_rows, phases, rows_total, width)
    mine, near, words, table = lax.optimization_barrier((mine, near, words, table))
    other = [swap_cores(rows) for rows in mine]
    halo = mine + other
    own, ext = propagate(beams, place, positions, near, words, halo, table)
    far = across(ext, lambda s, y, c: (s - 1 + 2 * y, (1 - y, c)))
    same = across(ext, lambda s, y, c: (s - 1 + 2 * y, (y, c)))
    facing = across(own, lambda s, y, c: (s, (1 - y, c)))
    pieces = [own, facing, same, far]
    return put_together(place, positions, pieces + [swap_cores(piece) for piece in pieces])


def solution(mesh):
    in_specs = (P(None, "strip", None), P(), P("beam"), P("beam", None), P("strip", None))
    out_specs = P("strip", None)
    return jax.shard_map(local, mesh=mesh, in_specs=in_specs, out_specs=out_specs, check_vma=False)
```

time: 86.5 us -> 56.7 us (0.66)
  Pallas kernels: 37.9 us -> 21.1 us
  blocking collectives: 5.51 us -> 0 us
  waiting for transfers between devices: 22.6 us -> 17.3 us
  local copies, waits for them, and re-layouts: 4.92 us -> 1.1 us
  starting transfers between devices: 14 us -> 15.4 us
    pallas_call x4, Pallas kernels: 32.4 us -> 17.9 us  [the longest x1 9.75 us: propagate(): pl.pallas_call(kernel, out_shape=[shape, shape, pltpu.VMEM(words.shape, j...]
    all_gather x1 -> x0, blocking collectives: 5.51 us -> none  [local(): beam_rows = lax.all_gather(beam_rows, 'beam', axis=0, tiled=True)]
    ppermute x9 -> x15, waiting for transfers between devices: 22.6 us -> 17.3 us  [across(): return lax.ppermute(array, ('beam', 'strip'), pairs)]
    unnamed x37 -> x14, local copies, waits for them, and re-layouts: 4.83 us -> 0.92 us
    pallas_call x1, Pallas kernels: 5.49 us -> 3.19 us  [put_together(): pl.pallas_call(gather_kernel, out_shape=jax.ShapeDtypeStruct((probes, WIN...]
    ppermute x9 -> x15, starting transfers between devices: 14 us -> 15.4 us  [across(): return lax.ppermute(array, ('beam', 'strip'), pairs)]
  transfers between devices with their start and end apart: 9 -> 15, of which waited for: 5 -> 6; matrix products, arithmetic and copies ran while one was open for 0% -> 2% of each run, Pallas kernels for 13% -> 10%
where the time goes in v2:
time: 56.7 us; the launch traced here: 56.3 us
  Pallas kernels  21.1 us (37%)
  waiting for transfers between devices  17.3 us (31%)
  starting transfers between devices  15.4 us (27%)
  other arithmetic  1.37 us (2%)
  local copies, waits for them, and re-layouts  1.1 us (2%)
    ppermute x15, waiting for transfers between devices, across(): return lax.ppermute(array, ('beam', 'strip'), pairs)  17.3 us
    ppermute x15, starting transfers between devices, across(): return lax.ppermute(array, ('beam', 'strip'), pairs)  15.4 us
    pallas_call x1, Pallas kernels, propagate(): pl.pallas_call(kernel, out_shape=[shape, shape, pltpu.VMEM(words.shape, j...  9.75 us
    pallas_call x1, Pallas kernels, own_words(): pl.pallas_call(words_kernel, out_shape=pltpu.VMEM((width // LANES, 2 * GR...  3.77 us
    pallas_call x1, Pallas kernels, put_together(): pl.pallas_call(gather_kernel, out_shape=jax.ShapeDtypeStruct((probes, WIN...  3.19 us
    pallas_call x1, Pallas kernels, pack_rows(): pl.pallas_call(pack_kernel, out_shape=[jax.ShapeDtypeStruct((depth, half)...  2.68 us
    pallas_call x1, Pallas kernels, probe_table(): pl.pallas_call(kernel, out_shape=[pltpu.VMEM((2, 2, TABLE, LANES), jnp.fl...  1.69 us
  transfers between devices with their start and end apart: 15, of which 6 were waited for; matrix products, arithmetic and copies ran while one was open for 2% of the time, Pallas kernels for 10%

profile of v2, /device:TPU:0, one launch (start us, length us, event | category | flops | bytes accessed | tf_op | source)
XLA Modules:
  0.0 56.3 jit_solution(17711398976052511657)
XLA Ops:
  0.0 0.6 %pad_add_fusion.place_ref.refs_0_ = s32[4]{0:T(128)} fusion(s32[1]{0:T(128)} %bitcast.3, s32[1]{0:T(128)} %bitcast.2, s32[1]{0:T(128)} %bitcast.1, s32[1]{0:T(128)} %bitcast), kind=kLoop, calls=%fused_computation.2 | loop fusion | flops 12 | bytes 32 | tf_op jit(solution)/shard_map/stack | solution.py:483
  0.6 2.7 %shard_map.82 = (s16[64,2048]{1,0:T(8,128)(2,1)}, s16[32,2048]{1,0:T(8,128)(2,1)}) custom-call(s32[4]{0:T(128)} %pad_add_fusion.place_ref.refs_0_, s32[2,192,4096]{2,1,0:T(8,128)} %atoms_hbm.3), custom_call_target="tpu_custom_call" | custom-call | tf_op jit(solution)/shard_map/pallas_call | solution.py:93
  3.3 3.0 %collective-permute-start = (s16[64,2048]{1,0:T(8,128)(2,1)}, s16[64,2048]{1,0:T(8,128)(2,1)S(1)}, u32[]{:S(2)}, u32[]{:S(2)}) collective-permute-start(s16[64,2048]{1,0:T(8,128)(2,1)} %get-tuple-element.20), channel_id=1, source_target_pairs={{0,1},{8,9},{16,23},{24,31},{1,2},{9,10},{17,16},{25,24},{2,3},{10... | collective-permute-start | bytes 786440 | tf_op jit(solution)/shard_map/ppermute | solution.py:491
  6.3 1.5 %collective-permute-start.1 = (s16[32,2048]{1,0:T(8,128)(2,1)}, s16[32,2048]{1,0:T(8,128)(2,1)}, u32[]{:S(2)}, u32[]{:S(2)}) collective-permute-start(s16[32,2048]{1,0:T(8,128)(2,1)} %get-tuple-element.21), channel_id=1, source_target_pairs={{0,1},{8,9},{16,23},{24,31},{1,2},{9,10},{17,16},{25,24},{2,3},{10... | collective-permute-start | bytes 393224 | tf_op jit(solution)/shard_map/ppermute | solution.py:491
  7.9 0.1 copy.11
  7.9 0.1 pad_maximum_fusion.1
  8.0 2.4 %collective-permute-start.5 = (f32[2,3]{1,0:T(2,128)S(1)}, f32[2,3]{1,0:T(2,128)S(1)}, u32[]{:S(2)}, u32[]{:S(2)}) collective-permute-start(f32[2,3]{1,0:T(2,128)S(1)} %pad_maximum_fusion.1), channel_id=1, source_target_pairs={{0,24},{8,16},{16,8},{24,0},{1,25},{9,17},{17,9},{25,1},{2,26},{10... | collective-permute-start | bytes 80 | tf_op jit(solution)/shard_map/ppermute | solution.py:491
  10.4 1.2 %collective-permute-start.4 = (f32[2,3]{1,0:T(2,128)S(1)}, f32[2,3]{1,0:T(2,128)S(1)}, u32[]{:S(2)}, u32[]{:S(2)}) collective-permute-start(f32[2,3]{1,0:T(2,128)S(1)} %pad_maximum_fusion.1), channel_id=1, source_target_pairs={{0,16},{8,24},{16,0},{24,8},{1,17},{9,25},{17,1},{25,9},{2,18},{10... | collective-permute-start | bytes 80 | tf_op jit(solution)/shard_map/ppermute | solution.py:491
  11.6 0.0 collective-permute-start.3
  11.7 0.1 copy.13.refs_1_.pos_ref
  11.8 3.8 %shard_map.83.refs_3_ = s32[32,128,128]{2,1,0:T(8,128)S(1)} custom-call(s32[4]{0:T(128)} %pad_add_fusion.place_ref.refs_0_, s32[2,192,4096]{2,1,0:T(8,128)} %atoms_hbm.3), custom_call_target="tpu_custom_call" | custom-call | flops 31457280 | bytes 9437184 | tf_op jit(solution)/shard_map/pallas_call | solution.py:136
  15.6 0.0 collective-permute-done.5
  15.6 1.5 %collective-permute-start.2 = (s32[32,2]{1,0:T(8,128)S(1)}, s32[32,2]{1,0:T(8,128)S(1)}, u32[]{:S(2)}, u32[]{:S(2)}) collective-permute-start(s32[32,2]{1,0:T(8,128)S(1)} %copy.13.refs_1_.pos_ref), channel_id=1, source_target_pairs={{0,1},{8,9},{16,23},{24,31},{1,2},{9,10},{17,16},{25,24},{2,3},{10... | collective-permute-start | bytes 776 | tf_op jit(solution)/shard_map/ppermute | solution.py:491
  17.1 0.0 collective-permute-done.4
  17.1 0.0 collective-permute-done.3
  17.1 0.7 %pad_maximum_fusion.refs_0_ = f32[8,3]{1,0:T(8,128)} fusion(f32[2,3]{1,0:T(2,128)S(1)} %collective-permute-done.5, f32[2,3]{1,0:T(2,128)S(1)} %collective-permute-done.4, f32[2,3]{1,0:T(2,128)S(1)} %collective-permute-done.3, f32[2,1]{1,0:T(2,128)S(1)} %copy.11, f32[2,2]{1,0:T(2,128)S(1)} %convert_element_type.3), kind=kLoop, calls=%fused_computation | loop fusion | flops 96 | bytes 192 | tf_op jit(solution)/shard_map/concatenate | solution.py:507
  17.8 1.7 %shard_map.84 = (f32[2,2,384,128]{3,2,1,0:T(8,128)S(1)}, f32[16,128]{1,0:T(8,128)S(1)}) custom-call(f32[8,3]{1,0:T(8,128)} %pad_maximum_fusion.refs_0_, f32[2,4]{1,0:T(2,128)} %refs_1_.1), custom_call_target="tpu_custom_call" | custom-call | flops 100000000 | bytes 1000000 | tf_op jit(solution)/shard_map/pallas_call | solution.py:203
  19.5 2.6 %collective-permute-done.2.refs_2_ = s32[32,2]{1,0:T(8,128)S(1)} collective-permute-done((s32[32,2]{1,0:T(8,128)S(1)}, s32[32,2]{1,0:T(8,128)S(1)}, u32[]{:S(2)}, u32[]{:S(2)}) %collective-permute-start.2) | collective-permute-done | bytes 288 | tf_op jit(solution)/shard_map/ppermute | solution.py:491
  22.1 0.0 collective-permute-done.1.refs_5_
  22.1 0.5 collective-permute-start.7
  22.6 1.4 %collective-permute-done.7.refs_7_ = s16[32,2048]{1,0:T(8,128)(2,1)S(1)} collective-permute-done((s16[32,2048]{1,0:T(8,128)(2,1)}, s16[32,2048]{1,0:T(8,128)(2,1)S(1)}, u32[]{:S(2)}, u32[]{:S(2)}) %collective-permute-start.7) | collective-permute-done | bytes 131104 | tf_op jit(solution)/shard_map/ppermute | solution.py:491
  24.0 0.0 copy-start.1
  24.0 0.9 %copy-done.1 = bf16[256,256]{1,0:T(8,128)(2,1)S(1)} copy-done((bf16[256,256]{1,0:T(8,128)(2,1)S(1)}, bf16[256,256]{1,0:T(8,128)(2,1)}, u32[]{:S(2)}) %copy-start.1) | copy-done | bytes 131096
  24.9 9.8 %shard_map.85 = (bf16[16,64,128]{2,1,0:T(8,128)(2,1)S(1)}, bf16[16,64,128]{2,1,0:T(8,128)(2,1)S(1)}, s32[32,128,128]{2,1,0:T(8,128)S(1)}) custom-call(s32[4]{0:T(128)S(1)} %copy-done.3, s32[32,2]{1,0:T(8,128)S(1)} %copy.13.refs_1_.pos_ref, s32[32,2]{1,0:T(8,128)S(1)} %collective-permute-done.2.refs_2_, ...), custom_call_target="tpu_custom_call", output_to_operand_aliasing={{2}: (3, {})} | custom-call | tf_op jit(solution)/shard_map/pallas_call | solution.py:399
  34.7 4.6 %collective-permute-start.10 = (bf16[16,64,128]{2,1,0:T(8,128)(2,1)S(1)}, bf16[16,64,128]{2,1,0:T(8,128)(2,1)S(1)}, u32[]{:S(2)}, u32[]{:S(2)}) collective-permute-start(bf16[16,64,128]{2,1,0:T(8,128)(2,1)S(1)} %get-tuple-element.34), channel_id=1, source_target_pairs={{0,23},{8,31},{16,1},{24,9},{1,16},{9,24},{17,2},{25,10},{2,17},{1... | collective-permute-start | bytes 786440 | tf_op jit(solution)/shard_map/ppermute | solution.py:491
  39.3 0.0 collective-permute-start.8
  39.3 7.9 %collective-permute-done.10.refs_3_ = bf16[16,64,128]{2,1,0:T(8,128)(2,1)S(1)} collective-permute-done((bf16[16,64,128]{2,1,0:T(8,128)(2,1)S(1)}, bf16[16,64,128]{2,1,0:T(8,128)(2,1)S(1)}, u32[]{:S(2)}, u32[]{:S(2)}) %collective-permute-start.10) | collective-permute-done | bytes 262176 | tf_op jit(solution)/shard_map/ppermute | solution.py:491
  47.2 0.6 collective-permute-start.14
  47.8 1.6 %collective-permute-done.9.refs_2_ = bf16[16,64,128]{2,1,0:T(8,128)(2,1)S(1)} collective-permute-done((bf16[16,64,128]{2,1,0:T(8,128)(2,1)S(1)}, bf16[16,64,128]{2,1,0:T(8,128)(2,1)S(1)}, u32[]{:S(2)}, u32[]{:S(2)}) %collective-permute-start.9) | collective-permute-done | bytes 262176 | tf_op jit(solution)/shard_map/ppermute | solution.py:491
  49.4 2.2 %collective-permute-done.8.refs_1_ = bf16[16,64,128]{2,1,0:T(8,128)(2,1)S(1)} collective-permute-done((bf16[16,64,128]{2,1,0:T(8,128)(2,1)S(1)}, bf16[16,64,128]{2,1,0:T(8,128)(2,1)S(1)}, u32[]{:S(2)}, u32[]{:S(2)}) %collective-permute-start.8) | collective-permute-done | bytes 262176 | tf_op jit(solution)/shard_map/ppermute | solution.py:491
  51.6 1.5 %collective-permute-done.12.refs_5_ = bf16[16,64,128]{2,1,0:T(8,128)(2,1)S(1)} collective-permute-done((bf16[16,64,128]{2,1,0:T(8,128)(2,1)S(1)}, bf16[16,64,128]{2,1,0:T(8,128)(2,1)S(1)}, u32[]{:S(2)}, u32[]{:S(2)}) %collective-permute-start.12) | collective-permute-done | bytes 262176 | tf_op jit(solution)/shard_map/ppermute | solution.py:491
  53.2 3.2 %shard_map.86 = f32[32,16384]{1,0:T(8,128)} custom-call(s32[4]{0:T(128)S(1)} %copy-done.3, s32[32,2]{1,0:T(8,128)S(1)} %copy.13.refs_1_.pos_ref, bf16[16,64,128]{2,1,0:T(8,128)(2,1)S(1)} %get-tuple-element.33.refs_0_, bf16[16,64,128]{2,1,0:T(8,128)(2,1)S(1)} %collective-permute-done.8.refs_1_, bf16[16,64,128]{2,1,0:T(8,128)(2,1)S(1)} %collective-permute-done.9.refs_2_, ...), custom_call_target="tpu_custom_call" | custom-call | tf_op jit(solution)/shard_map/pallas_call | solution.py:458
  (23 shorter events, 0.1 us)
Async XLA Ops:
  0.6 7.2 %copy-start.5 = (s32[2,2]{1,0:T(2,128)S(1)}, s32[2,2]{1,0:T(2,128)}, u32[]{:S(2)}) copy-start(s32[2,2]{1,0:T(2,128)} %param.11) | copy-start | bytes 52
  0.6 7.2 %copy-start.6 = (f32[2]{0:T(128)S(1)}, f32[2]{0:T(128)}, u32[]{:S(2)}) copy-start(f32[2]{0:T(128)} %param.10) | copy-start | bytes 28
  0.6 11.1 %copy-start.4 = (s32[32,2]{0,1:T(2,128)S(1)}, s32[32,2]{0,1:T(2,128)}, u32[]{:S(2)}) copy-start(s32[32,2]{0,1:T(2,128)} %param.12) | copy-start | bytes 772
  3.3 18.8 %collective-permute-start = (s16[64,2048]{1,0:T(8,128)(2,1)}, s16[64,2048]{1,0:T(8,128)(2,1)S(1)}, u32[]{:S(2)}, u32[]{:S(2)}) collective-permute-start(s16[64,2048]{1,0:T(8,128)(2,1)} %get-tuple-element.20), channel_id=1, source_target_pairs={{0,1},{8,9},{16,23},{24,31},{1,2},{9,10},{17,16},{25,24},{2,3},{10... | collective-permute-start | bytes 786440 | tf_op jit(solution)/shard_map/ppermute | solution.py:491
  6.3 15.8 %collective-permute-start.1 = (s16[32,2048]{1,0:T(8,128)(2,1)}, s16[32,2048]{1,0:T(8,128)(2,1)}, u32[]{:S(2)}, u32[]{:S(2)}) collective-permute-start(s16[32,2048]{1,0:T(8,128)(2,1)} %get-tuple-element.21), channel_id=1, source_target_pairs={{0,1},{8,9},{16,23},{24,31},{1,2},{9,10},{17,16},{25,24},{2,3},{10... | collective-permute-start | bytes 393224 | tf_op jit(solution)/shard_map/ppermute | solution.py:491
  8.0 7.5 %collective-permute-start.5 = (f32[2,3]{1,0:T(2,128)S(1)}, f32[2,3]{1,0:T(2,128)S(1)}, u32[]{:S(2)}, u32[]{:S(2)}) collective-permute-start(f32[2,3]{1,0:T(2,128)S(1)} %pad_maximum_fusion.1), channel_id=1, source_target_pairs={{0,24},{8,16},{16,8},{24,0},{1,25},{9,17},{17,9},{25,1},{2,26},{10... | collective-permute-start | bytes 80 | tf_op jit(solution)/shard_map/ppermute | solution.py:491
  10.4 6.7 %collective-permute-start.4 = (f32[2,3]{1,0:T(2,128)S(1)}, f32[2,3]{1,0:T(2,128)S(1)}, u32[]{:S(2)}, u32[]{:S(2)}) collective-permute-start(f32[2,3]{1,0:T(2,128)S(1)} %pad_maximum_fusion.1), channel_id=1, source_target_pairs={{0,16},{8,24},{16,0},{24,8},{1,17},{9,25},{17,1},{25,9},{2,18},{10... | collective-permute-start | bytes 80 | tf_op jit(solution)/shard_map/ppermute | solution.py:491
  11.6 5.5 %collective-permute-start.3 = (f32[2,3]{1,0:T(2,128)S(1)}, f32[2,3]{1,0:T(2,128)S(1)}, u32[]{:S(2)}, u32[]{:S(2)}) collective-permute-start(f32[2,3]{1,0:T(2,128)S(1)} %pad_maximum_fusion.1), channel_id=1, source_target_pairs={{0,8},{8,0},{16,24},{24,16},{1,9},{9,1},{17,25},{25,17},{2,10},{10... | collective-permute-start | bytes 80 | tf_op jit(solution)/shard_map/ppermute | solution.py:491
  11.8 12.2 %copy-start = (bf16[512,256]{1,0:T(8,128)(2,1)S(1)}, bf16[512,256]{1,0:T(8,128)(2,1)}, u32[]{:S(2)}) copy-start(bf16[512,256]{1,0:T(8,128)(2,1)} %constant.56.clone.refs_10_) | copy-start | bytes 786436
  11.8 12.2 %copy-start.2 = (bf16[128,256]{1,0:T(8,128)(2,1)S(1)}, bf16[128,256]{1,0:T(8,128)(2,1)}, u32[]{:S(2)}) copy-start(bf16[128,256]{1,0:T(8,128)(2,1)} %constant.58.clone.refs_12_) | copy-start | bytes 196612
  11.8 12.2 %copy-start.3 = (s32[4]{0:T(128)S(1)}, s32[4]{0:T(128)}, u32[]{:S(2)}) copy-start(s32[4]{0:T(128)} %pad_add_fusion.place_ref.refs_0_) | copy-start | bytes 52
  15.6 6.5 %collective-permute-start.2 = (s32[32,2]{1,0:T(8,128)S(1)}, s32[32,2]{1,0:T(8,128)S(1)}, u32[]{:S(2)}, u32[]{:S(2)}) collective-permute-start(s32[32,2]{1,0:T(8,128)S(1)} %copy.13.refs_1_.pos_ref), channel_id=1, source_target_pairs={{0,1},{8,9},{16,23},{24,31},{1,2},{9,10},{17,16},{25,24},{2,3},{10... | collective-permute-start | bytes 776 | tf_op jit(solution)/shard_map/ppermute | solution.py:491
  22.1 1.9 %collective-permute-start.6 = (s16[64,2048]{1,0:T(8,128)(2,1)S(1)}, s16[64,2048]{1,0:T(8,128)(2,1)S(1)}, u32[]{:S(2)}, u32[]{:S(2)}) collective-permute-start(s16[64,2048]{1,0:T(8,128)(2,1)S(1)} %collective-permute-done.refs_4_), channel_id=1, source_target_pairs={{0,8},{8,0},{16,24},{24,16},{1,9},{9,1},{17,25},{25,17},{2,10},{10... | collective-permute-start | bytes 786440 | tf_op jit(solution)/shard_map/ppermute | solution.py:491
  22.1 1.9 %collective-permute-start.7 = (s16[32,2048]{1,0:T(8,128)(2,1)}, s16[32,2048]{1,0:T(8,128)(2,1)S(1)}, u32[]{:S(2)}, u32[]{:S(2)}) collective-permute-start(s16[32,2048]{1,0:T(8,128)(2,1)} %collective-permute-done.1.refs_5_), channel_id=1, source_target_pairs={{0,8},{8,0},{16,24},{24,16},{1,9},{9,1},{17,25},{25,17},{2,10},{10... | collective-permute-start | bytes 393224 | tf_op jit(solution)/shard_map/ppermute | solution.py:491
  24.0 0.9 %copy-start.1 = (bf16[256,256]{1,0:T(8,128)(2,1)S(1)}, bf16[256,256]{1,0:T(8,128)(2,1)}, u32[]{:S(2)}) copy-start(bf16[256,256]{1,0:T(8,128)(2,1)} %constant.57.clone.refs_11_) | copy-start | bytes 393220
  34.7 12.5 %collective-permute-start.10 = (bf16[16,64,128]{2,1,0:T(8,128)(2,1)S(1)}, bf16[16,64,128]{2,1,0:T(8,128)(2,1)S(1)}, u32[]{:S(2)}, u32[]{:S(2)}) collective-permute-start(bf16[16,64,128]{2,1,0:T(8,128)(2,1)S(1)} %get-tuple-element.34), channel_id=1, source_target_pairs={{0,23},{8,31},{16,1},{24,9},{1,16},{9,24},{17,2},{25,10},{2,17},{1... | collective-permute-start | bytes 786440 | tf_op jit(solution)/shard_map/ppermute | solution.py:491
  39.3 10.1 %collective-permute-start.9 = (bf16[16,64,128]{2,1,0:T(8,128)(2,1)S(1)}, bf16[16,64,128]{2,1,0:T(8,128)(2,1)S(1)}, u32[]{:S(2)}, u32[]{:S(2)}) collective-permute-start(bf16[16,64,128]{2,1,0:T(8,128)(2,1)S(1)} %get-tuple-element.34), channel_id=1, source_target_pairs={{0,7},{8,15},{16,17},{24,25},{1,0},{9,8},{17,18},{25,26},{2,1},{10... | collective-permute-start | bytes 786440 | tf_op jit(solution)/shard_map/ppermute | solution.py:491
  39.3 12.3 %collective-permute-start.8 = (bf16[16,64,128]{2,1,0:T(8,128)(2,1)S(1)}, bf16[16,64,128]{2,1,0:T(8,128)(2,1)S(1)}, u32[]{:S(2)}, u32[]{:S(2)}) collective-permute-start(bf16[16,64,128]{2,1,0:T(8,128)(2,1)S(1)} %get-tuple-element.33.refs_0_), channel_id=1, source_target_pairs={{0,16},{8,24},{16,0},{24,8},{1,17},{9,25},{17,1},{25,9},{2,18},{10... | collective-permute-start | bytes 786440 | tf_op jit(solution)/shard_map/ppermute | solution.py:491
  39.3 12.3 %collective-permute-start.11 = (bf16[16,64,128]{2,1,0:T(8,128)(2,1)S(1)}, bf16[16,64,128]{2,1,0:T(8,128)(2,1)S(1)}, u32[]{:S(2)}, u32[]{:S(2)}) collective-permute-start(bf16[16,64,128]{2,1,0:T(8,128)(2,1)S(1)} %get-tuple-element.33.refs_0_), channel_id=1, source_target_pairs={{0,8},{8,0},{16,24},{24,16},{1,9},{9,1},{17,25},{25,17},{2,10},{10... | collective-permute-start | bytes 786440 | tf_op jit(solution)/shard_map/ppermute | solution.py:491
  47.2 4.4 %collective-permute-start.14 = (bf16[16,64,128]{2,1,0:T(8,128)(2,1)S(1)}, bf16[16,64,128]{2,1,0:T(8,128)(2,1)S(1)}, u32[]{:S(2)}, u32[]{:S(2)}) collective-permute-start(bf16[16,64,128]{2,1,0:T(8,128)(2,1)S(1)} %collective-permute-done.10.refs_3_), channel_id=1, source_target_pairs={{0,8},{8,0},{16,24},{24,16},{1,9},{9,1},{17,25},{25,17},{2,10},{10... | collective-permute-start | bytes 786440 | tf_op jit(solution)/shard_map/ppermute | solution.py:491
  49.4 2.2 %collective-permute-start.13 = (bf16[16,64,128]{2,1,0:T(8,128)(2,1)S(1)}, bf16[16,64,128]{2,1,0:T(8,128)(2,1)S(1)}, u32[]{:S(2)}, u32[]{:S(2)}) collective-permute-start(bf16[16,64,128]{2,1,0:T(8,128)(2,1)S(1)} %collective-permute-done.9.refs_2_), channel_id=1, source_target_pairs={{0,8},{8,0},{16,24},{24,16},{1,9},{9,1},{17,25},{25,17},{2,10},{10... | collective-permute-start | bytes 786440 | tf_op jit(solution)/shard_map/ppermute | solution.py:491
  51.6 1.5 %collective-permute-start.12 = (bf16[16,64,128]{2,1,0:T(8,128)(2,1)S(1)}, bf16[16,64,128]{2,1,0:T(8,128)(2,1)S(1)}, u32[]{:S(2)}, u32[]{:S(2)}) collective-permute-start(bf16[16,64,128]{2,1,0:T(8,128)(2,1)S(1)} %collective-permute-done.8.refs_1_), channel_id=1, source_target_pairs={{0,8},{8,0},{16,24},{24,16},{1,9},{9,1},{17,25},{25,17},{2,10},{10... | collective-permute-start | bytes 786440 | tf_op jit(solution)/shard_map/ppermute | solution.py:491

commit v3 on v2

v3 whole, which is shorter than its diff:
```python
import math

import jax
import jax.numpy as jnp
import ml_dtypes
import numpy as np
from jax import lax
from jax.experimental import pallas as pl
from jax.experimental.pallas import tpu as pltpu
from jax.sharding import PartitionSpec as P

HALFW = 32
TYPES = 4
WIN = 128
LANES = 128
GROUP = 64
PACK = 32
GROUPS = 6
BITS = 4
HALO0 = 64
HALO1 = 32
TABLE = 384
MIB = 1024 * 1024
CORES = 2


def taps(offset):
    steps = np.arange(-HALFW, HALFW + 1, dtype=np.float32)
    weights = 1.0 - 0.5 * (steps / (HALFW + 1.0)) ** 2
    scale = np.sqrt(np.sum(weights * weights))
    offset = offset.astype(np.float32)
    weight = (1.0 - 0.5 * (offset / (HALFW + 1.0)) ** 2) / scale
    chirp = np.float32(math.pi) * offset * offset / np.float32(2.0 * HALFW + 1.0)
    inside = np.abs(offset) <= HALFW
    real = np.where(inside, np.cos(chirp) * weight, 0.0)
    imag = np.where(inside, np.sin(chirp) * weight, 0.0)
    return real.astype(np.float32), imag.astype(np.float32)


def x_matrix(sources, targets):
    rows = []
    for start in range(0, len(sources), LANES):
        src = sources[start : start + LANES]
        real, imag = taps(targets[None, :] - src[:, None] + HALFW)
        rows.append(np.concatenate([real, imag], axis=1))
        rows.append(np.concatenate([-imag, real], axis=1))
    return np.concatenate(rows, axis=0).astype(ml_dtypes.bfloat16)


def y_matrix():
    out = np.arange(GROUP)[:, None]
    src = np.arange(2 * GROUP)[None, :]
    real, imag = taps(out - src + HALFW)
    upper = np.concatenate([real, -imag], axis=1)
    lower = np.concatenate([imag, real], axis=1)
    return np.concatenate([upper, lower], axis=0).astype(ml_dtypes.bfloat16)


def matrices():
    first = x_matrix(np.arange(2 * LANES), np.arange(LANES))
    second = x_matrix(np.arange(LANES, 2 * LANES), np.arange(LANES, 2 * LANES))
    second = second.reshape(2 * LANES, 2, LANES)
    second[:, :, LANES // 2 :] = 0
    return first, second.reshape(2 * LANES, 2 * LANES), y_matrix()


def pack_kernel(atoms_hbm, pos_ref, out_ref, zero_buf, one_buf, pos_buf, sems):
    half = zero_buf.shape[1]
    rows = atoms_hbm.shape[1]
    beam = lax.axis_index("beam")
    side, core = beam // CORES, beam % CORES
    parts = sems.shape[0] // 2
    step = half // parts
    copies = []
    for layer, buf in ((0, zero_buf), (1, one_buf)):
        depth = buf.shape[0]
        top = pl.multiple_of((1 - side) * (rows - depth), depth)
        for part in range(parts):
            left = pl.multiple_of(core * half + part * step, LANES)
            copies.append(
                pltpu.make_async_copy(
                    atoms_hbm.at[layer, pl.ds(top, depth), pl.ds(left, step)],
                    buf.at[:, pl.ds(part * step, step)],
                    sems.at[parts * layer + part],
                )
            )
    for copy in copies:
        copy.start()
    pos_buf[...] = jnp.zeros(pos_buf.shape, jnp.int32)
    pos_buf[:2, : pos_ref.shape[1]] = pos_ref[...]
    out_ref[:16, half:] = pos_buf[...].astype(jnp.int16)
    for layer, (buf, first) in enumerate(((zero_buf, 0), (one_buf, HALO0))):
        for part in range(parts):
            copies[parts * layer + part].wait()
            cols = slice(part * step, (part + 1) * step)
            out_ref[first : first + buf.shape[0], cols] = buf[:, cols].astype(jnp.int16)


def pack_rows(atoms, positions):
    half = atoms.shape[2] // CORES
    vmem = pl.BlockSpec(memory_space=pltpu.VMEM)
    return pl.pallas_call(
        pack_kernel,
        out_shape=pltpu.VMEM((HALO0 + HALO1, half + LANES), jnp.int16),
        in_specs=[pl.BlockSpec(memory_space=pltpu.HBM), vmem],
        out_specs=vmem,
        scratch_shapes=[
            pltpu.VMEM((HALO0, half), jnp.int32),
            pltpu.VMEM((HALO1, half), jnp.int32),
            pltpu.VMEM((16, LANES), jnp.int32),
            pltpu.SemaphoreType.DMA((4,)),
        ],
        compiler_params=pltpu.CompilerParams(vmem_limit_bytes=60 * MIB),
    )(atoms, positions)


def words_kernel(place_ref, atoms_hbm, out_ref, buf, sems):
    upper = place_ref[0] == 1
    parts = sems.shape[0]
    step = buf.shape[2] // parts
    copies = [
        pltpu.make_async_copy(
            atoms_hbm.at[:, :, pl.ds(k * step, step)], buf.at[:, :, pl.ds(k * step, step)], sems.at[k]
        )
        for k in range(parts)
    ]
    for copy in copies:
        copy.start()
    depth = out_ref.shape[1]
    for k in range(parts):
        copies[k].wait()
        for tile in range(k * step // LANES, (k + 1) * step // LANES):
            at = slice(tile * LANES, (tile + 1) * LANES)
            code = buf[0, :, at] + TYPES * buf[1, :, at]
            blocks = [code[n * PACK : (n + 1) * PACK] for n in range(buf.shape[1] // PACK)]
            halo = HALO0 // PACK
            for w in range(depth // PACK):
                words = []
                for first in (halo, 0):
                    word = None
                    for g in range(GROUPS):
                        block = w + g - first
                        if 0 <= block < len(blocks):
                            term = blocks[block] << (BITS * g)
                            word = term if word is None else word | term
                    words.append(word)
                out_ref[tile, w * PACK : (w + 1) * PACK, :] = jnp.where(upper, words[1], words[0])


def own_words(place, atoms):
    width = atoms.shape[2]
    return pl.pallas_call(
        words_kernel,
        out_shape=pltpu.VMEM((width // LANES, GROUP + PACK, LANES), jnp.int32),
        in_specs=[pl.BlockSpec(memory_space=pltpu.SMEM), pl.BlockSpec(memory_space=pltpu.HBM)],
        out_specs=pl.BlockSpec(memory_space=pltpu.VMEM),
        scratch_shapes=[pltpu.VMEM(atoms.shape, jnp.int32), pltpu.SemaphoreType.DMA((8,))],
        compiler_params=pltpu.CompilerParams(vmem_limit_bytes=60 * MIB),
        cost_estimate=pl.CostEstimate(flops=20 * atoms.size, bytes_accessed=6 * atoms.size, transcendentals=0),
    )(place, atoms)


def cos_turns(turns):
    angle = (2.0 * math.pi) * (0.25 - jnp.abs(turns - jnp.round(turns)))
    square = angle * angle
    total = jnp.full_like(square, 1.0)
    for k in (12, 10, 8, 6, 4, 2):
        total = 1.0 - square * total * (1.0 / (k * (k + 1)))
    return angle * total


def probe_kernel(rows_total, width, beam_ref, phase_ref, *refs):
    matrices_hbm, (out_ref, values_ref), matrices_ref, sems = refs[:3], refs[3:5], refs[5:8], refs[8]
    copies = [pltpu.make_async_copy(a, b, sems.at[n]) for n, (a, b) in enumerate(zip(matrices_hbm, matrices_ref))]
    for copy in copies:
        copy.start()
    beams = beam_ref.shape[0]
    precise = lax.Precision.HIGHEST
    lane = lax.broadcasted_iota(jnp.int32, (1, LANES), 1)
    tilt_y = jnp.zeros((1, LANES), jnp.float32)
    for beam in range(beams):
        tilt_y = jnp.where(lane % beams == beam, beam_ref[beam, 1], tilt_y)
    quarter = jnp.where(lane < beams, 0.0, 0.25)
    row = lax.broadcasted_iota(jnp.int32, (TABLE, LANES), 0) - TABLE // 2
    along_y = cos_turns(row.astype(jnp.float32) * tilt_y / rows_total - quarter)
    along_y = jnp.where(lane < 2 * beams, along_y, 0.0)

    sub = lax.broadcasted_iota(jnp.int32, (2 * beams, 1), 0)
    tilt_x = jnp.zeros((2 * beams, 1), jnp.float32)
    weight = jnp.zeros((2 * beams, 1), jnp.float32)
    for beam in range(beams):
        tilt_x = jnp.where(sub % beams == beam, beam_ref[beam, 0], tilt_x)
        weight = jnp.where(sub % beams == beam, beam_ref[beam, 2], weight)
    col = lax.broadcasted_iota(jnp.int32, (2 * beams, 2 * LANES), 1) - LANES
    turns = col.astype(jnp.float32) * tilt_x / width
    shift = jnp.where(sub < beams, 0.0, 0.25)
    right_re = weight * cos_turns(turns + shift)
    right_im = weight * cos_turns(turns + shift - 0.25)
    right = jnp.concatenate([right_re, right_im], axis=1)
    right = jnp.concatenate([right, jnp.zeros((LANES - 2 * beams, 4 * LANES), jnp.float32)], axis=0)
    table = jnp.dot(along_y, right, precision=precise, preferred_element_type=jnp.float32)
    for part in range(2):
        for tile in range(2):
            lo = (2 * part + tile) * LANES
            out_ref[part, tile] = table[:, lo : lo + LANES]

    sub = lax.broadcasted_iota(jnp.int32, (4 * TYPES, LANES), 0)
    angle = jnp.zeros((4 * TYPES, LANES), jnp.float32)
    for layer in range(2):
        for kind in range(TYPES):
            mine = (sub // (2 * TYPES) == layer) & (sub % TYPES == kind)
            angle = jnp.where(mine, phase_ref[layer, kind], angle)
    quarter = jnp.where((sub // TYPES) % 2 == 0, 0.0, 0.25)
    values_ref[...] = cos_turns(angle * (0.5 / math.pi) - quarter)
    for copy in copies:
        copy.wait()


def probe_table(beam_rows, phases, rows_total, width):
    bands = matrices()

    def kernel(*refs):
        probe_kernel(rows_total, width, *refs)

    smem = pl.BlockSpec(memory_space=pltpu.SMEM)
    vmem = pl.BlockSpec(memory_space=pltpu.VMEM)
    return pl.pallas_call(
        kernel,
        out_shape=[pltpu.VMEM((2, 2, TABLE, LANES), jnp.float32), pltpu.VMEM((4 * TYPES, LANES), jnp.float32)]
        + [pltpu.VMEM(matrix.shape, jnp.bfloat16) for matrix in bands],
        in_specs=[smem, smem] + [pl.BlockSpec(memory_space=pltpu.HBM)] * 3,
        out_specs=[vmem] * 5,
        scratch_shapes=[pltpu.SemaphoreType.DMA((3,))],
        compiler_params=pltpu.CompilerParams(vmem_limit_bytes=60 * MIB),
        cost_estimate=pl.CostEstimate(flops=10**8, bytes_accessed=10**6, transcendentals=10**5),
    )(beam_rows, phases, *bands)


def merge_rows(side, core, halo_refs, words_in, words):
    half_tiles = words.shape[0] // CORES

    depth = words.shape[1]

    def merge(upper):
        top = PACK * GROUPS + GROUP - HALO0 if upper else 0
        lo = 0 if upper else HALO0 - HALO1
        for source, at in zip(halo_refs, (core, 1 - core)):
            for tile in range(half_tiles):
                cols = slice(tile * LANES, (tile + 1) * LANES)
                zero = source[:HALO0, cols].astype(jnp.int32)
                one = source[HALO0:, cols].astype(jnp.int32) * TYPES
                blocks = [zero[:PACK], zero[PACK:]]
                blocks[lo // PACK] = blocks[lo // PACK] + one
                index = at * half_tiles + tile
                for w in range(depth // PACK):
                    word = None
                    for g in range(GROUPS):
                        block = w + g - top // PACK
                        if 0 <= block < 2:
                            term = blocks[block] << (BITS * g)
                            word = term if word is None else word | term
                    if word is not None:
                        rows = slice(w * PACK, (w + 1) * PACK)
                        words[index, rows, :] = words_in[index, rows, :] | word

    @pl.when(side == 0)
    def _():
        merge(False)

    @pl.when(side == 1)
    def _():
        merge(True)


def run_tasks(beams, batch_size, side, total, words, table_ref, values_ref, first_ref, second_ref, ymat_ref, result, scratch):
    left, crossed, right, codes_new, codes_old, row_list, col_list, slot_list = scratch
    tiles = words.shape[0]
    f32, bf16, i16 = jnp.float32, jnp.bfloat16, jnp.int16

    def values(layer):
        rows = [values_ref[2 * TYPES * layer + k : 2 * TYPES * layer + k + 1, :].astype(bf16) for k in range(2 * TYPES)]
        return rows[:TYPES], rows[TYPES:]

    cos0, sin0 = values(0)
    cos1, sin1 = values(1)
    lane = lax.broadcasted_iota(jnp.int32, (1, LANES), 1)

    def transmission(code, bit, cos_v, sin_v):
        b0 = (code & i16(1 << bit)) != 0
        b1 = (code & i16(2 << bit if bit < 14 else -(1 << 15))) != 0
        out = []
        for v in (cos_v, sin_v):
            spread = [jnp.broadcast_to(value, code.shape) for value in v]
            out.append(jnp.where(b1, jnp.where(b0, spread[3], spread[2]), jnp.where(b0, spread[1], spread[0])))
        return out

    def split(word):
        return word.astype(i16), (word >> 16).astype(i16)

    def tile_cols(j, part):
        return slice((2 * j + part) * LANES, (2 * j + part + 1) * LANES)

    def waves(batch):
        for k in range(batch_size):
            at = jnp.minimum(batch_size * batch + k, total - 1)
            row, col = row_list[at], col_list[at]
            start = jnp.clip(row - GROUP, 0, GROUP)
            delta = start - GROUP * (1 - side) - row + TABLE // 2
            tile0 = col // LANES + tiles - 1
            shift = lax.rem(col, LANES)
            back = lax.rem(LANES - shift, LANES)
            rolled = []
            for j in range(3):
                word = words[lax.rem(tile0 + j, tiles), pl.ds(start, PACK), :]
                rolled.append(pltpu.roll(word, back, 1))
            keep = lane < LANES - shift
            window = [jnp.where(keep, rolled[j], rolled[j + 1]) for j in range(2)]
            turned = [pltpu.roll(w, LANES - HALFW, 1) for w in window]
            inner = [jnp.where(lane < LANES - HALFW, turned[0], turned[1]), turned[1]]
            for j in range(2):
                codes_new[k, j, 0], codes_new[k, j, 1] = split(inner[j])
                codes = split(window[j])
                for g in range(GROUPS):
                    t_re, t_im = transmission(codes[g // 4], BITS * (g % 4), cos0, sin0)
                    p_re = table_ref[0, j, pl.ds(delta + g * PACK, PACK), :].astype(bf16)
                    p_im = table_ref[1, j, pl.ds(delta + g * PACK, PACK), :].astype(bf16)
                    rows = slice(k * 3 * GROUP + g * PACK, k * 3 * GROUP + (g + 1) * PACK)
                    left[rows, tile_cols(j, 0)] = p_re * t_re - p_im * t_im
                    left[rows, tile_cols(j, 1)] = p_re * t_im + p_im * t_re
        for k in range(batch_size):
            rows = slice(k * 3 * GROUP, (k + 1) * 3 * GROUP)
            one = jnp.dot(left[rows, :], first_ref[...], preferred_element_type=f32).astype(bf16)
            two = jnp.dot(left[rows, 2 * LANES :], second_ref[...], preferred_element_type=f32).astype(bf16)
            for part in range(2):
                cols = slice(part * LANES, (part + 1) * LANES)
                crossed[k, part, :, :LANES] = one[:, cols]
                crossed[k, part, :, LANES:] = two[:, cols]

    def stack(k, b):
        rows = slice(b * GROUP, b * GROUP + 2 * GROUP)
        return jnp.concatenate([crossed[k, part, rows] for part in range(2)], axis=0)

    def rest(batch):
        for k in range(batch_size):
            for b in range(2):
                down = jnp.dot(ymat_ref[...], stack(k, b), preferred_element_type=f32)
                for j in range(2):
                    cols = slice(j * LANES, (j + 1) * LANES)
                    for part in range(2):
                        group = 2 * b + part + 1
                        t_re, t_im = transmission(codes_old[k, j, group // 4], BITS * (group % 4) + 2, cos1, sin1)
                        d_re = down[part * PACK : (part + 1) * PACK, cols].astype(bf16)
                        d_im = down[GROUP + part * PACK : GROUP + (part + 1) * PACK, cols].astype(bf16)
                        top = (2 * k + b) * GROUP + part * PACK
                        right[top : top + PACK, tile_cols(j, 0)] = d_re * t_re - d_im * t_im
                        right[top : top + PACK, tile_cols(j, 1)] = d_re * t_im + d_im * t_re
        one = jnp.dot(right[...], first_ref[...], preferred_element_type=f32).astype(bf16)
        stacks = []
        for k in range(batch_size):
            rows = slice(2 * k * GROUP, (2 * k + 2) * GROUP)
            stacks.append(jnp.concatenate([one[rows, :LANES], one[rows, LANES:]], axis=0))
        exit_waves = jnp.dot(ymat_ref[...], jnp.concatenate(stacks, axis=1), preferred_element_type=f32)
        exit_waves = exit_waves.astype(bf16).astype(f32)
        for k in range(batch_size):
            cols = slice(k * LANES, (k + 1) * LANES)
            re, im = exit_waves[:GROUP, cols], exit_waves[GROUP:, cols]
            slot = slot_list[jnp.minimum(batch_size * batch + k, total - 1)]
            result[slot] = ((re * re + im * im) * (1.0 / beams)).astype(bf16)

    def step(batch, carry):
        rest(batch - 1)
        waves(batch)
        codes_old[...] = codes_new[...]
        return carry

    batches = (total + batch_size - 1) // batch_size
    waves(0)
    codes_old[...] = codes_new[...]
    lax.fori_loop(1, batches, step, 0)
    rest(batches - 1)


def ext_kernel(beams, batch_size, place_ref, near_ref, words_in, mine_ref, other_ref, *refs):
    constants, (out_ref, words), scratch = refs[:5], refs[5:7], refs[7:]
    row_list, col_list, slot_list = scratch[5:]
    side, core, near_base = place_ref[0], place_ref[1], place_ref[3]
    merge_rows(side, core, (mine_ref, other_ref), words_in, words)

    def add(k, found):
        probe = CORES * k + core
        row = near_ref[0, probe] - near_base
        reaches = jnp.where(side == 0, row > -GROUP, row < 4 * GROUP)
        row_list[found] = row
        col_list[found] = near_ref[1, probe]
        slot_list[found] = k
        return found + reaches.astype(jnp.int32)

    total = lax.fori_loop(0, out_ref.shape[0], add, 0)

    @pl.when(total > 0)
    def _():
        run_tasks(beams, batch_size, side, total, words, *constants, out_ref, scratch)


def own_kernel(beams, batch_size, place_ref, pos_ref, words, *refs):
    constants, out_ref, scratch = refs[:5], refs[5], refs[6:]
    row_list, col_list, slot_list = scratch[5:]
    side, core, row_base = place_ref[0], place_ref[1], place_ref[2]
    count = out_ref.shape[0]

    def add(k, carry):
        probe = CORES * k + core
        row_list[k] = pos_ref[0, probe] - row_base
        col_list[k] = pos_ref[1, probe]
        slot_list[k] = k
        return carry

    lax.fori_loop(0, count, add, 0)
    run_tasks(beams, batch_size, side, count, words, *constants, out_ref, scratch)


def propagate(beams, place, probes, words, halo, constants):
    count = probes.shape[1] // CORES
    smem = pl.BlockSpec(memory_space=pltpu.SMEM)
    vmem = pl.BlockSpec(memory_space=pltpu.VMEM)
    ext = bool(halo)
    body = ext_kernel if ext else own_kernel
    batch_size = 4 if ext else count

    def kernel(*refs):
        body(beams, batch_size, *refs)

    shape = jax.ShapeDtypeStruct((count, GROUP, WIN), jnp.bfloat16)
    return pl.pallas_call(
        kernel,
        out_shape=[shape, pltpu.VMEM(words.shape, jnp.int32)] if ext else shape,
        in_specs=[smem] * 2 + [vmem] * (8 if ext else 6),
        out_specs=[vmem, vmem] if ext else vmem,
        input_output_aliases={2: 1} if ext else {},
        scratch_shapes=[
            pltpu.VMEM((batch_size * 3 * GROUP, 4 * LANES), jnp.bfloat16),
            pltpu.VMEM((batch_size, 2, 3 * GROUP, 2 * LANES), jnp.bfloat16),
            pltpu.VMEM((batch_size * 2 * GROUP, 4 * LANES), jnp.bfloat16),
            pltpu.VMEM((batch_size, 2, 2, PACK, LANES), jnp.int16),
            pltpu.VMEM((batch_size, 2, 2, PACK, LANES), jnp.int16),
            pltpu.SMEM((count + 1,), jnp.int32),
            pltpu.SMEM((count + 1,), jnp.int32),
            pltpu.SMEM((count + 1,), jnp.int32),
        ],
        compiler_params=pltpu.CompilerParams(vmem_limit_bytes=40 * MIB),
        cost_estimate=pl.CostEstimate(flops=4 * 10**9, bytes_accessed=4 * 10**6, transcendentals=0),
    )(place, probes, words, *halo, *constants)


PAD = 3 * WIN


def gather_kernel(place_ref, pos_ref, *refs):
    out_hbm, window, out_buf, sems = refs[8:]
    side, core, row_base = place_ref[0], place_ref[1], place_ref[2]

    def copy(group):
        rows = pl.ds(pl.multiple_of(8 * group, 8), 8)
        return pltpu.make_async_copy(out_buf.at[rows], out_hbm.at[rows], sems.at[group])

    def step(group, carry):
        for par in range(2):
            parity = core if par == 0 else 1 - core
            for i in range(4):
                k = 4 * group + i
                row = pos_ref[0, 2 * k + parity] - row_base
                start = jnp.where(row < GROUP, row, jnp.where(row > 2 * GROUP, row - GROUP, GROUP))
                base = (2 * i + parity) * PAD + WIN - start
                places = (GROUP + GROUP * side, 2 * GROUP - GROUP * side, 3 * GROUP * (1 - side), 3 * GROUP * side)
                for piece, at in zip(refs[4 * par : 4 * par + 4], places):
                    window[pl.ds(base + at, GROUP), :] = piece[k].astype(jnp.float32)
        rows = pl.ds(pl.multiple_of(8 * group, 8), 8)
        for u in range(WIN):
            out_buf[rows, u * WIN : (u + 1) * WIN] = window[pl.ds(WIN + u, 8, stride=PAD), :]
        copy(group).start()
        return carry

    groups = out_buf.shape[0] // 8
    lax.fori_loop(0, groups, step, 0)
    for group in range(groups):
        copy(group).wait()


def put_together(place, positions, pieces):
    probes = positions.shape[1]
    smem = pl.BlockSpec(memory_space=pltpu.SMEM)
    vmem = pl.BlockSpec(memory_space=pltpu.VMEM)
    return pl.pallas_call(
        gather_kernel,
        out_shape=jax.ShapeDtypeStruct((probes, WIN * WIN), jnp.float32),
        in_specs=[smem, smem] + [vmem] * 8,
        out_specs=pl.BlockSpec(memory_space=pltpu.HBM),
        scratch_shapes=[
            pltpu.VMEM((8 * PAD, LANES), jnp.float32),
            pltpu.VMEM((probes, WIN * WIN), jnp.float32),
            pltpu.SemaphoreType.DMA((probes // 8,)),
        ],
        compiler_params=pltpu.CompilerParams(vmem_limit_bytes=16 * MIB),
    )(place, positions, *pieces)


def local(atoms, phases, aperture, tilts, positions):
    rows_here, width = atoms.shape[1], atoms.shape[2]
    probes = positions.shape[0]
    positions = positions.T
    strip, beam = lax.axis_index("strip"), lax.axis_index("beam")
    strips, ways = lax.axis_size("strip"), lax.axis_size("beam")
    rows_total = rows_here * strips
    beams = tilts.shape[0] * ways
    cores = CORES
    side, core = beam // cores, beam % cores
    near_strip = jnp.where(side == 0, strip - 1 + strips, strip + 1) % strips
    near_base = near_strip * rows_here + jnp.where(side == 0, rows_here, -rows_here)
    place = jnp.stack([side, core, strip * rows_here, near_base]).astype(jnp.int32)

    def across(array, dest):
        pairs = []
        for s in range(strips):
            for b in range(ways):
                to_s, to_b = dest(s, b // cores, b % cores)
                pairs.append((b * strips + s, (to_b[0] * cores + to_b[1]) * strips + to_s % strips))
        return lax.ppermute(array, ("beam", "strip"), pairs)

    def swap_cores(array):
        return across(array, lambda s, y, c: (s, (y, 1 - c)))

    packed = pack_rows(atoms, positions)
    mine = across(packed, lambda s, y, c: (s + 1 - 2 * y, (y, c)))
    packed, tilts, aperture = lax.optimization_barrier((packed, tilts, aperture))
    beam_rows = jnp.concatenate([tilts.astype(jnp.float32), aperture[:, None]], axis=1)
    beam_rows = [
        beam_rows,
        swap_cores(beam_rows),
        across(beam_rows, lambda s, y, c: (s, (1 - y, c))),
        across(beam_rows, lambda s, y, c: (s, (1 - y, 1 - c))),
    ]
    beam_rows = jnp.concatenate(beam_rows, axis=0)
    words = own_words(place, atoms)
    table = probe_table(beam_rows, phases, rows_total, width)
    mine, words, table = lax.optimization_barrier((mine, words, table))
    near = mine[:2, width // cores : width // cores + probes].astype(jnp.int32)
    ext, words = propagate(beams, place, near, words, [mine, swap_cores(mine)], table)
    far = across(ext, lambda s, y, c: (s - 1 + 2 * y, (1 - y, c)))
    own = propagate(beams, place, positions, words, [], table)
    own, far, ext = lax.optimization_barrier((own, far, ext))
    facing = across(own, lambda s, y, c: (s, (1 - y, c)))
    same = across(ext, lambda s, y, c: (s - 1 + 2 * y, (y, c)))
    pieces = [own, facing, same, far]
    return put_together(place, positions, pieces + [swap_cores(piece) for piece in pieces])


def solution(mesh):
    in_specs = (P(None, "strip", None), P(), P("beam"), P("beam", None), P("strip", None))
    out_specs = P("strip", None)
    return jax.shard_map(local, mesh=mesh, in_specs=in_specs, out_specs=out_specs, check_vma=False)
```

time: 56.7 us -> 49.5 us (0.87)
  waiting for transfers between devices: 17.3 us -> 13.7 us
  Pallas kernels: 21.1 us -> 19.5 us
  starting transfers between devices: 15.4 us -> 14.2 us
  local copies, waits for them, and re-layouts: 1.1 us -> 0.11 us
    ppermute x15 -> x12, waiting for transfers between devices: 17.3 us -> 13.7 us  [across(): return lax.ppermute(array, ('beam', 'strip'), pairs)]
    pallas_call x3 -> x4, Pallas kernels: 16.2 us -> 14.8 us  [the longest x2 9.16 us: propagate(): pl.pallas_call(kernel, out_shape=[shape, pltpu.VMEM(words.shape, jnp.int3...]
    ppermute x15 -> x12, starting transfers between devices: 15.4 us -> 14.2 us  [across(): return lax.ppermute(array, ('beam', 'strip'), pairs)]
    unnamed x14 -> x8, local copies, waits for them, and re-layouts: 0.92 us -> 0.01 us
  transfers between devices with their start and end apart: 15 -> 12, of which waited for: 6 -> 6; matrix products, arithmetic and copies ran while one was open for 2% -> 3% of each run, Pallas kernels for 10% -> 22%
where the time goes in v3:
time: 49.5 us; the launch traced here: 49 us
  Pallas kernels  19.5 us (39%)
  starting transfers between devices  14.2 us (29%)
  waiting for transfers between devices  13.7 us (28%)
  other arithmetic  1.34 us (3%)
    ppermute x12, starting transfers between devices, across(): return lax.ppermute(array, ('beam', 'strip'), pairs)  14.2 us
    ppermute x12, waiting for transfers between devices, across(): return lax.ppermute(array, ('beam', 'strip'), pairs)  13.7 us
    pallas_call x2, Pallas kernels, propagate(): pl.pallas_call(kernel, out_shape=[shape, pltpu.VMEM(words.shape, jnp.int3...  9.16 us
    pallas_call x1, Pallas kernels, own_words(): pl.pallas_call(words_kernel, out_shape=pltpu.VMEM((width // LANES, GROUP...  3.81 us
    pallas_call x1, Pallas kernels, put_together(): pl.pallas_call(gather_kernel, out_shape=jax.ShapeDtypeStruct((probes, WIN...  2.93 us
    pallas_call x1, Pallas kernels, pack_rows(): pl.pallas_call(pack_kernel, out_shape=pltpu.VMEM((HALO0 + HALO1, half + L...  1.86 us
    pallas_call x1, Pallas kernels, probe_table(): pl.pallas_call(kernel, out_shape=[pltpu.VMEM((2, 2, TABLE, LANES), jnp.fl...  1.77 us
  transfers between devices with their start and end apart: 12, of which 6 were waited for; matrix products, arithmetic and copies ran while one was open for 3% of the time, Pallas kernels for 22%

profile of v3, /device:TPU:0, one launch (start us, length us, event | category | flops | bytes accessed | tf_op | source)
XLA Modules:
  0.0 49.0 jit_solution(7459504197282087450)
XLA Ops:
  0.0 1.9 %shard_map.82 = s16[96,2176]{1,0:T(8,128)(2,1)S(1)} custom-call(s32[2,192,4096]{2,1,0:T(8,128)} %atoms_hbm.3, s32[2,32]{1,0:T(2,128)} %bitcast.6), custom_call_target="tpu_custom_call" | custom-call | tf_op jit(solution)/shard_map/pallas_call | solution.py:102
  1.9 3.0 %collective-permute-start = (s16[96,2176]{1,0:T(8,128)(2,1)S(1)}, s16[96,2176]{1,0:T(8,128)(2,1)S(1)}, u32[]{:S(2)}, u32[]{:S(2)}) collective-permute-start(s16[96,2176]{1,0:T(8,128)(2,1)S(1)} %shard_map.82), channel_id=1, source_target_pairs={{0,1},{8,9},{16,23},{24,31},{1,2},{9,10},{17,16},{25,24},{2,3},{10... | collective-permute-start | bytes 1253384 | tf_op jit(solution)/shard_map/ppermute | solution.py:527
  4.9 0.1 copy.10
  5.0 0.1 pad_maximum_fusion.1
  5.0 3.7 %collective-permute-start.3 = (f32[2,3]{1,0:T(2,128)S(1)}, f32[2,3]{1,0:T(2,128)S(1)}, u32[]{:S(2)}, u32[]{:S(2)}) collective-permute-start(f32[2,3]{1,0:T(2,128)S(1)} %pad_maximum_fusion.1), channel_id=1, source_target_pairs={{0,24},{8,16},{16,8},{24,0},{1,25},{9,17},{17,9},{25,1},{2,26},{10... | collective-permute-start | bytes 80 | tf_op jit(solution)/shard_map/ppermute | solution.py:527
  8.8 0.9 %collective-permute-start.2 = (f32[2,3]{1,0:T(2,128)S(1)}, f32[2,3]{1,0:T(2,128)S(1)}, u32[]{:S(2)}, u32[]{:S(2)}) collective-permute-start(f32[2,3]{1,0:T(2,128)S(1)} %pad_maximum_fusion.1), channel_id=1, source_target_pairs={{0,16},{8,24},{16,0},{24,8},{1,17},{9,25},{17,1},{25,9},{2,18},{10... | collective-permute-start | bytes 80 | tf_op jit(solution)/shard_map/ppermute | solution.py:527
  9.7 0.0 collective-permute-start.1
  9.7 0.6 %pad_add_fusion.place_ref.refs_0_ = s32[4]{0:T(128)} fusion(s32[1]{0:T(128)} %bitcast.3, s32[1]{0:T(128)} %bitcast.2, s32[1]{0:T(128)} %bitcast.1, s32[1]{0:T(128)} %bitcast), kind=kLoop, calls=%fused_computation.2 | loop fusion | flops 12 | bytes 32 | tf_op jit(solution)/shard_map/stack | solution.py:519
  10.3 3.8 %shard_map.83.refs_2_ = s32[32,96,128]{2,1,0:T(8,128)S(1)} custom-call(s32[4]{0:T(128)} %pad_add_fusion.place_ref.refs_0_, s32[2,192,4096]{2,1,0:T(8,128)} %atoms_hbm.3), custom_call_target="tpu_custom_call" | custom-call | flops 31457280 | bytes 9437184 | tf_op jit(solution)/shard_map/pallas_call | solution.py:152
  14.1 0.0 collective-permute-done.3
  14.1 0.0 collective-permute-done.2
  14.1 0.0 collective-permute-done.1
  14.2 0.7 %pad_maximum_fusion.refs_0_ = f32[8,3]{1,0:T(8,128)} fusion(f32[2,3]{1,0:T(2,128)S(1)} %collective-permute-done.3, f32[2,3]{1,0:T(2,128)S(1)} %collective-permute-done.2, f32[2,3]{1,0:T(2,128)S(1)} %collective-permute-done.1, f32[2,1]{1,0:T(2,128)S(1)} %copy.10, f32[2,2]{1,0:T(2,128)S(1)} %convert_element_type.6), kind=kLoop, calls=%fused_computation | loop fusion | flops 96 | bytes 192 | tf_op jit(solution)/shard_map/concatenate | solution.py:542
  14.8 1.8 %shard_map.84 = (f32[2,2,384,128]{3,2,1,0:T(8,128)S(1)}, f32[16,128]{1,0:T(8,128)S(1)}, bf16[512,256]{1,0:T(8,128)(2,1)S(1)}, bf16[256,256]{1,0:T(8,128)(2,1)S(1)}, bf16[128,256]{1,0:T(8,128)(2,1)S(1)}) custom-call(f32[8,3]{1,0:T(8,128)} %pad_maximum_fusion.refs_0_, f32[2,4]{1,0:T(2,128)} %refs_1_.1, bf16[512,256]{1,0:T(8,128)(2,1)} %constant.56.clone.refs_2_, ...), custom_call_target="tpu_custom_call" | custom-call | flops 100000000 | bytes 1000000 | tf_op jit(solution)/shard_map/pallas_call | solution.py:227
  16.6 0.9 %collective-permute-done.refs_3_ = s16[96,2176]{1,0:T(8,128)(2,1)S(1)} collective-permute-done((s16[96,2176]{1,0:T(8,128)(2,1)S(1)}, s16[96,2176]{1,0:T(8,128)(2,1)S(1)}, u32[]{:S(2)}, u32[]{:S(2)}) %collective-permute-start) | collective-permute-done | bytes 417824 | tf_op jit(solution)/shard_map/ppermute | solution.py:527
  17.5 0.0 collective-permute-start.4
  17.6 1.7 %collective-permute-done.4.refs_4_ = s16[96,2176]{1,0:T(8,128)(2,1)S(1)} collective-permute-done((s16[96,2176]{1,0:T(8,128)(2,1)S(1)}, s16[96,2176]{1,0:T(8,128)(2,1)S(1)}, u32[]{:S(2)}, u32[]{:S(2)}) %collective-permute-start.4) | collective-permute-done | bytes 417824 | tf_op jit(solution)/shard_map/ppermute | solution.py:527
  19.3 4.0 %shard_map.85 = (bf16[16,64,128]{2,1,0:T(8,128)(2,1)S(1)}, s32[32,96,128]{2,1,0:T(8,128)S(1)}) custom-call(s32[4]{0:T(128)S(1)} %copy-done, s32[2,32]{1,0:T(2,128)S(1)} %slice_convert_fusion.refs_1_, s32[32,96,128]{2,1,0:T(8,128)S(1)} %shard_map.83.refs_2_, s16[96,2176]{1,0:T(8,128)(2,1)S(1)} %collective-permute-done.refs_3_, ...), custom_call_target="tpu_custom_call", output_to_operand_aliasing={{1}: (2, {})} | custom-call | flops 4000000000 | bytes 4000000 | tf_op jit(solution)/shard_map/pallas_call | solution.py:434
  23.3 5.5 %collective-permute-start.5 = (bf16[16,64,128]{2,1,0:T(8,128)(2,1)S(1)}, bf16[16,64,128]{2,1,0:T(8,128)(2,1)S(1)}, u32[]{:S(2)}, u32[]{:S(2)}) collective-permute-start(bf16[16,64,128]{2,1,0:T(8,128)(2,1)S(1)} %get-tuple-element.41), channel_id=1, source_target_pairs={{0,23},{8,31},{16,1},{24,9},{1,16},{9,24},{17,2},{25,10},{2,17},{1... | collective-permute-start | bytes 786440 | tf_op jit(solution)/shard_map/ppermute | solution.py:527
  28.8 5.2 %shard_map.86.refs_0_ = bf16[16,64,128]{2,1,0:T(8,128)(2,1)S(1)} custom-call(s32[4]{0:T(128)S(1)} %copy-done, s32[2,32]{1,0:T(2,128)S(1)} %bitcast.7, s32[32,96,128]{2,1,0:T(8,128)S(1)} %get-tuple-element.38.refs_2_, f32[2,2,384,128]{3,2,1,0:T(8,128)S(1)} %get-tuple-element.33.refs_5_.refs_3_, f32[16,128]{1,0:T(8,128)S(1)} %get-tuple-element.34.refs_6_.refs_4_, ...), custom_call_target="tpu_custom_call" | custom-call | flops 4000000000 | bytes 4000000 | tf_op jit(solution)/shard_map/pallas_call | solution.py:434
  34.0 1.5 %collective-permute-done.5.refs_3_ = bf16[16,64,128]{2,1,0:T(8,128)(2,1)S(1)} collective-permute-done((bf16[16,64,128]{2,1,0:T(8,128)(2,1)S(1)}, bf16[16,64,128]{2,1,0:T(8,128)(2,1)S(1)}, u32[]{:S(2)}, u32[]{:S(2)}) %collective-permute-start.5) | collective-permute-done | bytes 262176 | tf_op jit(solution)/shard_map/ppermute | solution.py:527
  35.5 0.0 collective-permute-start.7
  35.5 0.0 collective-permute-start.6
  35.5 0.4 collective-permute-start.8
  35.9 0.1 collective-permute-start.11
  36.0 8.1 %collective-permute-done.7.refs_2_ = bf16[16,64,128]{2,1,0:T(8,128)(2,1)S(1)} collective-permute-done((bf16[16,64,128]{2,1,0:T(8,128)(2,1)S(1)}, bf16[16,64,128]{2,1,0:T(8,128)(2,1)S(1)}, u32[]{:S(2)}, u32[]{:S(2)}) %collective-permute-start.7) | collective-permute-done | bytes 262176 | tf_op jit(solution)/shard_map/ppermute | solution.py:527
  44.2 0.0 collective-permute-start.10
  44.2 0.0 collective-permute-done.6.refs_1_
  44.2 0.5 %collective-permute-start.9 = (bf16[16,64,128]{2,1,0:T(8,128)(2,1)S(1)}, bf16[16,64,128]{2,1,0:T(8,128)(2,1)S(1)}, u32[]{:S(2)}, u32[]{:S(2)}) collective-permute-start(bf16[16,64,128]{2,1,0:T(8,128)(2,1)S(1)} %collective-permute-done.6.refs_1_), channel_id=1, source_target_pairs={{0,8},{8,0},{16,24},{24,16},{1,9},{9,1},{17,25},{25,17},{2,10},{10... | collective-permute-start | bytes 786440 | tf_op jit(solution)/shard_map/ppermute | solution.py:527
  44.7 1.0 %collective-permute-done.10.refs_6_ = bf16[16,64,128]{2,1,0:T(8,128)(2,1)S(1)} collective-permute-done((bf16[16,64,128]{2,1,0:T(8,128)(2,1)S(1)}, bf16[16,64,128]{2,1,0:T(8,128)(2,1)S(1)}, u32[]{:S(2)}, u32[]{:S(2)}) %collective-permute-start.10) | collective-permute-done | bytes 262176 | tf_op jit(solution)/shard_map/ppermute | solution.py:527
  45.7 0.4 collective-permute-done.9.refs_5_
  46.1 2.9 %shard_map.87 = f32[32,16384]{1,0:T(8,128)} custom-call(s32[4]{0:T(128)S(1)} %copy-done, s32[2,32]{1,0:T(2,128)S(1)} %bitcast.8, bf16[16,64,128]{2,1,0:T(8,128)(2,1)S(1)} %shard_map.86.refs_0_, bf16[16,64,128]{2,1,0:T(8,128)(2,1)S(1)} %collective-permute-done.6.refs_1_, bf16[16,64,128]{2,1,0:T(8,128)(2,1)S(1)} %collective-permute-done.7.refs_2_, ...), custom_call_target="tpu_custom_call" | custom-call | tf_op jit(solution)/shard_map/pallas_call | solution.py:493
  (12 shorter events, 0.0 us)
Async XLA Ops:
  0.0 4.9 %copy-start.3 = (f32[2]{0:T(128)S(1)}, f32[2]{0:T(128)}, u32[]{:S(2)}) copy-start(f32[2]{0:T(128)} %param.10) | copy-start | bytes 28
  0.0 5.0 %copy-start.2 = (s32[2,2]{1,0:T(2,128)S(1)}, s32[2,2]{1,0:T(2,128)}, u32[]{:S(2)}) copy-start(s32[2,2]{1,0:T(2,128)} %param.11) | copy-start | bytes 52
  1.9 15.7 %collective-permute-start = (s16[96,2176]{1,0:T(8,128)(2,1)S(1)}, s16[96,2176]{1,0:T(8,128)(2,1)S(1)}, u32[]{:S(2)}, u32[]{:S(2)}) collective-permute-start(s16[96,2176]{1,0:T(8,128)(2,1)S(1)} %shard_map.82), channel_id=1, source_target_pairs={{0,1},{8,9},{16,23},{24,31},{1,2},{9,10},{17,16},{25,24},{2,3},{10... | collective-permute-start | bytes 1253384 | tf_op jit(solution)/shard_map/ppermute | solution.py:527
  5.0 9.1 %collective-permute-start.3 = (f32[2,3]{1,0:T(2,128)S(1)}, f32[2,3]{1,0:T(2,128)S(1)}, u32[]{:S(2)}, u32[]{:S(2)}) collective-permute-start(f32[2,3]{1,0:T(2,128)S(1)} %pad_maximum_fusion.1), channel_id=1, source_target_pairs={{0,24},{8,16},{16,8},{24,0},{1,25},{9,17},{17,9},{25,1},{2,26},{10... | collective-permute-start | bytes 80 | tf_op jit(solution)/shard_map/ppermute | solution.py:527
  8.8 5.4 %collective-permute-start.2 = (f32[2,3]{1,0:T(2,128)S(1)}, f32[2,3]{1,0:T(2,128)S(1)}, u32[]{:S(2)}, u32[]{:S(2)}) collective-permute-start(f32[2,3]{1,0:T(2,128)S(1)} %pad_maximum_fusion.1), channel_id=1, source_target_pairs={{0,16},{8,24},{16,0},{24,8},{1,17},{9,25},{17,1},{25,9},{2,18},{10... | collective-permute-start | bytes 80 | tf_op jit(solution)/shard_map/ppermute | solution.py:527
  9.7 4.5 %collective-permute-start.1 = (f32[2,3]{1,0:T(2,128)S(1)}, f32[2,3]{1,0:T(2,128)S(1)}, u32[]{:S(2)}, u32[]{:S(2)}) collective-permute-start(f32[2,3]{1,0:T(2,128)S(1)} %pad_maximum_fusion.1), channel_id=1, source_target_pairs={{0,8},{8,0},{16,24},{24,16},{1,9},{9,1},{17,25},{25,17},{2,10},{10... | collective-permute-start | bytes 80 | tf_op jit(solution)/shard_map/ppermute | solution.py:527
  10.3 9.0 %copy-start = (s32[4]{0:T(128)S(1)}, s32[4]{0:T(128)}, u32[]{:S(2)}) copy-start(s32[4]{0:T(128)} %pad_add_fusion.place_ref.refs_0_) | copy-start | bytes 52
  17.5 1.8 %collective-permute-start.4 = (s16[96,2176]{1,0:T(8,128)(2,1)S(1)}, s16[96,2176]{1,0:T(8,128)(2,1)S(1)}, u32[]{:S(2)}, u32[]{:S(2)}) collective-permute-start(s16[96,2176]{1,0:T(8,128)(2,1)S(1)} %collective-permute-done.refs_3_), channel_id=1, source_target_pairs={{0,8},{8,0},{16,24},{24,16},{1,9},{9,1},{17,25},{25,17},{2,10},{10... | collective-permute-start | bytes 1253384 | tf_op jit(solution)/shard_map/ppermute | solution.py:527
  17.5 11.2 %copy-start.1 = (s32[32,2]{0,1:T(2,128)S(1)}, s32[32,2]{0,1:T(2,128)}, u32[]{:S(2)}) copy-start(s32[32,2]{0,1:T(2,128)} %param.12) | copy-start | bytes 772
  23.3 12.2 %collective-permute-start.5 = (bf16[16,64,128]{2,1,0:T(8,128)(2,1)S(1)}, bf16[16,64,128]{2,1,0:T(8,128)(2,1)S(1)}, u32[]{:S(2)}, u32[]{:S(2)}) collective-permute-start(bf16[16,64,128]{2,1,0:T(8,128)(2,1)S(1)} %get-tuple-element.41), channel_id=1, source_target_pairs={{0,23},{8,31},{16,1},{24,9},{1,16},{9,24},{17,2},{25,10},{2,17},{1... | collective-permute-start | bytes 786440 | tf_op jit(solution)/shard_map/ppermute | solution.py:527
  35.5 8.6 %collective-permute-start.7 = (bf16[16,64,128]{2,1,0:T(8,128)(2,1)S(1)}, bf16[16,64,128]{2,1,0:T(8,128)(2,1)S(1)}, u32[]{:S(2)}, u32[]{:S(2)}) collective-permute-start(bf16[16,64,128]{2,1,0:T(8,128)(2,1)S(1)} %get-tuple-element.41), channel_id=1, source_target_pairs={{0,7},{8,15},{16,17},{24,25},{1,0},{9,8},{17,18},{25,26},{2,1},{10... | collective-permute-start | bytes 786440 | tf_op jit(solution)/shard_map/ppermute | solution.py:527
  35.5 8.6 %collective-permute-start.6 = (bf16[16,64,128]{2,1,0:T(8,128)(2,1)S(1)}, bf16[16,64,128]{2,1,0:T(8,128)(2,1)S(1)}, u32[]{:S(2)}, u32[]{:S(2)}) collective-permute-start(bf16[16,64,128]{2,1,0:T(8,128)(2,1)S(1)} %shard_map.86.refs_0_), channel_id=1, source_target_pairs={{0,16},{8,24},{16,0},{24,8},{1,17},{9,25},{17,1},{25,9},{2,18},{10... | collective-permute-start | bytes 786440 | tf_op jit(solution)/shard_map/ppermute | solution.py:527
  35.5 9.2 %collective-permute-start.8 = (bf16[16,64,128]{2,1,0:T(8,128)(2,1)S(1)}, bf16[16,64,128]{2,1,0:T(8,128)(2,1)S(1)}, u32[]{:S(2)}, u32[]{:S(2)}) collective-permute-start(bf16[16,64,128]{2,1,0:T(8,128)(2,1)S(1)} %shard_map.86.refs_0_), channel_id=1, source_target_pairs={{0,8},{8,0},{16,24},{24,16},{1,9},{9,1},{17,25},{25,17},{2,10},{10... | collective-permute-start | bytes 786440 | tf_op jit(solution)/shard_map/ppermute | solution.py:527
  35.9 8.7 %collective-permute-start.11 = (bf16[16,64,128]{2,1,0:T(8,128)(2,1)S(1)}, bf16[16,64,128]{2,1,0:T(8,128)(2,1)S(1)}, u32[]{:S(2)}, u32[]{:S(2)}) collective-permute-start(bf16[16,64,128]{2,1,0:T(8,128)(2,1)S(1)} %collective-permute-done.5.refs_3_), channel_id=1, source_target_pairs={{0,8},{8,0},{16,24},{24,16},{1,9},{9,1},{17,25},{25,17},{2,10},{10... | collective-permute-start | bytes 786440 | tf_op jit(solution)/shard_map/ppermute | solution.py:527
  44.2 1.5 %collective-permute-start.10 = (bf16[16,64,128]{2,1,0:T(8,128)(2,1)S(1)}, bf16[16,64,128]{2,1,0:T(8,128)(2,1)S(1)}, u32[]{:S(2)}, u32[]{:S(2)}) collective-permute-start(bf16[16,64,128]{2,1,0:T(8,128)(2,1)S(1)} %collective-permute-done.7.refs_2_), channel_id=1, source_target_pairs={{0,8},{8,0},{16,24},{24,16},{1,9},{9,1},{17,25},{25,17},{2,10},{10... | collective-permute-start | bytes 786440 | tf_op jit(solution)/shard_map/ppermute | solution.py:527
  44.2 1.9 %collective-permute-start.9 = (bf16[16,64,128]{2,1,0:T(8,128)(2,1)S(1)}, bf16[16,64,128]{2,1,0:T(8,128)(2,1)S(1)}, u32[]{:S(2)}, u32[]{:S(2)}) collective-permute-start(bf16[16,64,128]{2,1,0:T(8,128)(2,1)S(1)} %collective-permute-done.6.refs_1_), channel_id=1, source_target_pairs={{0,8},{8,0},{16,24},{24,16},{1,9},{9,1},{17,25},{25,17},{2,10},{10... | collective-permute-start | bytes 786440 | tf_op jit(solution)/shard_map/ppermute | solution.py:527

commit v4 on v3

--- a/solution.py
+++ b/solution.py
@@ -19,6 +19,7 @@
 BITS = 4
 HALO0 = 64
 HALO1 = 32
+HALO = HALO0 + HALO1
 TABLE = 384
 MIB = 1024 * 1024
 CORES = 2
@@ -88,12 +89,13 @@
         copy.start()
     pos_buf[...] = jnp.zeros(pos_buf.shape, jnp.int32)
     pos_buf[:2, : pos_ref.shape[1]] = pos_ref[...]
-    out_ref[:16, half:] = pos_buf[...].astype(jnp.int16)
+    out_ref[half // LANES * HALO :, :] = pos_buf[...].astype(jnp.int16)
     for layer, (buf, first) in enumerate(((zero_buf, 0), (one_buf, HALO0))):
         for part in range(parts):
             copies[parts * layer + part].wait()
-            cols = slice(part * step, (part + 1) * step)
-            out_ref[first : first + buf.shape[0], cols] = buf[:, cols].astype(jnp.int16)
+            for tile in range(part * step // LANES, (part + 1) * step // LANES):
+                rows = slice(tile * HALO + first, tile * HALO + first + buf.shape[0])
+                out_ref[rows, :] = buf[:, tile * LANES : (tile + 1) * LANES].astype(jnp.int16)
 
 
 def pack_rows(atoms, positions):
@@ -101,7 +103,7 @@
     vmem = pl.BlockSpec(memory_space=pltpu.VMEM)
     return pl.pallas_call(
         pack_kernel,
-        out_shape=pltpu.VMEM((HALO0 + HALO1, half + LANES), jnp.int16),
+        out_shape=pltpu.VMEM((half // LANES * HALO + 16, LANES), jnp.int16),
         in_specs=[pl.BlockSpec(memory_space=pltpu.HBM), vmem],
         out_specs=vmem,
         scratch_shapes=[
@@ -246,9 +248,8 @@
         lo = 0 if upper else HALO0 - HALO1
         for source, at in zip(halo_refs, (core, 1 - core)):
             for tile in range(half_tiles):
-                cols = slice(tile * LANES, (tile + 1) * LANES)
-                zero = source[:HALO0, cols].astype(jnp.int32)
-                one = source[HALO0:, cols].astype(jnp.int32) * TYPES
+                zero = source[tile * HALO : tile * HALO + HALO0, :].astype(jnp.int32)
+                one = source[tile * HALO + HALO0 : (tile + 1) * HALO, :].astype(jnp.int32) * TYPES
                 blocks = [zero[:PACK], zero[PACK:]]
                 blocks[lo // PACK] = blocks[lo // PACK] + one
                 index = at * half_tiles + tile
@@ -381,7 +382,7 @@
 
 
 def ext_kernel(beams, batch_size, place_ref, near_ref, words_in, mine_ref, other_ref, *refs):
-    constants, (out_ref, words), scratch = refs[:5], refs[5:7], refs[7:]
+    constants, (low_ref, high_ref, words), out_ref, scratch = refs[:5], refs[5:8], refs[8], refs[9:]
     row_list, col_list, slot_list = scratch[5:]
     side, core, near_base = place_ref[0], place_ref[1], place_ref[3]
     merge_rows(side, core, (mine_ref, other_ref), words_in, words)
@@ -395,15 +396,19 @@
         slot_list[found] = k
         return found + reaches.astype(jnp.int32)
 
-    total = lax.fori_loop(0, out_ref.shape[0], add, 0)
+    total = lax.fori_loop(0, out_ref.shape[0], add, 0, unroll=True)
 
     @pl.when(total > 0)
     def _():
         run_tasks(beams, batch_size, side, total, words, *constants, out_ref, scratch)
 
+    half = low_ref.shape[0]
+    low_ref[...] = out_ref[:half]
+    high_ref[...] = out_ref[half:]
+
 
 def own_kernel(beams, batch_size, place_ref, pos_ref, words, *refs):
-    constants, out_ref, scratch = refs[:5], refs[5], refs[6:]
+    constants, (low_ref, high_ref), out_ref, scratch = refs[:5], refs[5:7], refs[7], refs[8:]
     row_list, col_list, slot_list = scratch[5:]
     side, core, row_base = place_ref[0], place_ref[1], place_ref[2]
     count = out_ref.shape[0]
@@ -415,8 +420,10 @@
         slot_list[k] = k
         return carry
 
-    lax.fori_loop(0, count, add, 0)
+    lax.fori_loop(0, count, add, 0, unroll=True)
     run_tasks(beams, batch_size, side, count, words, *constants, out_ref, scratch)
+    low_ref[...] = out_ref[: count // 2]
+    high_ref[...] = out_ref[count // 2 :]
 
 
 def propagate(beams, place, probes, words, halo, constants):
@@ -425,19 +432,20 @@
     vmem = pl.BlockSpec(memory_space=pltpu.VMEM)
     ext = bool(halo)
     body = ext_kernel if ext else own_kernel
-    batch_size = 4 if ext else count
+    batch_size = 10 if ext else count
 
     def kernel(*refs):
         body(beams, batch_size, *refs)
 
-    shape = jax.ShapeDtypeStruct((count, GROUP, WIN), jnp.bfloat16)
+    half = jax.ShapeDtypeStruct((count // 2, GROUP, WIN), jnp.bfloat16)
     return pl.pallas_call(
         kernel,
-        out_shape=[shape, pltpu.VMEM(words.shape, jnp.int32)] if ext else shape,
+        out_shape=[half, half, pltpu.VMEM(words.shape, jnp.int32)] if ext else [half, half],
         in_specs=[smem] * 2 + [vmem] * (8 if ext else 6),
-        out_specs=[vmem, vmem] if ext else vmem,
-        input_output_aliases={2: 1} if ext else {},
+        out_specs=[vmem] * (3 if ext else 2),
+        input_output_aliases={2: 2} if ext else {},
         scratch_shapes=[
+            pltpu.VMEM((count, GROUP, WIN), jnp.bfloat16),
             pltpu.VMEM((batch_size * 3 * GROUP, 4 * LANES), jnp.bfloat16),
             pltpu.VMEM((batch_size, 2, 3 * GROUP, 2 * LANES), jnp.bfloat16),
             pltpu.VMEM((batch_size * 2 * GROUP, 4 * LANES), jnp.bfloat16),
@@ -452,7 +460,33 @@
     )(place, probes, words, *halo, *constants)
 
 
-PAD = 3 * WIN
+def merge_kernel(half, place_ref, pos_ref, own_ref, same_ref, out_ref):
+    side, core, row_base = place_ref[0], place_ref[1], place_ref[2]
+    line = lax.broadcasted_iota(jnp.int32, (GROUP, LANES), 0).astype(jnp.int16)
+    for k in range(out_ref.shape[0]):
+        row = pos_ref[0, CORES * (k + half * out_ref.shape[0]) + core] - row_base
+        low = jnp.where(side == 0, jnp.clip(row - 2 * GROUP, 0, GROUP), 0)
+        high = jnp.where(side == 0, GROUP, jnp.clip(row, 0, GROUP))
+        kept = (line >= low.astype(jnp.int16)) & (line < high.astype(jnp.int16))
+        out_ref[k] = jnp.where(kept, own_ref[k], same_ref[k])
+
+
+def merge_pieces(half, place, positions, own, same):
+    def kernel(*refs):
+        merge_kernel(half, *refs)
+
+    smem = pl.BlockSpec(memory_space=pltpu.SMEM)
+    vmem = pl.BlockSpec(memory_space=pltpu.VMEM)
+    return pl.pallas_call(
+        kernel,
+        out_shape=jax.ShapeDtypeStruct(own.shape, own.dtype),
+        in_specs=[smem, smem, vmem, vmem],
+        out_specs=vmem,
+        compiler_params=pltpu.CompilerParams(vmem_limit_bytes=16 * MIB),
+    )(place, positions, own, same)
+
+
+PAD = 3 * WIN + 1
 
 
 def gather_kernel(place_ref, pos_ref, *refs):
@@ -463,17 +497,22 @@
         rows = pl.ds(pl.multiple_of(8 * group, 8), 8)
         return pltpu.make_async_copy(out_buf.at[rows], out_hbm.at[rows], sems.at[group])
 
-    def step(group, carry):
+    def step(half, local, carry):
+        group = local + half * groups // 2
         for par in range(2):
             parity = core if par == 0 else 1 - core
+            own, facing = refs[4 * par + half], refs[4 * par + 2 + half]
             for i in range(4):
-                k = 4 * group + i
-                row = pos_ref[0, 2 * k + parity] - row_base
-                start = jnp.where(row < GROUP, row, jnp.where(row > 2 * GROUP, row - GROUP, GROUP))
+                row = pos_ref[0, 2 * (4 * group + i) + parity] - row_base
+                k = 4 * local + i
+                below = row > 2 * GROUP
+                start = jnp.where(row < GROUP, row, jnp.where(below, row - GROUP, GROUP))
                 base = (2 * i + parity) * PAD + WIN - start
-                places = (GROUP + GROUP * side, 2 * GROUP - GROUP * side, 3 * GROUP * (1 - side), 3 * GROUP * side)
-                for piece, at in zip(refs[4 * par : 4 * par + 4], places):
-                    window[pl.ds(base + at, GROUP), :] = piece[k].astype(jnp.float32)
+                mine, across = own[k].astype(jnp.float32), facing[k].astype(jnp.float32)
+                window[pl.ds(base + GROUP + GROUP * side, GROUP), :] = mine
+                window[pl.ds(base + 2 * GROUP - GROUP * side, GROUP), :] = across
+                wrapped = jnp.where(below == (side == 0), mine, across)
+                window[pl.ds(base + jnp.where(below, 3 * GROUP, 0), GROUP), :] = wrapped
         rows = pl.ds(pl.multiple_of(8 * group, 8), 8)
         for u in range(WIN):
             out_buf[rows, u * WIN : (u + 1) * WIN] = window[pl.ds(WIN + u, 8, stride=PAD), :]
@@ -481,7 +520,8 @@
         return carry
 
     groups = out_buf.shape[0] // 8
-    lax.fori_loop(0, groups, step, 0)
+    for half in range(2):
+        lax.fori_loop(0, groups // 2, lambda local, carry, half=half: step(half, local, carry), 0)
     for group in range(groups):
         copy(group).wait()
 
@@ -543,14 +583,13 @@
     words = own_words(place, atoms)
     table = probe_table(beam_rows, phases, rows_total, width)
     mine, words, table = lax.optimization_barrier((mine, words, table))
-    near = mine[:2, width // cores : width // cores + probes].astype(jnp.int32)
-    ext, words = propagate(beams, place, near, words, [mine, swap_cores(mine)], table)
-    far = across(ext, lambda s, y, c: (s - 1 + 2 * y, (1 - y, c)))
+    near = mine[width // cores // LANES * HALO :][:2, :probes].astype(jnp.int32)
+    *ext, words = propagate(beams, place, near, words, [mine, swap_cores(mine)], table)
+    same = [across(half, lambda s, y, c: (s - 1 + 2 * y, (y, c))) for half in ext]
     own = propagate(beams, place, positions, words, [], table)
-    own, far, ext = lax.optimization_barrier((own, far, ext))
-    facing = across(own, lambda s, y, c: (s, (1 - y, c)))
-    same = across(ext, lambda s, y, c: (s - 1 + 2 * y, (y, c)))
-    pieces = [own, facing, same, far]
+    own = [merge_pieces(n, place, positions, *pair) for n, pair in enumerate(zip(own, same))]
+    facing = [across(half, lambda s, y, c: (s, (1 - y, c))) for half in own]
+    pieces = own + facing
     return put_together(place, positions, pieces + [swap_cores(piece) for piece in pieces])
 
 

time: 49.5 us -> 43.6 us (0.88)
  waiting for transfers between devices: 13.7 us -> 6.72 us
  Pallas kernels: 19.5 us -> 23 us
  starting transfers between devices: 14.2 us -> 12 us
    ppermute x12 -> x13, waiting for transfers between devices: 13.7 us -> 6.72 us  [across(): return lax.ppermute(array, ('beam', 'strip'), pairs)]
    pallas_call x3 -> x5, Pallas kernels: 11 us -> 15.4 us  [the longest x2 12.3 us: propagate(): pl.pallas_call(kernel, out_shape=[half, half, pltpu.VMEM(words.shape, jnp...]
    ppermute x12 -> x13, starting transfers between devices: 14.2 us -> 12 us  [across(): return lax.ppermute(array, ('beam', 'strip'), pairs)]
    pallas_call x1, Pallas kernels: 2.93 us -> 2.01 us  [put_together(): pl.pallas_call(gather_kernel, out_shape=jax.ShapeDtypeStruct((probes, WIN...]
  transfers between devices with their start and end apart: 12 -> 13, of which waited for: 6 -> 5; matrix products, arithmetic and copies ran while one was open for 3% -> 3% of each run, Pallas kernels for 22% -> 27%
where the time goes in v4:
time: 43.6 us; the launch traced here: 43.5 us
  Pallas kernels  23 us (53%)
  starting transfers between devices  12 us (28%)
  waiting for transfers between devices  6.72 us (15%)
  other arithmetic  1.38 us (3%)
    pallas_call x2, Pallas kernels, propagate(): pl.pallas_call(kernel, out_shape=[half, half, pltpu.VMEM(words.shape, jnp...  12.3 us
    ppermute x13, starting transfers between devices, across(): return lax.ppermute(array, ('beam', 'strip'), pairs)  12 us
    ppermute x13, waiting for transfers between devices, across(): return lax.ppermute(array, ('beam', 'strip'), pairs)  6.72 us
    pallas_call x1, Pallas kernels, own_words(): pl.pallas_call(words_kernel, out_shape=pltpu.VMEM((width // LANES, GROUP...  3.81 us
    pallas_call x1, Pallas kernels, put_together(): pl.pallas_call(gather_kernel, out_shape=jax.ShapeDtypeStruct((probes, WIN...  2.01 us
    pallas_call x1, Pallas kernels, pack_rows(): pl.pallas_call(pack_kernel, out_shape=pltpu.VMEM((half // LANES * HALO +...  1.86 us
    pallas_call x1, Pallas kernels, probe_table(): pl.pallas_call(kernel, out_shape=[pltpu.VMEM((2, 2, TABLE, LANES), jnp.fl...  1.77 us
    pallas_call x2, Pallas kernels, merge_pieces(): pl.pallas_call(kernel, out_shape=jax.ShapeDtypeStruct(own.shape, own.dtyp...  1.22 us
  transfers between devices with their start and end apart: 13, of which 5 were waited for; matrix products, arithmetic and copies ran while one was open for 3% of the time, Pallas kernels for 27%

profile of v4, /device:TPU:0, one launch (start us, length us, event | category | flops | bytes accessed | tf_op | source)
XLA Modules:
  0.0 43.5 jit_solution(11997826941406259670)
XLA Ops:
  0.0 1.9 %shard_map.82 = s16[1552,128]{1,0:T(8,128)(2,1)S(1)} custom-call(s32[2,192,4096]{2,1,0:T(8,128)} %atoms_hbm.3, s32[2,32]{1,0:T(2,128)} %bitcast.6), custom_call_target="tpu_custom_call" | custom-call | tf_op jit(solution)/shard_map/pallas_call | solution.py:104
  1.9 3.0 %collective-permute-start = (s16[1552,128]{1,0:T(8,128)(2,1)S(1)}, s16[1552,128]{1,0:T(8,128)(2,1)S(1)}, u32[]{:S(2)}, u32[]{:S(2)}) collective-permute-start(s16[1552,128]{1,0:T(8,128)(2,1)S(1)} %shard_map.82), channel_id=1, source_target_pairs={{0,1},{8,9},{16,23},{24,31},{1,2},{9,10},{17,16},{25,24},{2,3},{10... | collective-permute-start | bytes 1191944 | tf_op jit(solution)/shard_map/ppermute | solution.py:567
  4.9 0.1 copy.10
  5.0 0.1 pad_maximum_fusion.1
  5.0 3.7 %collective-permute-start.3 = (f32[2,3]{1,0:T(2,128)S(1)}, f32[2,3]{1,0:T(2,128)S(1)}, u32[]{:S(2)}, u32[]{:S(2)}) collective-permute-start(f32[2,3]{1,0:T(2,128)S(1)} %pad_maximum_fusion.1), channel_id=1, source_target_pairs={{0,24},{8,16},{16,8},{24,0},{1,25},{9,17},{17,9},{25,1},{2,26},{10... | collective-permute-start | bytes 80 | tf_op jit(solution)/shard_map/ppermute | solution.py:567
  8.8 0.9 %collective-permute-start.2 = (f32[2,3]{1,0:T(2,128)S(1)}, f32[2,3]{1,0:T(2,128)S(1)}, u32[]{:S(2)}, u32[]{:S(2)}) collective-permute-start(f32[2,3]{1,0:T(2,128)S(1)} %pad_maximum_fusion.1), channel_id=1, source_target_pairs={{0,16},{8,24},{16,0},{24,8},{1,17},{9,25},{17,1},{25,9},{2,18},{10... | collective-permute-start | bytes 80 | tf_op jit(solution)/shard_map/ppermute | solution.py:567
  9.7 0.0 collective-permute-start.1
  9.7 0.6 %pad_add_fusion.place_ref.refs_0_ = s32[4]{0:T(128)} fusion(s32[1]{0:T(128)} %bitcast.3, s32[1]{0:T(128)} %bitcast.2, s32[1]{0:T(128)} %bitcast.1, s32[1]{0:T(128)} %bitcast), kind=kLoop, calls=%fused_computation.2 | loop fusion | flops 12 | bytes 32 | tf_op jit(solution)/shard_map/stack | solution.py:559
  10.3 3.8 %shard_map.83.refs_2_ = s32[32,96,128]{2,1,0:T(8,128)S(1)} custom-call(s32[4]{0:T(128)} %pad_add_fusion.place_ref.refs_0_, s32[2,192,4096]{2,1,0:T(8,128)} %atoms_hbm.3), custom_call_target="tpu_custom_call" | custom-call | flops 31457280 | bytes 9437184 | tf_op jit(solution)/shard_map/pallas_call | solution.py:154
  14.2 0.0 collective-permute-done.3
  14.2 0.0 collective-permute-done.1
  14.2 0.7 %pad_maximum_fusion.refs_0_ = f32[8,3]{1,0:T(8,128)} fusion(f32[2,3]{1,0:T(2,128)S(1)} %collective-permute-done.3, f32[2,3]{1,0:T(2,128)S(1)} %collective-permute-done.2, f32[2,3]{1,0:T(2,128)S(1)} %collective-permute-done.1, f32[2,1]{1,0:T(2,128)S(1)} %copy.10, f32[2,2]{1,0:T(2,128)S(1)} %convert_element_type.6), kind=kLoop, calls=%fused_computation | loop fusion | flops 96 | bytes 192 | tf_op jit(solution)/shard_map/concatenate | solution.py:582
  14.9 1.8 %shard_map.84 = (f32[2,2,384,128]{3,2,1,0:T(8,128)S(1)}, f32[16,128]{1,0:T(8,128)S(1)}, bf16[512,256]{1,0:T(8,128)(2,1)S(1)}, bf16[256,256]{1,0:T(8,128)(2,1)S(1)}, bf16[128,256]{1,0:T(8,128)(2,1)S(1)}) custom-call(f32[8,3]{1,0:T(8,128)} %pad_maximum_fusion.refs_0_, f32[2,4]{1,0:T(2,128)} %refs_1_.1, bf16[512,256]{1,0:T(8,128)(2,1)} %constant.56.clone.refs_2_, ...), custom_call_target="tpu_custom_call" | custom-call | flops 100000000 | bytes 1000000 | tf_op jit(solution)/shard_map/pallas_call | solution.py:229
  16.6 0.5 %collective-permute-done.refs_3_ = s16[1552,128]{1,0:T(8,128)(2,1)S(1)} collective-permute-done((s16[1552,128]{1,0:T(8,128)(2,1)S(1)}, s16[1552,128]{1,0:T(8,128)(2,1)S(1)}, u32[]{:S(2)}, u32[]{:S(2)}) %collective-permute-start) | collective-permute-done | bytes 397344 | tf_op jit(solution)/shard_map/ppermute | solution.py:567
  17.1 0.1 collective-permute-start.4
  17.2 1.6 %collective-permute-done.4.refs_4_ = s16[1552,128]{1,0:T(8,128)(2,1)S(1)} collective-permute-done((s16[1552,128]{1,0:T(8,128)(2,1)S(1)}, s16[1552,128]{1,0:T(8,128)(2,1)S(1)}, u32[]{:S(2)}, u32[]{:S(2)}) %collective-permute-start.4) | collective-permute-done | bytes 397344 | tf_op jit(solution)/shard_map/ppermute | solution.py:567
  18.8 7.2 %shard_map.85 = (bf16[8,64,128]{2,1,0:T(8,128)(2,1)S(1)}, bf16[8,64,128]{2,1,0:T(8,128)(2,1)S(1)}, s32[32,96,128]{2,1,0:T(8,128)S(1)}) custom-call(s32[4]{0:T(128)S(1)} %copy-done.1, s32[2,32]{1,0:T(2,128)S(1)} %slice_convert_fusion.refs_1_, s32[32,96,128]{2,1,0:T(8,128)S(1)} %shard_map.83.refs_2_, ...), custom_call_target="tpu_custom_call", output_to_operand_aliasing={{2}: (2, {})} | custom-call | flops 4000000000 | bytes 4000000 | tf_op jit(solution)/shard_map/pallas_call | solution.py:441
  26.1 0.1 collective-permute-start.5
  26.1 0.2 collective-permute-start.6
  26.4 5.1 %shard_map.86 = (bf16[8,64,128]{2,1,0:T(8,128)(2,1)S(1)}, bf16[8,64,128]{2,1,0:T(8,128)(2,1)S(1)}) custom-call(s32[4]{0:T(128)S(1)} %copy-done.1, s32[2,32]{1,0:T(2,128)S(1)} %bitcast.7, s32[32,96,128]{2,1,0:T(8,128)S(1)} %get-tuple-element.38.refs_2_, f32[2,2,384,128]{3,2,1,0:T(8,128)S(1)} %get-tuple-element.33.refs_5_.refs_3_, ...), custom_call_target="tpu_custom_call" | custom-call | flops 4000000000 | bytes 4000000 | tf_op jit(solution)/shard_map/pallas_call | solution.py:441
  31.5 0.0 collective-permute-done.5.refs_3_
  31.5 0.6 %shard_map.87.refs_0_ = bf16[8,64,128]{2,1,0:T(8,128)(2,1)S(1)} custom-call(s32[4]{0:T(128)S(1)} %copy-done.1, s32[2,32]{1,0:T(2,128)S(1)} %bitcast.8, bf16[8,64,128]{2,1,0:T(8,128)(2,1)S(1)} %get-tuple-element.39.refs_2_, bf16[8,64,128]{2,1,0:T(8,128)(2,1)S(1)} %collective-permute-done.5.refs_3_), custom_call_target="tpu_custom_call" | custom-call | tf_op jit(solution)/shard_map/pallas_call | solution.py:480
  32.1 1.9 %collective-permute-start.7 = (bf16[8,64,128]{2,1,0:T(8,128)(2,1)S(1)}, bf16[8,64,128]{2,1,0:T(8,128)(2,1)S(1)}, u32[]{:S(2)}, u32[]{:S(2)}) collective-permute-start(bf16[8,64,128]{2,1,0:T(8,128)(2,1)S(1)} %shard_map.87.refs_0_), channel_id=1, source_target_pairs={{0,16},{8,24},{16,0},{24,8},{1,17},{9,25},{17,1},{25,9},{2,18},{10... | collective-permute-start | bytes 393224 | tf_op jit(solution)/shard_map/ppermute | solution.py:567
  34.0 0.6 %shard_map.88.refs_1_ = bf16[8,64,128]{2,1,0:T(8,128)(2,1)S(1)} custom-call(s32[4]{0:T(128)S(1)} %copy-done.1, s32[2,32]{1,0:T(2,128)S(1)} %bitcast.9, bf16[8,64,128]{2,1,0:T(8,128)(2,1)S(1)} %get-tuple-element.41.refs_2_, bf16[8,64,128]{2,1,0:T(8,128)(2,1)S(1)} %collective-permute-done.6.refs_3_), custom_call_target="tpu_custom_call" | custom-call | tf_op jit(solution)/shard_map/pallas_call | solution.py:480
  34.7 1.5 %collective-permute-start.8 = (bf16[8,64,128]{2,1,0:T(8,128)(2,1)S(1)}, bf16[8,64,128]{2,1,0:T(8,128)(2,1)S(1)}, u32[]{:S(2)}, u32[]{:S(2)}) collective-permute-start(bf16[8,64,128]{2,1,0:T(8,128)(2,1)S(1)} %shard_map.88.refs_1_), channel_id=1, source_target_pairs={{0,16},{8,24},{16,0},{24,8},{1,17},{9,25},{17,1},{25,9},{2,18},{10... | collective-permute-start | bytes 393224 | tf_op jit(solution)/shard_map/ppermute | solution.py:567
  36.2 0.0 collective-permute-start.9
  36.2 0.5 %collective-permute-start.10 = (bf16[8,64,128]{2,1,0:T(8,128)(2,1)S(1)}, bf16[8,64,128]{2,1,0:T(8,128)(2,1)S(1)}, u32[]{:S(2)}, u32[]{:S(2)}) collective-permute-start(bf16[8,64,128]{2,1,0:T(8,128)(2,1)S(1)} %shard_map.88.refs_1_), channel_id=1, source_target_pairs={{0,8},{8,0},{16,24},{24,16},{1,9},{9,1},{17,25},{25,17},{2,10},{10... | collective-permute-start | bytes 393224 | tf_op jit(solution)/shard_map/ppermute | solution.py:567
  36.7 1.2 %collective-permute-done.7.refs_2_ = bf16[8,64,128]{2,1,0:T(8,128)(2,1)S(1)} collective-permute-done((bf16[8,64,128]{2,1,0:T(8,128)(2,1)S(1)}, bf16[8,64,128]{2,1,0:T(8,128)(2,1)S(1)}, u32[]{:S(2)}, u32[]{:S(2)}) %collective-permute-start.7) | collective-permute-done | bytes 131104 | tf_op jit(solution)/shard_map/ppermute | solution.py:567
  37.9 0.0 collective-permute-start.11
  37.9 2.1 %collective-permute-done.8.refs_3_ = bf16[8,64,128]{2,1,0:T(8,128)(2,1)S(1)} collective-permute-done((bf16[8,64,128]{2,1,0:T(8,128)(2,1)S(1)}, bf16[8,64,128]{2,1,0:T(8,128)(2,1)S(1)}, u32[]{:S(2)}, u32[]{:S(2)}) %collective-permute-start.8) | collective-permute-done | bytes 131104 | tf_op jit(solution)/shard_map/ppermute | solution.py:567
  40.0 1.3 %collective-permute-done.12.refs_7_ = bf16[8,64,128]{2,1,0:T(8,128)(2,1)S(1)} collective-permute-done((bf16[8,64,128]{2,1,0:T(8,128)(2,1)S(1)}, bf16[8,64,128]{2,1,0:T(8,128)(2,1)S(1)}, u32[]{:S(2)}, u32[]{:S(2)}) %collective-permute-start.12) | collective-permute-done | bytes 131104 | tf_op jit(solution)/shard_map/ppermute | solution.py:567
  41.3 2.0 %shard_map.89 = f32[32,16384]{1,0:T(8,128)} custom-call(s32[4]{0:T(128)S(1)} %copy-done.1, s32[2,32]{1,0:T(2,128)S(1)} %bitcast.10, bf16[8,64,128]{2,1,0:T(8,128)(2,1)S(1)} %shard_map.87.refs_0_, bf16[8,64,128]{2,1,0:T(8,128)(2,1)S(1)} %shard_map.88.refs_1_, bf16[8,64,128]{2,1,0:T(8,128)(2,1)S(1)} %collective-permute-done.7.refs_2_, ...), custom_call_target="tpu_custom_call" | custom-call | tf_op jit(solution)/shard_map/pallas_call | solution.py:533
  (16 shorter events, 0.0 us)
Async XLA Ops:
  0.0 4.9 %copy-start.3 = (f32[2]{0:T(128)S(1)}, f32[2]{0:T(128)}, u32[]{:S(2)}) copy-start(f32[2]{0:T(128)} %param.10) | copy-start | bytes 28
  0.0 5.0 %copy-start.2 = (s32[2,2]{1,0:T(2,128)S(1)}, s32[2,2]{1,0:T(2,128)}, u32[]{:S(2)}) copy-start(s32[2,2]{1,0:T(2,128)} %param.11) | copy-start | bytes 52
  1.9 15.2 %collective-permute-start = (s16[1552,128]{1,0:T(8,128)(2,1)S(1)}, s16[1552,128]{1,0:T(8,128)(2,1)S(1)}, u32[]{:S(2)}, u32[]{:S(2)}) collective-permute-start(s16[1552,128]{1,0:T(8,128)(2,1)S(1)} %shard_map.82), channel_id=1, source_target_pairs={{0,1},{8,9},{16,23},{24,31},{1,2},{9,10},{17,16},{25,24},{2,3},{10... | collective-permute-start | bytes 1191944 | tf_op jit(solution)/shard_map/ppermute | solution.py:567
  5.0 9.1 %collective-permute-start.3 = (f32[2,3]{1,0:T(2,128)S(1)}, f32[2,3]{1,0:T(2,128)S(1)}, u32[]{:S(2)}, u32[]{:S(2)}) collective-permute-start(f32[2,3]{1,0:T(2,128)S(1)} %pad_maximum_fusion.1), channel_id=1, source_target_pairs={{0,24},{8,16},{16,8},{24,0},{1,25},{9,17},{17,9},{25,1},{2,26},{10... | collective-permute-start | bytes 80 | tf_op jit(solution)/shard_map/ppermute | solution.py:567
  8.8 5.4 %collective-permute-start.2 = (f32[2,3]{1,0:T(2,128)S(1)}, f32[2,3]{1,0:T(2,128)S(1)}, u32[]{:S(2)}, u32[]{:S(2)}) collective-permute-start(f32[2,3]{1,0:T(2,128)S(1)} %pad_maximum_fusion.1), channel_id=1, source_target_pairs={{0,16},{8,24},{16,0},{24,8},{1,17},{9,25},{17,1},{25,9},{2,18},{10... | collective-permute-start | bytes 80 | tf_op jit(solution)/shard_map/ppermute | solution.py:567
  9.7 4.5 %collective-permute-start.1 = (f32[2,3]{1,0:T(2,128)S(1)}, f32[2,3]{1,0:T(2,128)S(1)}, u32[]{:S(2)}, u32[]{:S(2)}) collective-permute-start(f32[2,3]{1,0:T(2,128)S(1)} %pad_maximum_fusion.1), channel_id=1, source_target_pairs={{0,8},{8,0},{16,24},{24,16},{1,9},{9,1},{17,25},{25,17},{2,10},{10... | collective-permute-start | bytes 80 | tf_op jit(solution)/shard_map/ppermute | solution.py:567
  10.3 8.5 %copy-start.1 = (s32[4]{0:T(128)S(1)}, s32[4]{0:T(128)}, u32[]{:S(2)}) copy-start(s32[4]{0:T(128)} %pad_add_fusion.place_ref.refs_0_) | copy-start | bytes 52
  17.1 1.7 %collective-permute-start.4 = (s16[1552,128]{1,0:T(8,128)(2,1)S(1)}, s16[1552,128]{1,0:T(8,128)(2,1)S(1)}, u32[]{:S(2)}, u32[]{:S(2)}) collective-permute-start(s16[1552,128]{1,0:T(8,128)(2,1)S(1)} %collective-permute-done.refs_3_), channel_id=1, source_target_pairs={{0,8},{8,0},{16,24},{24,16},{1,9},{9,1},{17,25},{25,17},{2,10},{10... | collective-permute-start | bytes 1191944 | tf_op jit(solution)/shard_map/ppermute | solution.py:567
  17.2 9.2 %copy-start = (s32[32,2]{0,1:T(2,128)S(1)}, s32[32,2]{0,1:T(2,128)}, u32[]{:S(2)}) copy-start(s32[32,2]{0,1:T(2,128)} %param.12) | copy-start | bytes 772
  26.1 5.4 %collective-permute-start.5 = (bf16[8,64,128]{2,1,0:T(8,128)(2,1)S(1)}, bf16[8,64,128]{2,1,0:T(8,128)(2,1)S(1)}, u32[]{:S(2)}, u32[]{:S(2)}) collective-permute-start(bf16[8,64,128]{2,1,0:T(8,128)(2,1)S(1)} %get-tuple-element.40), channel_id=1, source_target_pairs={{0,7},{8,15},{16,17},{24,25},{1,0},{9,8},{17,18},{25,26},{2,1},{10... | collective-permute-start | bytes 393224 | tf_op jit(solution)/shard_map/ppermute | solution.py:567
  26.1 7.9 %collective-permute-start.6 = (bf16[8,64,128]{2,1,0:T(8,128)(2,1)S(1)}, bf16[8,64,128]{2,1,0:T(8,128)(2,1)S(1)}, u32[]{:S(2)}, u32[]{:S(2)}) collective-permute-start(bf16[8,64,128]{2,1,0:T(8,128)(2,1)S(1)} %get-tuple-element.42), channel_id=1, source_target_pairs={{0,7},{8,15},{16,17},{24,25},{1,0},{9,8},{17,18},{25,26},{2,1},{10... | collective-permute-start | bytes 393224 | tf_op jit(solution)/shard_map/ppermute | solution.py:567
  32.1 5.7 %collective-permute-start.7 = (bf16[8,64,128]{2,1,0:T(8,128)(2,1)S(1)}, bf16[8,64,128]{2,1,0:T(8,128)(2,1)S(1)}, u32[]{:S(2)}, u32[]{:S(2)}) collective-permute-start(bf16[8,64,128]{2,1,0:T(8,128)(2,1)S(1)} %shard_map.87.refs_0_), channel_id=1, source_target_pairs={{0,16},{8,24},{16,0},{24,8},{1,17},{9,25},{17,1},{25,9},{2,18},{10... | collective-permute-start | bytes 393224 | tf_op jit(solution)/shard_map/ppermute | solution.py:567
  34.7 5.3 %collective-permute-start.8 = (bf16[8,64,128]{2,1,0:T(8,128)(2,1)S(1)}, bf16[8,64,128]{2,1,0:T(8,128)(2,1)S(1)}, u32[]{:S(2)}, u32[]{:S(2)}) collective-permute-start(bf16[8,64,128]{2,1,0:T(8,128)(2,1)S(1)} %shard_map.88.refs_1_), channel_id=1, source_target_pairs={{0,16},{8,24},{16,0},{24,8},{1,17},{9,25},{17,1},{25,9},{2,18},{10... | collective-permute-start | bytes 393224 | tf_op jit(solution)/shard_map/ppermute | solution.py:567
  36.2 3.8 %collective-permute-start.9 = (bf16[8,64,128]{2,1,0:T(8,128)(2,1)S(1)}, bf16[8,64,128]{2,1,0:T(8,128)(2,1)S(1)}, u32[]{:S(2)}, u32[]{:S(2)}) collective-permute-start(bf16[8,64,128]{2,1,0:T(8,128)(2,1)S(1)} %shard_map.87.refs_0_), channel_id=1, source_target_pairs={{0,8},{8,0},{16,24},{24,16},{1,9},{9,1},{17,25},{25,17},{2,10},{10... | collective-permute-start | bytes 393224 | tf_op jit(solution)/shard_map/ppermute | solution.py:567
  36.2 3.8 %collective-permute-start.10 = (bf16[8,64,128]{2,1,0:T(8,128)(2,1)S(1)}, bf16[8,64,128]{2,1,0:T(8,128)(2,1)S(1)}, u32[]{:S(2)}, u32[]{:S(2)}) collective-permute-start(bf16[8,64,128]{2,1,0:T(8,128)(2,1)S(1)} %shard_map.88.refs_1_), channel_id=1, source_target_pairs={{0,8},{8,0},{16,24},{24,16},{1,9},{9,1},{17,25},{25,17},{2,10},{10... | collective-permute-start | bytes 393224 | tf_op jit(solution)/shard_map/ppermute | solution.py:567
  37.9 2.1 %collective-permute-start.11 = (bf16[8,64,128]{2,1,0:T(8,128)(2,1)S(1)}, bf16[8,64,128]{2,1,0:T(8,128)(2,1)S(1)}, u32[]{:S(2)}, u32[]{:S(2)}) collective-permute-start(bf16[8,64,128]{2,1,0:T(8,128)(2,1)S(1)} %collective-permute-done.7.refs_2_), channel_id=1, source_target_pairs={{0,8},{8,0},{16,24},{24,16},{1,9},{9,1},{17,25},{25,17},{2,10},{10... | collective-permute-start | bytes 393224 | tf_op jit(solution)/shard_map/ppermute | solution.py:567
  40.0 1.3 %collective-permute-start.12 = (bf16[8,64,128]{2,1,0:T(8,128)(2,1)S(1)}, bf16[8,64,128]{2,1,0:T(8,128)(2,1)S(1)}, u32[]{:S(2)}, u32[]{:S(2)}) collective-permute-start(bf16[8,64,128]{2,1,0:T(8,128)(2,1)S(1)} %collective-permute-done.8.refs_3_), channel_id=1, source_target_pairs={{0,8},{8,0},{16,24},{24,16},{1,9},{9,1},{17,25},{25,17},{2,10},{10... | collective-permute-start | bytes 393224 | tf_op jit(solution)/shard_map/ppermute | solution.py:567

commit v5 on v4

--- a/solution.py
+++ b/solution.py
@@ -355,7 +355,7 @@
                         top = (2 * k + b) * GROUP + part * PACK
                         right[top : top + PACK, tile_cols(j, 0)] = d_re * t_re - d_im * t_im
                         right[top : top + PACK, tile_cols(j, 1)] = d_re * t_im + d_im * t_re
-        one = jnp.dot(right[...], first_ref[...], preferred_element_type=f32).astype(bf16)
+        one = jnp.dot(right[: 2 * batch_size * GROUP], first_ref[...], preferred_element_type=f32).astype(bf16)
         stacks = []
         for k in range(batch_size):
             rows = slice(2 * k * GROUP, (2 * k + 2) * GROUP)
@@ -398,7 +398,13 @@
 
     total = lax.fori_loop(0, out_ref.shape[0], add, 0, unroll=True)
 
-    @pl.when(total > 0)
+    few = 6
+
+    @pl.when((total > 0) & (total <= few))
+    def _():
+        run_tasks(beams, few, side, total, words, *constants, out_ref, scratch)
+
+    @pl.when(total > few)
     def _():
         run_tasks(beams, batch_size, side, total, words, *constants, out_ref, scratch)
 

time: 43.6 us -> 43.1 us (0.989); the launches traced: 43.5 us -> 42.4 us
  Pallas kernels: 23 us -> 19 us
  starting transfers between devices: 12 us -> 15.2 us
    pallas_call x2, Pallas kernels: 12.3 us -> 8.29 us  [propagate(): pl.pallas_call(kernel, out_shape=[half, half, pltpu.VMEM(words.shape, jnp...]
    ppermute x13, starting transfers between devices: 12 us -> 15.2 us  [across(): return lax.ppermute(array, ('beam', 'strip'), pairs)]
  transfers between devices with their start and end apart: 13 -> 13, of which waited for: 5 -> 5; matrix products, arithmetic and copies ran while one was open for 3% -> 3% of each run, Pallas kernels for 27% -> 28%
where the time goes in v5:
time: 43.1 us; the launch traced here: 42.4 us
  Pallas kernels  19 us (44%)
  starting transfers between devices  15.2 us (35%)
  waiting for transfers between devices  6.5 us (15%)
  other arithmetic  1.38 us (3%)
    ppermute x13, starting transfers between devices, across(): return lax.ppermute(array, ('beam', 'strip'), pairs)  15.2 us
    pallas_call x2, Pallas kernels, propagate(): pl.pallas_call(kernel, out_shape=[half, half, pltpu.VMEM(words.shape, jnp...  8.29 us
    ppermute x13, waiting for transfers between devices, across(): return lax.ppermute(array, ('beam', 'strip'), pairs)  6.5 us
    pallas_call x1, Pallas kernels, own_words(): pl.pallas_call(words_kernel, out_shape=pltpu.VMEM((width // LANES, GROUP...  3.81 us
    pallas_call x1, Pallas kernels, put_together(): pl.pallas_call(gather_kernel, out_shape=jax.ShapeDtypeStruct((probes, WIN...  2.01 us
    pallas_call x1, Pallas kernels, pack_rows(): pl.pallas_call(pack_kernel, out_shape=pltpu.VMEM((half // LANES * HALO +...  1.86 us
    pallas_call x1, Pallas kernels, probe_table(): pl.pallas_call(kernel, out_shape=[pltpu.VMEM((2, 2, TABLE, LANES), jnp.fl...  1.77 us
    pallas_call x2, Pallas kernels, merge_pieces(): pl.pallas_call(kernel, out_shape=jax.ShapeDtypeStruct(own.shape, own.dtyp...  1.22 us
  transfers between devices with their start and end apart: 13, of which 5 were waited for; matrix products, arithmetic and copies ran while one was open for 3% of the time, Pallas kernels for 28%

profile of v5, /device:TPU:0, one launch (start us, length us, event | category | flops | bytes accessed | tf_op | source)
XLA Modules:
  0.0 42.4 jit_solution(4111527061105899230)
XLA Ops:
  0.0 1.9 %shard_map.82 = s16[1552,128]{1,0:T(8,128)(2,1)S(1)} custom-call(s32[2,192,4096]{2,1,0:T(8,128)} %atoms_hbm.3, s32[2,32]{1,0:T(2,128)} %bitcast.6), custom_call_target="tpu_custom_call" | custom-call | tf_op jit(solution)/shard_map/pallas_call | solution.py:104
  1.9 3.0 %collective-permute-start = (s16[1552,128]{1,0:T(8,128)(2,1)S(1)}, s16[1552,128]{1,0:T(8,128)(2,1)S(1)}, u32[]{:S(2)}, u32[]{:S(2)}) collective-permute-start(s16[1552,128]{1,0:T(8,128)(2,1)S(1)} %shard_map.82), channel_id=1, source_target_pairs={{0,1},{8,9},{16,23},{24,31},{1,2},{9,10},{17,16},{25,24},{2,3},{10... | collective-permute-start | bytes 1191944 | tf_op jit(solution)/shard_map/ppermute | solution.py:573
  4.9 0.1 copy.10
  5.0 0.1 pad_maximum_fusion.1
  5.0 3.7 %collective-permute-start.3 = (f32[2,3]{1,0:T(2,128)S(1)}, f32[2,3]{1,0:T(2,128)S(1)}, u32[]{:S(2)}, u32[]{:S(2)}) collective-permute-start(f32[2,3]{1,0:T(2,128)S(1)} %pad_maximum_fusion.1), channel_id=1, source_target_pairs={{0,24},{8,16},{16,8},{24,0},{1,25},{9,17},{17,9},{25,1},{2,26},{10... | collective-permute-start | bytes 80 | tf_op jit(solution)/shard_map/ppermute | solution.py:573
  8.8 0.9 %collective-permute-start.2 = (f32[2,3]{1,0:T(2,128)S(1)}, f32[2,3]{1,0:T(2,128)S(1)}, u32[]{:S(2)}, u32[]{:S(2)}) collective-permute-start(f32[2,3]{1,0:T(2,128)S(1)} %pad_maximum_fusion.1), channel_id=1, source_target_pairs={{0,16},{8,24},{16,0},{24,8},{1,17},{9,25},{17,1},{25,9},{2,18},{10... | collective-permute-start | bytes 80 | tf_op jit(solution)/shard_map/ppermute | solution.py:573
  9.7 0.0 collective-permute-start.1
  9.7 0.6 %pad_add_fusion.place_ref.refs_0_ = s32[4]{0:T(128)} fusion(s32[1]{0:T(128)} %bitcast.3, s32[1]{0:T(128)} %bitcast.2, s32[1]{0:T(128)} %bitcast.1, s32[1]{0:T(128)} %bitcast), kind=kLoop, calls=%fused_computation.2 | loop fusion | flops 12 | bytes 32 | tf_op jit(solution)/shard_map/stack | solution.py:565
  10.3 3.8 %shard_map.83.refs_2_ = s32[32,96,128]{2,1,0:T(8,128)S(1)} custom-call(s32[4]{0:T(128)} %pad_add_fusion.place_ref.refs_0_, s32[2,192,4096]{2,1,0:T(8,128)} %atoms_hbm.3), custom_call_target="tpu_custom_call" | custom-call | flops 31457280 | bytes 9437184 | tf_op jit(solution)/shard_map/pallas_call | solution.py:154
  14.2 0.0 collective-permute-done.3
  14.2 0.0 collective-permute-done.1
  14.2 0.7 %pad_maximum_fusion.refs_0_ = f32[8,3]{1,0:T(8,128)} fusion(f32[2,3]{1,0:T(2,128)S(1)} %collective-permute-done.3, f32[2,3]{1,0:T(2,128)S(1)} %collective-permute-done.2, f32[2,3]{1,0:T(2,128)S(1)} %collective-permute-done.1, f32[2,1]{1,0:T(2,128)S(1)} %copy.10, f32[2,2]{1,0:T(2,128)S(1)} %convert_element_type.6), kind=kLoop, calls=%fused_computation | loop fusion | flops 96 | bytes 192 | tf_op jit(solution)/shard_map/concatenate | solution.py:588
  14.9 1.8 %shard_map.84 = (f32[2,2,384,128]{3,2,1,0:T(8,128)S(1)}, f32[16,128]{1,0:T(8,128)S(1)}, bf16[512,256]{1,0:T(8,128)(2,1)S(1)}, bf16[256,256]{1,0:T(8,128)(2,1)S(1)}, bf16[128,256]{1,0:T(8,128)(2,1)S(1)}) custom-call(f32[8,3]{1,0:T(8,128)} %pad_maximum_fusion.refs_0_, f32[2,4]{1,0:T(2,128)} %refs_1_.1, bf16[512,256]{1,0:T(8,128)(2,1)} %constant.56.clone.refs_2_, ...), custom_call_target="tpu_custom_call" | custom-call | flops 100000000 | bytes 1000000 | tf_op jit(solution)/shard_map/pallas_call | solution.py:229
  16.6 0.5 %collective-permute-done.refs_3_ = s16[1552,128]{1,0:T(8,128)(2,1)S(1)} collective-permute-done((s16[1552,128]{1,0:T(8,128)(2,1)S(1)}, s16[1552,128]{1,0:T(8,128)(2,1)S(1)}, u32[]{:S(2)}, u32[]{:S(2)}) %collective-permute-start) | collective-permute-done | bytes 397344 | tf_op jit(solution)/shard_map/ppermute | solution.py:573
  17.1 0.1 collective-permute-start.4
  17.2 1.6 %collective-permute-done.4.refs_4_ = s16[1552,128]{1,0:T(8,128)(2,1)S(1)} collective-permute-done((s16[1552,128]{1,0:T(8,128)(2,1)S(1)}, s16[1552,128]{1,0:T(8,128)(2,1)S(1)}, u32[]{:S(2)}, u32[]{:S(2)}) %collective-permute-start.4) | collective-permute-done | bytes 397344 | tf_op jit(solution)/shard_map/ppermute | solution.py:573
  18.8 3.2 %shard_map.85 = (bf16[8,64,128]{2,1,0:T(8,128)(2,1)S(1)}, bf16[8,64,128]{2,1,0:T(8,128)(2,1)S(1)}, s32[32,96,128]{2,1,0:T(8,128)S(1)}) custom-call(s32[4]{0:T(128)S(1)} %copy-done.1, s32[2,32]{1,0:T(2,128)S(1)} %slice_convert_fusion.refs_1_, s32[32,96,128]{2,1,0:T(8,128)S(1)} %shard_map.83.refs_2_, ...), custom_call_target="tpu_custom_call", output_to_operand_aliasing={{2}: (2, {})} | custom-call | flops 4000000000 | bytes 4000000 | tf_op jit(solution)/shard_map/pallas_call | solution.py:447
  22.0 1.8 %collective-permute-start.5 = (bf16[8,64,128]{2,1,0:T(8,128)(2,1)S(1)}, bf16[8,64,128]{2,1,0:T(8,128)(2,1)S(1)}, u32[]{:S(2)}, u32[]{:S(2)}) collective-permute-start(bf16[8,64,128]{2,1,0:T(8,128)(2,1)S(1)} %get-tuple-element.40), channel_id=1, source_target_pairs={{0,7},{8,15},{16,17},{24,25},{1,0},{9,8},{17,18},{25,26},{2,1},{10... | collective-permute-start | bytes 393224 | tf_op jit(solution)/shard_map/ppermute | solution.py:573
  23.9 1.4 %collective-permute-start.6 = (bf16[8,64,128]{2,1,0:T(8,128)(2,1)S(1)}, bf16[8,64,128]{2,1,0:T(8,128)(2,1)S(1)}, u32[]{:S(2)}, u32[]{:S(2)}) collective-permute-start(bf16[8,64,128]{2,1,0:T(8,128)(2,1)S(1)} %get-tuple-element.42), channel_id=1, source_target_pairs={{0,7},{8,15},{16,17},{24,25},{1,0},{9,8},{17,18},{25,26},{2,1},{10... | collective-permute-start | bytes 393224 | tf_op jit(solution)/shard_map/ppermute | solution.py:573
  25.3 5.1 %shard_map.86 = (bf16[8,64,128]{2,1,0:T(8,128)(2,1)S(1)}, bf16[8,64,128]{2,1,0:T(8,128)(2,1)S(1)}) custom-call(s32[4]{0:T(128)S(1)} %copy-done.1, s32[2,32]{1,0:T(2,128)S(1)} %bitcast.7, s32[32,96,128]{2,1,0:T(8,128)S(1)} %get-tuple-element.38.refs_2_, f32[2,2,384,128]{3,2,1,0:T(8,128)S(1)} %get-tuple-element.33.refs_5_.refs_3_, ...), custom_call_target="tpu_custom_call" | custom-call | flops 4000000000 | bytes 4000000 | tf_op jit(solution)/shard_map/pallas_call | solution.py:447
  30.4 0.6 %shard_map.87.refs_0_ = bf16[8,64,128]{2,1,0:T(8,128)(2,1)S(1)} custom-call(s32[4]{0:T(128)S(1)} %copy-done.1, s32[2,32]{1,0:T(2,128)S(1)} %bitcast.8, bf16[8,64,128]{2,1,0:T(8,128)(2,1)S(1)} %get-tuple-element.39.refs_2_, bf16[8,64,128]{2,1,0:T(8,128)(2,1)S(1)} %collective-permute-done.5.refs_3_), custom_call_target="tpu_custom_call" | custom-call | tf_op jit(solution)/shard_map/pallas_call | solution.py:486
  31.0 2.1 %collective-permute-start.7 = (bf16[8,64,128]{2,1,0:T(8,128)(2,1)S(1)}, bf16[8,64,128]{2,1,0:T(8,128)(2,1)S(1)}, u32[]{:S(2)}, u32[]{:S(2)}) collective-permute-start(bf16[8,64,128]{2,1,0:T(8,128)(2,1)S(1)} %shard_map.87.refs_0_), channel_id=1, source_target_pairs={{0,16},{8,24},{16,0},{24,8},{1,17},{9,25},{17,1},{25,9},{2,18},{10... | collective-permute-start | bytes 393224 | tf_op jit(solution)/shard_map/ppermute | solution.py:573
  33.2 0.0 collective-permute-done.6.refs_3_
  33.2 0.6 %shard_map.88.refs_1_ = bf16[8,64,128]{2,1,0:T(8,128)(2,1)S(1)} custom-call(s32[4]{0:T(128)S(1)} %copy-done.1, s32[2,32]{1,0:T(2,128)S(1)} %bitcast.9, bf16[8,64,128]{2,1,0:T(8,128)(2,1)S(1)} %get-tuple-element.41.refs_2_, bf16[8,64,128]{2,1,0:T(8,128)(2,1)S(1)} %collective-permute-done.6.refs_3_), custom_call_target="tpu_custom_call" | custom-call | tf_op jit(solution)/shard_map/pallas_call | solution.py:486
  33.8 1.6 %collective-permute-start.8 = (bf16[8,64,128]{2,1,0:T(8,128)(2,1)S(1)}, bf16[8,64,128]{2,1,0:T(8,128)(2,1)S(1)}, u32[]{:S(2)}, u32[]{:S(2)}) collective-permute-start(bf16[8,64,128]{2,1,0:T(8,128)(2,1)S(1)} %shard_map.88.refs_1_), channel_id=1, source_target_pairs={{0,16},{8,24},{16,0},{24,8},{1,17},{9,25},{17,1},{25,9},{2,18},{10... | collective-permute-start | bytes 393224 | tf_op jit(solution)/shard_map/ppermute | solution.py:573
  35.4 0.0 collective-permute-start.9
  35.4 0.5 %collective-permute-start.10 = (bf16[8,64,128]{2,1,0:T(8,128)(2,1)S(1)}, bf16[8,64,128]{2,1,0:T(8,128)(2,1)S(1)}, u32[]{:S(2)}, u32[]{:S(2)}) collective-permute-start(bf16[8,64,128]{2,1,0:T(8,128)(2,1)S(1)} %shard_map.88.refs_1_), channel_id=1, source_target_pairs={{0,8},{8,0},{16,24},{24,16},{1,9},{9,1},{17,25},{25,17},{2,10},{10... | collective-permute-start | bytes 393224 | tf_op jit(solution)/shard_map/ppermute | solution.py:573
  35.9 0.6 %collective-permute-done.7.refs_2_ = bf16[8,64,128]{2,1,0:T(8,128)(2,1)S(1)} collective-permute-done((bf16[8,64,128]{2,1,0:T(8,128)(2,1)S(1)}, bf16[8,64,128]{2,1,0:T(8,128)(2,1)S(1)}, u32[]{:S(2)}, u32[]{:S(2)}) %collective-permute-start.7) | collective-permute-done | bytes 131104 | tf_op jit(solution)/shard_map/ppermute | solution.py:573
  36.5 0.0 collective-permute-start.11
  36.5 2.4 %collective-permute-done.8.refs_3_ = bf16[8,64,128]{2,1,0:T(8,128)(2,1)S(1)} collective-permute-done((bf16[8,64,128]{2,1,0:T(8,128)(2,1)S(1)}, bf16[8,64,128]{2,1,0:T(8,128)(2,1)S(1)}, u32[]{:S(2)}, u32[]{:S(2)}) %collective-permute-start.8) | collective-permute-done | bytes 131104 | tf_op jit(solution)/shard_map/ppermute | solution.py:573
  38.9 1.3 %collective-permute-done.12.refs_7_ = bf16[8,64,128]{2,1,0:T(8,128)(2,1)S(1)} collective-permute-done((bf16[8,64,128]{2,1,0:T(8,128)(2,1)S(1)}, bf16[8,64,128]{2,1,0:T(8,128)(2,1)S(1)}, u32[]{:S(2)}, u32[]{:S(2)}) %collective-permute-start.12) | collective-permute-done | bytes 131104 | tf_op jit(solution)/shard_map/ppermute | solution.py:573
  40.3 2.0 %shard_map.89 = f32[32,16384]{1,0:T(8,128)} custom-call(s32[4]{0:T(128)S(1)} %copy-done.1, s32[2,32]{1,0:T(2,128)S(1)} %bitcast.10, bf16[8,64,128]{2,1,0:T(8,128)(2,1)S(1)} %shard_map.87.refs_0_, bf16[8,64,128]{2,1,0:T(8,128)(2,1)S(1)} %shard_map.88.refs_1_, bf16[8,64,128]{2,1,0:T(8,128)(2,1)S(1)} %collective-permute-done.7.refs_2_, ...), custom_call_target="tpu_custom_call" | custom-call | tf_op jit(solution)/shard_map/pallas_call | solution.py:539
  (16 shorter events, 0.0 us)
Async XLA Ops:
  0.0 4.9 %copy-start.3 = (f32[2]{0:T(128)S(1)}, f32[2]{0:T(128)}, u32[]{:S(2)}) copy-start(f32[2]{0:T(128)} %param.10) | copy-start | bytes 28
  0.0 5.0 %copy-start.2 = (s32[2,2]{1,0:T(2,128)S(1)}, s32[2,2]{1,0:T(2,128)}, u32[]{:S(2)}) copy-start(s32[2,2]{1,0:T(2,128)} %param.11) | copy-start | bytes 52
  1.9 15.2 %collective-permute-start = (s16[1552,128]{1,0:T(8,128)(2,1)S(1)}, s16[1552,128]{1,0:T(8,128)(2,1)S(1)}, u32[]{:S(2)}, u32[]{:S(2)}) collective-permute-start(s16[1552,128]{1,0:T(8,128)(2,1)S(1)} %shard_map.82), channel_id=1, source_target_pairs={{0,1},{8,9},{16,23},{24,31},{1,2},{9,10},{17,16},{25,24},{2,3},{10... | collective-permute-start | bytes 1191944 | tf_op jit(solution)/shard_map/ppermute | solution.py:573
  5.0 9.1 %collective-permute-start.3 = (f32[2,3]{1,0:T(2,128)S(1)}, f32[2,3]{1,0:T(2,128)S(1)}, u32[]{:S(2)}, u32[]{:S(2)}) collective-permute-start(f32[2,3]{1,0:T(2,128)S(1)} %pad_maximum_fusion.1), channel_id=1, source_target_pairs={{0,24},{8,16},{16,8},{24,0},{1,25},{9,17},{17,9},{25,1},{2,26},{10... | collective-permute-start | bytes 80 | tf_op jit(solution)/shard_map/ppermute | solution.py:573
  8.8 5.4 %collective-permute-start.2 = (f32[2,3]{1,0:T(2,128)S(1)}, f32[2,3]{1,0:T(2,128)S(1)}, u32[]{:S(2)}, u32[]{:S(2)}) collective-permute-start(f32[2,3]{1,0:T(2,128)S(1)} %pad_maximum_fusion.1), channel_id=1, source_target_pairs={{0,16},{8,24},{16,0},{24,8},{1,17},{9,25},{17,1},{25,9},{2,18},{10... | collective-permute-start | bytes 80 | tf_op jit(solution)/shard_map/ppermute | solution.py:573
  9.7 4.5 %collective-permute-start.1 = (f32[2,3]{1,0:T(2,128)S(1)}, f32[2,3]{1,0:T(2,128)S(1)}, u32[]{:S(2)}, u32[]{:S(2)}) collective-permute-start(f32[2,3]{1,0:T(2,128)S(1)} %pad_maximum_fusion.1), channel_id=1, source_target_pairs={{0,8},{8,0},{16,24},{24,16},{1,9},{9,1},{17,25},{25,17},{2,10},{10... | collective-permute-start | bytes 80 | tf_op jit(solution)/shard_map/ppermute | solution.py:573
  10.3 8.5 %copy-start.1 = (s32[4]{0:T(128)S(1)}, s32[4]{0:T(128)}, u32[]{:S(2)}) copy-start(s32[4]{0:T(128)} %pad_add_fusion.place_ref.refs_0_) | copy-start | bytes 52
  17.1 1.7 %collective-permute-start.4 = (s16[1552,128]{1,0:T(8,128)(2,1)S(1)}, s16[1552,128]{1,0:T(8,128)(2,1)S(1)}, u32[]{:S(2)}, u32[]{:S(2)}) collective-permute-start(s16[1552,128]{1,0:T(8,128)(2,1)S(1)} %collective-permute-done.refs_3_), channel_id=1, source_target_pairs={{0,8},{8,0},{16,24},{24,16},{1,9},{9,1},{17,25},{25,17},{2,10},{10... | collective-permute-start | bytes 1191944 | tf_op jit(solution)/shard_map/ppermute | solution.py:573
  17.2 8.1 %copy-start = (s32[32,2]{0,1:T(2,128)S(1)}, s32[32,2]{0,1:T(2,128)}, u32[]{:S(2)}) copy-start(s32[32,2]{0,1:T(2,128)} %param.12) | copy-start | bytes 772
  22.0 8.4 %collective-permute-start.5 = (bf16[8,64,128]{2,1,0:T(8,128)(2,1)S(1)}, bf16[8,64,128]{2,1,0:T(8,128)(2,1)S(1)}, u32[]{:S(2)}, u32[]{:S(2)}) collective-permute-start(bf16[8,64,128]{2,1,0:T(8,128)(2,1)S(1)} %get-tuple-element.40), channel_id=1, source_target_pairs={{0,7},{8,15},{16,17},{24,25},{1,0},{9,8},{17,18},{25,26},{2,1},{10... | collective-permute-start | bytes 393224 | tf_op jit(solution)/shard_map/ppermute | solution.py:573
  23.9 9.3 %collective-permute-start.6 = (bf16[8,64,128]{2,1,0:T(8,128)(2,1)S(1)}, bf16[8,64,128]{2,1,0:T(8,128)(2,1)S(1)}, u32[]{:S(2)}, u32[]{:S(2)}) collective-permute-start(bf16[8,64,128]{2,1,0:T(8,128)(2,1)S(1)} %get-tuple-element.42), channel_id=1, source_target_pairs={{0,7},{8,15},{16,17},{24,25},{1,0},{9,8},{17,18},{25,26},{2,1},{10... | collective-permute-start | bytes 393224 | tf_op jit(solution)/shard_map/ppermute | solution.py:573
  31.0 5.5 %collective-permute-start.7 = (bf16[8,64,128]{2,1,0:T(8,128)(2,1)S(1)}, bf16[8,64,128]{2,1,0:T(8,128)(2,1)S(1)}, u32[]{:S(2)}, u32[]{:S(2)}) collective-permute-start(bf16[8,64,128]{2,1,0:T(8,128)(2,1)S(1)} %shard_map.87.refs_0_), channel_id=1, source_target_pairs={{0,16},{8,24},{16,0},{24,8},{1,17},{9,25},{17,1},{25,9},{2,18},{10... | collective-permute-start | bytes 393224 | tf_op jit(solution)/shard_map/ppermute | solution.py:573
  33.8 5.1 %collective-permute-start.8 = (bf16[8,64,128]{2,1,0:T(8,128)(2,1)S(1)}, bf16[8,64,128]{2,1,0:T(8,128)(2,1)S(1)}, u32[]{:S(2)}, u32[]{:S(2)}) collective-permute-start(bf16[8,64,128]{2,1,0:T(8,128)(2,1)S(1)} %shard_map.88.refs_1_), channel_id=1, source_target_pairs={{0,16},{8,24},{16,0},{24,8},{1,17},{9,25},{17,1},{25,9},{2,18},{10... | collective-permute-start | bytes 393224 | tf_op jit(solution)/shard_map/ppermute | solution.py:573
  35.4 3.6 %collective-permute-start.9 = (bf16[8,64,128]{2,1,0:T(8,128)(2,1)S(1)}, bf16[8,64,128]{2,1,0:T(8,128)(2,1)S(1)}, u32[]{:S(2)}, u32[]{:S(2)}) collective-permute-start(bf16[8,64,128]{2,1,0:T(8,128)(2,1)S(1)} %shard_map.87.refs_0_), channel_id=1, source_target_pairs={{0,8},{8,0},{16,24},{24,16},{1,9},{9,1},{17,25},{25,17},{2,10},{10... | collective-permute-start | bytes 393224 | tf_op jit(solution)/shard_map/ppermute | solution.py:573
  35.4 3.6 %collective-permute-start.10 = (bf16[8,64,128]{2,1,0:T(8,128)(2,1)S(1)}, bf16[8,64,128]{2,1,0:T(8,128)(2,1)S(1)}, u32[]{:S(2)}, u32[]{:S(2)}) collective-permute-start(bf16[8,64,128]{2,1,0:T(8,128)(2,1)S(1)} %shard_map.88.refs_1_), channel_id=1, source_target_pairs={{0,8},{8,0},{16,24},{24,16},{1,9},{9,1},{17,25},{25,17},{2,10},{10... | collective-permute-start | bytes 393224 | tf_op jit(solution)/shard_map/ppermute | solution.py:573
  36.5 2.4 %collective-permute-start.11 = (bf16[8,64,128]{2,1,0:T(8,128)(2,1)S(1)}, bf16[8,64,128]{2,1,0:T(8,128)(2,1)S(1)}, u32[]{:S(2)}, u32[]{:S(2)}) collective-permute-start(bf16[8,64,128]{2,1,0:T(8,128)(2,1)S(1)} %collective-permute-done.7.refs_2_), channel_id=1, source_target_pairs={{0,8},{8,0},{16,24},{24,16},{1,9},{9,1},{17,25},{25,17},{2,10},{10... | collective-permute-start | bytes 393224 | tf_op jit(solution)/shard_map/ppermute | solution.py:573
  38.9 1.3 %collective-permute-start.12 = (bf16[8,64,128]{2,1,0:T(8,128)(2,1)S(1)}, bf16[8,64,128]{2,1,0:T(8,128)(2,1)S(1)}, u32[]{:S(2)}, u32[]{:S(2)}) collective-permute-start(bf16[8,64,128]{2,1,0:T(8,128)(2,1)S(1)} %collective-permute-done.8.refs_3_), channel_id=1, source_target_pairs={{0,8},{8,0},{16,24},{24,16},{1,9},{9,1},{17,25},{25,17},{2,10},{10... | collective-permute-start | bytes 393224 | tf_op jit(solution)/shard_map/ppermute | solution.py:573
